TPU v7x, 128 devices: a whole 4x4x4 slice. The times are simulated.
128 devices in a mesh: rows: 32 (over x, y_lo, z), cols: 4 (over y_hi, core).
Axes of the slice: x: 4, y: 4 (y_hi: 2, y_lo: 2; y = y_hi * 2 + y_lo), z: 4, core: 2. Of those that a mesh axis runs over, the one named last changes fastest.
Arguments:
- pair_feature_input: bfloat16 [64, 1024, 2048], P(None, 'rows', 'cols'), may hold values from -6 to 6
- tile_mask: int32 [8, 16], replicated, may hold values 0 or 1
- row_kernel_weights: bfloat16 [2, 3, 64, 64], replicated, may hold values from -0.4375 to 0.4375
- column_kernel_weights: bfloat16 [2, 3, 64, 64], replicated, may hold values from -0.4375 to 0.4375
- cotangent: bfloat16 [64, 1024, 2048], P(None, 'rows', 'cols'), may hold values from -6 to 6
Outputs:
- final_output_map: bfloat16 [64, 1024, 2048], P(None, 'rows', 'cols')
- map_grad: bfloat16 [64, 1024, 2048], P(None, 'rows', 'cols')
- row_grad: float32 [2, 3, 64, 64], replicated
- col_grad: float32 [2, 3, 64, 64], replicated
All inputs are finite; a program needn't handle non-finite values.
Results may differ from a plain program's by a relative error of at most 0.0075.
Values may be sent and summed in bfloat16 or wider, within the bound.
No kernel may reach another device: no remote copies, remote signals or barrier semaphores. Data moves between devices by JAX's collectives and lax.ppermute only.
A program may use at most 192 MiB of HBM per device.

v0:
```python
import functools
import math

import jax
import jax.numpy as jnp
from jax import lax
from jax.experimental import pallas as pl
from jax.experimental.pallas import tpu as pltpu
from jax.sharding import Mesh, PartitionSpec as P

FIRST_SPACING = 4
SECOND_SPACING = 8
TILE = 128
C = 64
R = 32
W = 512
E = 640
HALO = 12
EDGE = 32
GROUPS = R // 4
HG = HALO // 4
F32 = jnp.float32
BF16 = jnp.bfloat16
VMEM_LIMIT = 60 * 1024 * 1024


def dot(a, b):
    return jnp.dot(a, b, preferred_element_type=F32)


def dot_nt(a, b):
    return lax.dot_general(a, b, (((1,), (1,)), ((), ())), preferred_element_type=F32)


def pack_kernel(x_ref, c_ref, xt, xtop, xbot, ct, ctop, cbot, to_left, to_right, scratch):
    w = pl.program_id(0)
    i = pl.program_id(1)
    lane = lax.broadcasted_iota(jnp.int32, (C, 128), 1)
    for a, (src, dst, top, bot) in enumerate(((x_ref, xt, xtop, xbot), (c_ref, ct, ctop, cbot))):
        scratch[...] = src[...].astype(F32).reshape(C * 16, 128)

        def row(r):
            return scratch[pl.ds(r, C, stride=16), :]

        for r in range(16):
            dst[r] = row(r).astype(BF16)

        @pl.when(i == 0)
        def _():
            top[...] = dst[0:HALO]

        @pl.when(i == 1)
        def _():
            bot[...] = dst[16 - HALO : 16]

        def pack(out, first):
            for g in range(4):
                acc = jnp.zeros((C, 128), F32)
                for k in range(4):
                    v = row(4 * g + k)
                    shift = (32 * k - first) % 128
                    if shift:
                        v = pltpu.roll(v, shift, 1)
                    acc = jnp.where(lane // 32 == k, v, acc)
                out[a, i * 4 + g] = acc.astype(BF16)

        @pl.when(w == 0)
        def _():
            pack(to_left, 0)

        @pl.when(w == W // 128 - 1)
        def _():
            pack(to_right, 96)


def pack_call(x, c):
    native = pl.BlockSpec((C, 16, 128), lambda w, i: (0, i, w))
    turned = pl.BlockSpec((16, C, 128), lambda w, i: (i, 0, w))
    halo = pl.BlockSpec((HALO, C, 128), lambda w, i: (0, 0, w))
    edge = pl.BlockSpec((2, GROUPS, C, 128), lambda w, i: (0, 0, 0, 0))
    full = jax.ShapeDtypeStruct((R, C, W), BF16)
    part = jax.ShapeDtypeStruct((HALO, C, W), BF16)
    edges = jax.ShapeDtypeStruct((2, GROUPS, C, 128), BF16)
    return pl.pallas_call(
        pack_kernel,
        grid=(W // 128, 2),
        in_specs=[native, native],
        out_specs=[turned, halo, halo, turned, halo, halo, edge, edge],
        out_shape=[full, part, part, full, part, part, edges, edges],
        scratch_shapes=[pltpu.VMEM((C * 16, 128), F32)],
        compiler_params=pltpu.CompilerParams(vmem_limit_bytes=VMEM_LIMIT),
    )(x, c)


def build_mask(tiles, mask):
    row_dev, col_dev = lax.axis_index("rows"), lax.axis_index("cols")
    n_rows, n_cols = tiles.shape
    first_row, first_tile = row_dev * R, col_dev * (W // TILE)
    lane = lax.broadcasted_iota(jnp.int32, (8, 128), 1)

    def value(p, ct):
        cell = first_row + (-1, 0, R)[p]
        inside = (cell >= 0) & (cell < n_rows * TILE) & (ct >= 0) & (ct < n_cols)
        rt = jnp.clip(cell, 0, n_rows * TILE - 1) // TILE
        return jnp.where(inside, tiles[rt, jnp.clip(ct, 0, n_cols - 1)], 0)

    for p in range(3):
        for t in range(W // 128):
            mask[p, :, t * 128 : (t + 1) * 128] = jnp.full((8, 128), value(p, first_tile + t), jnp.int32).astype(F32)
        right = jnp.full((8, 128), value(p, first_tile + W // TILE), jnp.int32)
        left = jnp.full((8, 128), value(p, first_tile - 1), jnp.int32)
        mask[p, :, W:E] = jnp.where(lane < 64, right, left).astype(F32)


def mask_row(mask, r):
    p = (r >= 0).astype(jnp.int32) + (r >= R).astype(jnp.int32)
    return mask[p][0:1, :]


def unpack_edges(left, right, dst, first):
    lane = lax.broadcasted_iota(jnp.int32, (C, 128), 1)
    for k in range(4):
        rv, lv = right.astype(F32), left.astype(F32)
        if k:
            rv = pltpu.roll(rv, 128 - 32 * k, 1)
        if k != 3:
            lv = pltpu.roll(lv, 96 - 32 * k, 1)
        tile = jnp.where(lane < EDGE, rv, jnp.where(lane >= 128 - EDGE, lv, 0.0))
        dst[first + k, :, W:E] = tile.astype(BF16)


def unpack_all(a, col_left, col_right, cor_top, cor_bot, dst):
    for g in range(HG):
        unpack_edges(cor_top[a, 0, g], cor_top[a, 1, g], dst, 4 * g)
        unpack_edges(cor_bot[a, 0, g], cor_bot[a, 1, g], dst, HALO + R + 4 * g)

    def own(g, _):
        unpack_edges(col_left[a, g], col_right[a, g], dst, HALO + 4 * g)
        return 0

    lax.fori_loop(0, GROUPS, own, 0)


def shifted(v, d):
    n = v.shape[1]
    return pltpu.roll(v, (-d) % n, 1)


def row_stack(v, d, reverse):
    ahead, behind = shifted(v, d), shifted(v, -d)
    parts = [ahead, v, behind] if reverse else [behind, v, ahead]
    return jnp.concatenate(parts, axis=0)


def col_stack(ref, r, d, reverse, width=E):
    parts = [ref[r - d, :, :width], ref[r, :, :width], ref[r + d, :, :width]]
    return jnp.concatenate(parts[::-1] if reverse else parts, axis=0)


def forward_matrix(w):
    return jnp.concatenate([w[j].astype(F32).T for j in range(3)], axis=0).T.astype(BF16)


def backward_matrix(w):
    return w.reshape(3 * C, C).astype(F32).T.astype(BF16)


def elu(p):
    return jnp.where(p > 0, p, jnp.exp(jnp.minimum(p, 0.0)) - 1.0)


def pairs(count, body):
    def step(i, _):
        body(2 * i)
        return 0

    lax.fori_loop(0, count // 2, step, 0)


def two(stack, matrix):
    both = dot(matrix, jnp.concatenate(stack, axis=1))
    n = stack[0].shape[1]
    return both[:, :n], both[:, n:]


def put_flat(flat, r, v):
    for t in range(W // 128):
        flat[t, pl.ds(r, C, stride=R), :] = v[:, t * 128 : (t + 1) * 128]


def narrow(flat, out):
    def channel(c, _):
        for t in range(W // 128):
            out[c, :, t * 128 : (t + 1) * 128] = flat[t, pl.ds(pl.multiple_of(c * R, R), R), :].astype(BF16)
        return 0

    lax.fori_loop(0, C, channel, 0)


def forward_kernel(
    tiles, x, xtop, xbot, col_left, col_right, cor_top, cor_bot, wr, wc,
    out, h1_out, b1_out, h2_out,
    xe, h1, b1, h2, flat, mask, sems,
):
    loads = [
        pltpu.make_async_copy(x, xe.at[HALO : HALO + R, :, 0:W], sems.at[0]),
        pltpu.make_async_copy(xtop, xe.at[0:HALO, :, 0:W], sems.at[1]),
        pltpu.make_async_copy(xbot, xe.at[HALO + R :, :, 0:W], sems.at[2]),
    ]
    for load in loads:
        load.start()
    build_mask(tiles, mask)
    unpack_all(0, col_left, col_right, cor_top, cor_bot, xe)
    wr1, wr2 = forward_matrix(wr[0]), forward_matrix(wr[1])
    wc1, wc2 = forward_matrix(wc[0]), forward_matrix(wc[1])
    for load in loads:
        load.wait()

    d1, d2 = FIRST_SPACING, SECOND_SPACING

    def hidden_one(r):
        pre = two([row_stack(xe[r + q], d1, False) for q in range(2)], wr1)
        for q in range(2):
            h1[r + q] = (elu(pre[q]) * mask_row(mask, r + q - HALO)).astype(BF16)

    pairs(R + 2 * HALO, hidden_one)
    save_h1 = pltpu.make_async_copy(h1.at[HALO : HALO + R], h1_out, sems.at[3])
    save_h1.start()

    def block_one(r):
        col = two([col_stack(h1, r + q + d1, d1, False) for q in range(2)], wc1)
        for q in range(2):
            kept = mask_row(mask, r + q + d1 - HALO) * col[q].astype(BF16).astype(F32)
            b1[r + q] = (xe[r + q + d1].astype(F32) + kept).astype(BF16)

    pairs(R + 2 * d2, block_one)
    save_b1 = pltpu.make_async_copy(b1.at[d2 : d2 + R], b1_out, sems.at[4])
    save_b1.start()

    def hidden_two(r):
        pre = two([row_stack(b1[r + q], d2, False) for q in range(2)], wr2)
        for q in range(2):
            h2[r + q] = (elu(pre[q]) * mask_row(mask, r + q - d2)).astype(BF16)

    pairs(R + 2 * d2, hidden_two)
    save_h2 = pltpu.make_async_copy(h2.at[d2 - d1 : d2 + R + d1], h2_out, sems.at[5])
    save_h2.start()

    def last(r):
        col = two([col_stack(h2, r + q + d2, d2, False, W) for q in range(2)], wc2)
        for q in range(2):
            kept = mask_row(mask, r + q)[:, :W] * col[q].astype(BF16).astype(F32)
            put_flat(flat, r + q, b1[r + q + d2, :, :W].astype(F32) + kept)

    pairs(R, last)

    narrow(flat, out)
    save_h1.wait()
    save_b1.wait()
    save_h2.wait()


ANY = pl.BlockSpec(memory_space=pl.ANY)
VM = pl.BlockSpec(memory_space=pltpu.VMEM)
SM = pl.BlockSpec(memory_space=pltpu.SMEM)


def forward_call(tiles, x, xtop, xbot, col_left, col_right, cor_top, cor_bot, wr, wc):
    d1, d2 = FIRST_SPACING, SECOND_SPACING
    return pl.pallas_call(
        forward_kernel,
        in_specs=[SM, ANY, ANY, ANY, VM, VM, VM, VM, VM, VM],
        out_specs=[VM, ANY, ANY, ANY],
        out_shape=[
            jax.ShapeDtypeStruct((C, R, W), BF16),
            jax.ShapeDtypeStruct((R, C, E), BF16),
            jax.ShapeDtypeStruct((R, C, E), BF16),
            jax.ShapeDtypeStruct((R + 2 * d1, C, E), BF16),
        ],
        scratch_shapes=[
            pltpu.VMEM((R + 2 * HALO, C, E), BF16),
            pltpu.VMEM((R + 2 * HALO, C, E), BF16),
            pltpu.VMEM((R + 2 * d2, C, E), BF16),
            pltpu.VMEM((R + 2 * d2, C, E), BF16),
            pltpu.VMEM((W // 128, C * R, 128), F32),
            pltpu.VMEM((3, 8, E), F32),
            pltpu.SemaphoreType.DMA((6,)),
        ],
        compiler_params=pltpu.CompilerParams(vmem_limit_bytes=VMEM_LIMIT),
    )(tiles, x, xtop, xbot, col_left, col_right, cor_top, cor_bot, wr, wc)


def backward_kernel(
    tiles, c, ctop, cbot, col_left, col_right, cor_top, cor_bot, wr, wc, x_in, h1_in, b1_in, h2_in,
    out, taps,
    ce, h1, b1, h2, x, a2, cg1, g1, a1, flat, mask, sems,
):
    d1, d2 = FIRST_SPACING, SECOND_SPACING
    loads = [
        pltpu.make_async_copy(c, ce.at[HALO : HALO + R, :, 0:W], sems.at[0]),
        pltpu.make_async_copy(ctop, ce.at[0:HALO, :, 0:W], sems.at[1]),
        pltpu.make_async_copy(cbot, ce.at[HALO + R :, :, 0:W], sems.at[2]),
    ]
    late = [
        pltpu.make_async_copy(h2_in, h2, sems.at[3]),
        pltpu.make_async_copy(b1_in, b1, sems.at[4]),
        pltpu.make_async_copy(h1_in, h1, sems.at[5]),
        pltpu.make_async_copy(x_in, x, sems.at[6]),
    ]
    for load in loads + late:
        load.start()
    build_mask(tiles, mask)
    unpack_all(1, col_left, col_right, cor_top, cor_bot, ce)
    wr1, wr2 = backward_matrix(wr[0]), backward_matrix(wr[1])
    wc1, wc2 = backward_matrix(wc[0]), backward_matrix(wc[1])
    taps[...] = jnp.zeros_like(taps)
    for load in loads + late:
        load.wait()

    def mask_cot(r):
        for q in range(2):
            v = ce[r + q]
            m = mask_row(mask, r + q - HALO)
            ce[r + q] = (v.astype(F32) * m).astype(BF16)

    def keep_cot(r):
        for q in range(2):
            g1[r + q] = ce[HALO - d1 + r + q].astype(F32)

    pairs(R + 2 * d1, keep_cot)
    pairs(R + 2 * HALO, mask_cot)

    def act_two(r):
        stacks = [col_stack(ce, r + q + HALO - d1, d2, True) for q in range(2)]
        hid = two(stacks, wc2)
        for q in range(2):
            m = mask_row(mask, r + q - d1)
            slope = 1.0 + jnp.minimum(h2[r + q].astype(F32), 0.0)
            a2[r + q] = (hid[q] * m * slope).astype(BF16)

    pairs(R + 2 * d1, act_two)

    def col_taps_two(r):
        acc = taps[0]
        for q in range(2):
            acc = acc + dot_nt(col_stack(ce, r + q + HALO, d2, True, W), h2[r + q + d1, :, :W])
        taps[0] = acc

    pairs(R, col_taps_two)

    def grad_one(r):
        stacks = [row_stack(a2[r + q], d2, True) for q in range(2)]
        mixed = two(stacks, wr2)
        for q in range(2):
            g = g1[r + q] + mixed[q]
            g1[r + q] = g
            cg1[r + q] = (g * mask_row(mask, r + q - d1)).astype(BF16)

    pairs(R + 2 * d1, grad_one)

    def row_taps_two(r):
        acc = taps[1]
        for q in range(2):
            stack = row_stack(a2[r + q + d1], d2, True)
            acc = acc + dot_nt(stack[:, :W], b1[r + q, :, :W])
        taps[1] = acc

    pairs(R, row_taps_two)

    def act_one(r):
        stacks = [col_stack(cg1, r + q + d1, d1, True) for q in range(2)]
        hid = two(stacks, wc1)
        acc = taps[2]
        for q in range(2):
            m = mask_row(mask, r + q)
            h = h1[r + q]
            slope = 1.0 + jnp.minimum(h.astype(F32), 0.0)
            a1[r + q] = (hid[q] * m * slope).astype(BF16)
            acc = acc + dot_nt(stacks[q][:, :W], h[:, :W])
        taps[2] = acc

    pairs(R, act_one)

    def last(r):
        stacks = [row_stack(a1[r + q], d1, True)[:, :W] for q in range(2)]
        mixed = two(stacks, wr1)
        acc = taps[3]
        for q in range(2):
            put_flat(flat, r + q, g1[r + q + d1, :, :W] + mixed[q])
            acc = acc + dot_nt(stacks[q], x[r + q])
        taps[3] = acc

    pairs(R, last)

    narrow(flat, out)


def backward_call(tiles, c, ctop, cbot, col_left, col_right, cor_top, cor_bot, wr, wc, x, h1, b1, h2):
    d1 = FIRST_SPACING
    return pl.pallas_call(
        backward_kernel,
        in_specs=[SM, ANY, ANY, ANY, VM, VM, VM, VM, VM, VM, ANY, ANY, ANY, ANY],
        out_specs=[VM, VM],
        out_shape=[
            jax.ShapeDtypeStruct((C, R, W), BF16),
            jax.ShapeDtypeStruct((4, 3 * C, C), F32),
        ],
        scratch_shapes=[
            pltpu.VMEM((R + 2 * HALO, C, E), BF16),
            pltpu.VMEM((R, C, E), BF16),
            pltpu.VMEM((R, C, E), BF16),
            pltpu.VMEM((R + 2 * d1, C, E), BF16),
            pltpu.VMEM((R, C, W), BF16),
            pltpu.VMEM((R + 2 * d1, C, E), BF16),
            pltpu.VMEM((R + 2 * d1, C, E), BF16),
            pltpu.VMEM((R + 2 * d1, C, E), F32),
            pltpu.VMEM((R, C, E), BF16),
            pltpu.VMEM((W // 128, C * R, 128), F32),
            pltpu.VMEM((3, 8, E), F32),
            pltpu.SemaphoreType.DMA((7,)),
        ],
        compiler_params=pltpu.CompilerParams(vmem_limit_bytes=VMEM_LIMIT),
    )(tiles, c, ctop, cbot, col_left, col_right, cor_top, cor_bot, wr, wc, x, h1, b1, h2)


def tap_sum(taps):
    flat = taps.reshape(-1, 128)
    wide = lax.axis_size("rows")
    part = lax.all_to_all(flat, "rows", 0, 0, tiled=True).reshape(wide, -1, 128).sum(0)
    cols = lax.axis_size("cols")
    spread = jnp.broadcast_to(part[None], (cols,) + part.shape).reshape(-1, 128)
    part = lax.all_to_all(spread, "cols", 0, 0, tiled=True).reshape(cols, -1, 128).sum(0)
    spread = jnp.broadcast_to(part[None], (wide,) + part.shape).reshape(-1, 128)
    whole = lax.all_to_all(spread, "rows", 0, 0, tiled=True)
    return whole.reshape(4, 3, C, C)


def on_device(x, tile_mask, wr, wc, cot):
    n_rows, n_cols = lax.axis_size("rows"), lax.axis_size("cols")
    factor = 1.0 / math.sqrt(R * n_rows * W * n_cols)
    down = [(i, i + 1) for i in range(n_rows - 1)]
    up = [(i + 1, i) for i in range(n_rows - 1)]
    right = [(i, i + 1) for i in range(n_cols - 1)]
    left = [(i + 1, i) for i in range(n_cols - 1)]

    xt, xtop, xbot, ct, ctop, cbot, to_left, to_right = pack_call(x, cot)
    col_right = lax.ppermute(to_left, "cols", left)
    col_left = lax.ppermute(to_right, "cols", right)
    xabove = lax.ppermute(xbot, "rows", down)
    xbelow = lax.ppermute(xtop, "rows", up)
    first = jnp.stack([col_left[:, :HG], col_right[:, :HG]], axis=1)
    last = jnp.stack([col_left[:, GROUPS - HG :], col_right[:, GROUPS - HG :]], axis=1)
    cor_bot = lax.ppermute(first, "rows", up)
    cor_top = lax.ppermute(last, "rows", down)
    cabove = lax.ppermute(cbot, "rows", down)
    cbelow = lax.ppermute(ctop, "rows", up)

    final, h1, b1, h2 = forward_call(
        tile_mask, xt, xabove, xbelow, col_left, col_right, cor_top, cor_bot, wr, wc
    )
    map_grad, taps = backward_call(
        tile_mask, ct, cabove, cbelow, col_left, col_right, cor_top, cor_bot, wr, wc, xt, h1, b1, h2
    )
    total = tap_sum(taps) * factor
    row_grad = jnp.stack([total[3], total[1]])
    col_grad = jnp.stack([total[2], total[0]])
    return final, map_grad, row_grad, col_grad


def solution(mesh):
    placed = (P(None, "rows", "cols"), P(), P(), P(), P(None, "rows", "cols"))
    return jax.shard_map(
        on_device,
        mesh=mesh,
        in_specs=placed,
        out_specs=(P(None, "rows", "cols"), P(None, "rows", "cols"), P(), P()),
        check_vma=False,
    )
```

profile of v0, /device:TPU:0, one launch (start us, length us, event | category | flops | bytes accessed | tf_op | source)
XLA Modules:
  0.0 200.9 jit_solution(8009127811918258634)
XLA Ops:
  0.6 10.3 %shard_map.84 = (bf16[32,64,512]{2,1,0:T(8,128)(2,1)}, bf16[12,64,512]{2,1,0:T(8,128)(2,1)}, bf16[12,64,512]{2,1,0:T(8,128)(2,1)}, bf16[32,64,512]{2,1,0:T(8,128...) custom-call(bf16[64,32,512]{2,1,0:T(8,128)(2,1)} %x_ref.1, ...), custom_call_target="tpu_custom_call" | custom-call | tf_op jit(solution)/shard_map/pallas_call | solution.py:84
  10.9 1.3 collective-permute-start.3
  12.2 3.0 %collective-permute-start.2 = (bf16[2,8,64,128]{3,2,1,0:T(8,128)(2,1)}, bf16[2,8,64,128]{3,2,1,0:T(8,128)(2,1)S(1)}, u32[]{:S(2)}, u32[]{:S(2)}) collective-permute-start(bf16[2,8,64,128]{3,2,1,0:T(8,128)(2,1)} %get-tuple-element.21), channel_id=1, source_target_pairs={{0,1},{1,2},{2,3},{4,5},{5,6},{6,7},{8,9},{9,10},{10,11},{12,13},{... | collective-permute-start | bytes 786440 | tf_op jit(solution)/shard_map/ppermute | solution.py:448
  15.2 4.0 %collective-permute-start = (bf16[12,64,512]{2,1,0:T(8,128)(2,1)}, bf16[12,64,512]{2,1,0:T(8,128)(2,1)S(1)}, u32[]{:S(2)}, u32[]{:S(2)}) collective-permute-start(bf16[12,64,512]{2,1,0:T(8,128)(2,1)} %get-tuple-element.19), channel_id=1, source_target_pairs={{0,4},{4,8},{8,12},{12,16},{16,20},{20,24},{24,28},{28,32},{32,36}... | collective-permute-start | bytes 2359304 | tf_op jit(solution)/shard_map/ppermute | solution.py:449
  19.2 1.3 collective-permute-start.1
  20.5 4.6 %collective-permute-start.6 = (bf16[12,64,512]{2,1,0:T(8,128)(2,1)}, bf16[12,64,512]{2,1,0:T(8,128)(2,1)S(1)}, u32[]{:S(2)}, u32[]{:S(2)}) collective-permute-start(bf16[12,64,512]{2,1,0:T(8,128)(2,1)} %get-tuple-element.25), channel_id=1, source_target_pairs={{0,4},{4,8},{8,12},{12,16},{16,20},{20,24},{24,28},{28,32},{32,36}... | collective-permute-start | bytes 2359304 | tf_op jit(solution)/shard_map/ppermute | solution.py:455
  25.1 0.0 collective-permute-done.3.col_right
  25.1 0.0 copy-start
  25.1 1.3 collective-permute-start.7
  26.5 0.0 collective-permute-done.2.col_left
  26.5 0.0 copy-start.1
  26.5 4.6 %collective-permute-start.4 = (bf16[2,2,3,64,128]{4,3,2,0,1:T(8,128)(2,1)S(1)}, bf16[2,2,3,64,128]{4,3,2,0,1:T(8,128)(2,1)S(1)}, u32[]{:S(2)}, u32[]{:S(2)}) collective-permute-start(bf16[2,2,3,64,128]{4,3,2,0,1:T(8,128)(2,1)S(1)} %pad_maximum_fusion), channel_id=1, source_target_pairs={{0,4},{4,8},{8,12},{12,16},{16,20},{20,24},{24,28},{28,32},{32,36}... | collective-permute-start | bytes 589832 | tf_op jit(solution)/shard_map/ppermute | solution.py:454
  31.1 25.3 %collective-permute-done.4 = bf16[2,2,3,64,128]{4,3,2,0,1:T(8,128)(2,1)S(1)} collective-permute-done((bf16[2,2,3,64,128]{4,3,2,0,1:T(8,128)(2,1)S(1)}, bf16[2,2,3,64,128]{4,3,2,0,1:T(8,128)(2,1)S(1)}, u32[]{:S(2)}, u32[]{:S(2)}) %collective-permute-start.4) | collective-permute-done | bytes 196640 | tf_op jit(solution)/shard_map/ppermute | solution.py:454
  56.5 1.3 collective-permute-start.5
  57.7 0.7 copy.19.cor_top
  58.4 7.1 %collective-permute-done.5.cor_bot = bf16[2,2,3,64,128]{4,3,2,1,0:T(8,128)(2,1)S(1)} collective-permute-done((bf16[2,2,3,64,128]{4,3,2,1,0:T(8,128)(2,1)S(1)}, bf16[2,2,3,64,128]{4,3,2,1,0:T(8,128)(2,1)S(1)}, u32[]{:S(2)}, u32[]{:S(2)}) %collective-permute-start.5) | collective-permute-done | bytes 196640 | tf_op jit(solution)/shard_map/ppermute | solution.py:453
  65.6 0.0 copy-start.2
  65.6 0.0 collective-permute-done.xtop
  65.6 0.0 copy-start.5
  65.6 0.0 collective-permute-done.1.xbot
  65.6 0.0 copy-start.6
  65.6 0.0 copy-done
  65.6 0.0 copy-done.1
  65.6 0.6 copy-done.2
  66.2 0.3 copy-done.5
  66.5 0.2 copy-done.6
  66.8 34.5 %shard_map.85 = (bf16[64,32,512]{2,1,0:T(8,128)(2,1)}, bf16[32,64,640]{2,1,0:T(8,128)(2,1)}, bf16[32,64,640]{2,1,0:T(8,128)(2,1)}, bf16[40,64,640]{2,1,0:T(8,128)(2,1)}) custom-call(s32[8,16]{1,0:T(8,128)} %tiles.3, bf16[32,64,512]{2,1,0:T(8,128)(2,1)} %get-tuple-element.18.x.x_in, bf16[12,64,512]{2,1,0:T(8,128)(2,1)} %copy-done.5, ...), custom_call_target="tpu_custom_call" | custom-call | tf_op jit(solution)/shard_map/pallas_call | solution.py:270
  101.3 0.0 collective-permute-done.6.ctop
  101.3 0.0 copy-start.3
  101.3 0.0 collective-permute-done.7.cbot
  101.3 0.0 copy-start.4
  101.3 0.9 copy-done.3
  102.2 0.3 copy-done.4
  102.5 44.0 %shard_map.86 = (bf16[64,32,512]{2,1,0:T(8,128)(2,1)}, f32[4,192,64]{2,1,0:T(8,128)}) custom-call(s32[8,16]{1,0:T(8,128)} %tiles.3, bf16[32,64,512]{2,1,0:T(8,128)(2,1)} %get-tuple-element.24.c, bf16[12,64,512]{2,1,0:T(8,128)(2,1)} %copy-done.3, bf16[12,64,512]{2,1,0:T(8,128)(2,1)} %copy-done.4, bf16[2,8,64,128]{3,2,1,0:T(8,128)(2,1)} %copy-done.1, ...), custom_call_target="tpu_custom_call" | custom-call | tf_op jit(solution)/shard_map/pallas_call | solution.py:400
  146.5 1.1 all_to_all.14
  147.7 22.2 %all_to_all.21 = f32[32,12,128]{2,1,0:T(8,128)S(1)} all-to-all(f32[32,12,128]{2,1,0:T(8,128)S(1)} %all_to_all.14), channel_id=1, replica_groups=mesh['rows'=32,'cols'=4] {'rows'}, dimensions={0} | all-to-all | bytes 393216 | tf_op jit(solution)/shard_map/all_to_all | solution.py:429
  169.9 17.4 %all_to_all.22 = f32[4,12,128]{2,1,0:T(8,128)S(1)} all-to-all(f32[4,12,128]{2,1,0:T(8,128)S(1)} %broadcast_in_dim.4), channel_id=1, replica_groups=mesh['rows'=32,'cols'=4] {'cols'}, dimensions={0} | all-to-all | bytes 49152 | tf_op jit(solution)/shard_map/all_to_all | solution.py:432
  187.3 12.4 %all_to_all.23 = f32[32,12,128]{2,1,0:T(8,128)S(1)} all-to-all(f32[32,12,128]{2,1,0:T(8,128)S(1)} %broadcast_in_dim.5), channel_id=1, replica_groups=mesh['rows'=32,'cols'=4] {'rows'}, dimensions={0} | all-to-all | bytes 393216 | tf_op jit(solution)/shard_map/all_to_all | solution.py:434
  199.8 0.1 slice.43
  199.8 0.1 slice.41
  199.9 0.1 slice.47
  200.0 0.1 slice.45
  200.1 0.8 pad_maximum_fusion.2
  (10 shorter events, 0.2 us)
Async XLA Ops:
  10.9 14.2 %collective-permute-start.3 = (bf16[2,8,64,128]{3,2,1,0:T(8,128)(2,1)}, bf16[2,8,64,128]{3,2,1,0:T(8,128)(2,1)S(1)}, u32[]{:S(2)}, u32[]{:S(2)}) collective-permute-start(bf16[2,8,64,128]{3,2,1,0:T(8,128)(2,1)} %get-tuple-element.22), channel_id=1, source_target_pairs={{1,0},{2,1},{3,2},{5,4},{6,5},{7,6},{9,8},{10,9},{11,10},{13,12},{... | collective-permute-start | bytes 786440 | tf_op jit(solution)/shard_map/ppermute | solution.py:447
  12.2 14.3 %collective-permute-start.2 = (bf16[2,8,64,128]{3,2,1,0:T(8,128)(2,1)}, bf16[2,8,64,128]{3,2,1,0:T(8,128)(2,1)S(1)}, u32[]{:S(2)}, u32[]{:S(2)}) collective-permute-start(bf16[2,8,64,128]{3,2,1,0:T(8,128)(2,1)} %get-tuple-element.21), channel_id=1, source_target_pairs={{0,1},{1,2},{2,3},{4,5},{5,6},{6,7},{8,9},{9,10},{10,11},{12,13},{... | collective-permute-start | bytes 786440 | tf_op jit(solution)/shard_map/ppermute | solution.py:448
  15.2 50.3 %collective-permute-start = (bf16[12,64,512]{2,1,0:T(8,128)(2,1)}, bf16[12,64,512]{2,1,0:T(8,128)(2,1)S(1)}, u32[]{:S(2)}, u32[]{:S(2)}) collective-permute-start(bf16[12,64,512]{2,1,0:T(8,128)(2,1)} %get-tuple-element.19), channel_id=1, source_target_pairs={{0,4},{4,8},{8,12},{12,16},{16,20},{20,24},{24,28},{28,32},{32,36}... | collective-permute-start | bytes 2359304 | tf_op jit(solution)/shard_map/ppermute | solution.py:449
  19.2 46.4 %collective-permute-start.1 = (bf16[12,64,512]{2,1,0:T(8,128)(2,1)}, bf16[12,64,512]{2,1,0:T(8,128)(2,1)S(1)}, u32[]{:S(2)}, u32[]{:S(2)}) collective-permute-start(bf16[12,64,512]{2,1,0:T(8,128)(2,1)} %get-tuple-element.20), channel_id=1, source_target_pairs={{4,0},{8,4},{12,8},{16,12},{20,16},{24,20},{28,24},{32,28},{36,32}... | collective-permute-start | bytes 2359304 | tf_op jit(solution)/shard_map/ppermute | solution.py:450
  20.5 80.8 %collective-permute-start.6 = (bf16[12,64,512]{2,1,0:T(8,128)(2,1)}, bf16[12,64,512]{2,1,0:T(8,128)(2,1)S(1)}, u32[]{:S(2)}, u32[]{:S(2)}) collective-permute-start(bf16[12,64,512]{2,1,0:T(8,128)(2,1)} %get-tuple-element.25), channel_id=1, source_target_pairs={{0,4},{4,8},{8,12},{12,16},{16,20},{20,24},{24,28},{28,32},{32,36}... | collective-permute-start | bytes 2359304 | tf_op jit(solution)/shard_map/ppermute | solution.py:455
  25.1 40.5 %copy-start = (bf16[2,8,64,128]{3,2,1,0:T(8,128)(2,1)}, bf16[2,8,64,128]{3,2,1,0:T(8,128)(2,1)S(1)}, u32[]{:S(2)}) copy-start(bf16[2,8,64,128]{3,2,1,0:T(8,128)(2,1)S(1)} %collective-permute-done.3.col_right) | copy-start | bytes 786436
  25.1 76.2 %collective-permute-start.7 = (bf16[12,64,512]{2,1,0:T(8,128)(2,1)}, bf16[12,64,512]{2,1,0:T(8,128)(2,1)S(1)}, u32[]{:S(2)}, u32[]{:S(2)}) collective-permute-start(bf16[12,64,512]{2,1,0:T(8,128)(2,1)} %get-tuple-element.26), channel_id=1, source_target_pairs={{4,0},{8,4},{12,8},{16,12},{20,16},{24,20},{28,24},{32,28},{36,32}... | collective-permute-start | bytes 2359304 | tf_op jit(solution)/shard_map/ppermute | solution.py:456
  26.5 39.1 %copy-start.1 = (bf16[2,8,64,128]{3,2,1,0:T(8,128)(2,1)}, bf16[2,8,64,128]{3,2,1,0:T(8,128)(2,1)S(1)}, u32[]{:S(2)}) copy-start(bf16[2,8,64,128]{3,2,1,0:T(8,128)(2,1)S(1)} %collective-permute-done.2.col_left) | copy-start | bytes 786436
  26.5 29.9 %collective-permute-start.4 = (bf16[2,2,3,64,128]{4,3,2,0,1:T(8,128)(2,1)S(1)}, bf16[2,2,3,64,128]{4,3,2,0,1:T(8,128)(2,1)S(1)}, u32[]{:S(2)}, u32[]{:S(2)}) collective-permute-start(bf16[2,2,3,64,128]{4,3,2,0,1:T(8,128)(2,1)S(1)} %pad_maximum_fusion), channel_id=1, source_target_pairs={{0,4},{4,8},{8,12},{12,16},{16,20},{20,24},{24,28},{28,32},{32,36}... | collective-permute-start | bytes 589832 | tf_op jit(solution)/shard_map/ppermute | solution.py:454
  56.5 9.1 %collective-permute-start.5 = (bf16[2,2,3,64,128]{4,3,2,1,0:T(8,128)(2,1)S(1)}, bf16[2,2,3,64,128]{4,3,2,1,0:T(8,128)(2,1)S(1)}, u32[]{:S(2)}, u32[]{:S(2)}) collective-permute-start(bf16[2,2,3,64,128]{4,3,2,1,0:T(8,128)(2,1)S(1)} %pad_maximum_fusion.1), channel_id=1, source_target_pairs={{4,0},{8,4},{12,8},{16,12},{20,16},{24,20},{28,24},{32,28},{36,32}... | collective-permute-start | bytes 589832 | tf_op jit(solution)/shard_map/ppermute | solution.py:453
  65.6 0.7 copy-start.2
  65.6 1.0 copy-start.5
  65.6 1.2 copy-start.6
  101.3 0.9 copy-start.3
  101.3 1.2 copy-start.4
where the time goes:
time: 202 us; the launch traced here: 201 us
  Pallas kernels  88.8 us (44%)
  blocking collectives  52 us (26%)
  waiting for transfers between devices  32.5 us (16%)
  starting transfers between devices  21.3 us (11%)
  local copies, waits for them, and re-layouts  4.52 us (2%)
    pallas_call x1, Pallas kernels, backward_call(): pl.pallas_call(backward_kernel, in_specs=[SM, ANY, ANY, ANY, VM, VM, VM,...  44 us
    pallas_call x1, Pallas kernels, forward_call(): pl.pallas_call(forward_kernel, in_specs=[SM, ANY, ANY, ANY, VM, VM, VM, V...  34.5 us
    ppermute x1, waiting for transfers between devices, on_device(): cor_top = lax.ppermute(last, 'rows', down)  25.3 us
    all_to_all x1, blocking collectives, tap_sum(): lax.all_to_all(flat, 'rows', 0, 0, tiled=True).reshape(wide, -1, 128).sum(0)  22.2 us
    all_to_all x1, blocking collectives, tap_sum(): lax.all_to_all(spread, 'cols', 0, 0, tiled=True).reshape(cols, -1, 128)  17.4 us
    all_to_all x1, blocking collectives, tap_sum(): whole = lax.all_to_all(spread, 'rows', 0, 0, tiled=True)  12.4 us
    pallas_call x1, Pallas kernels, pack_call(): pl.pallas_call(pack_kernel, grid=(W // 128, 2), in_specs=[native, native]...  10.3 us
    ppermute x1, waiting for transfers between devices, on_device(): cor_bot = lax.ppermute(first, 'rows', up)  7.12 us
  transfers between devices with their start and end apart: 8, of which 2 were waited for; matrix products, arithmetic and copies ran while one was open for 0% of the time, Pallas kernels for 17%

commit v1 on v0

v1 whole, which is shorter than its diff:
```python
import functools
import math

import jax
import jax.numpy as jnp
from jax import lax
from jax.experimental import pallas as pl
from jax.experimental.pallas import tpu as pltpu
from jax.sharding import Mesh, PartitionSpec as P

FIRST_SPACING = 4
SECOND_SPACING = 8
TILE = 128
C = 64
R = 32
W = 512
E = 640
HALO = 12
EDGE = 32
GROUPS = R // 4
HG = HALO // 4
F32 = jnp.float32
BF16 = jnp.bfloat16
VMEM_LIMIT = 60 * 1024 * 1024


def dot(a, b):
    return jnp.dot(a, b, preferred_element_type=F32)


def dot_nt(a, b):
    return lax.dot_general(a, b, (((1,), (1,)), ((), ())), preferred_element_type=F32)


def turn(block):
    return jnp.swapaxes(block, 0, 1)


def pack(out, a, i, block, first):
    lane = lax.broadcasted_iota(jnp.int32, (C, 128), 1)
    for g in range(4):
        acc = jnp.zeros((C, 128), F32)
        for k in range(4):
            v = block[4 * g + k].astype(F32)
            shift = (32 * k - first) % 128
            if shift:
                v = pltpu.roll(v, shift, 1)
            acc = jnp.where(lane // 32 == k, v, acc)
        out[a, i * 4 + g] = acc.astype(BF16)


def pack_x_kernel(x_ref, c_ref, xt, xtop, xbot, to_left, to_right):
    w = pl.program_id(0)
    i = pl.program_id(1)
    xt[...] = turn(x_ref[...])

    @pl.when(i == 0)
    def _():
        xtop[...] = xt[0:HALO]

    @pl.when(i == 1)
    def _():
        xbot[...] = xt[16 - HALO : 16]

    for out, at, first in ((to_left, 0, 0), (to_right, W // 128 - 1, 96)):

        @pl.when(w == at)
        def _():
            pack(out, 0, i, xt[...], first)
            pack(out, 1, i, turn(c_ref[...]), first)


def turn_c_kernel(c_ref, after, ct, ctop, cbot):
    i = pl.program_id(1)
    ct[...] = turn(c_ref[...])

    @pl.when(i == 0)
    def _():
        ctop[...] = ct[0:HALO]

    @pl.when(i == 1)
    def _():
        cbot[...] = ct[16 - HALO : 16]


NATIVE = pl.BlockSpec((C, 16, 128), lambda w, i: (0, i, w))
TURNED = pl.BlockSpec((16, C, 128), lambda w, i: (i, 0, w))
HALO_ROWS = pl.BlockSpec((HALO, C, 128), lambda w, i: (0, 0, w))
FULL = jax.ShapeDtypeStruct((R, C, W), BF16)
PART = jax.ShapeDtypeStruct((HALO, C, W), BF16)


def pack_x(x, c):
    edge = pl.BlockSpec((2, GROUPS, C, 128), lambda w, i: (0, 0, 0, 0))
    edges = jax.ShapeDtypeStruct((2, GROUPS, C, 128), BF16)
    return pl.pallas_call(
        pack_x_kernel,
        grid=(W // 128, 2),
        in_specs=[NATIVE, NATIVE],
        out_specs=[TURNED, HALO_ROWS, HALO_ROWS, edge, edge],
        out_shape=[FULL, PART, PART, edges, edges],
        compiler_params=pltpu.CompilerParams(vmem_limit_bytes=VMEM_LIMIT),
        name="pack_x",
    )(x, c)


def turn_c(c, after):
    return pl.pallas_call(
        turn_c_kernel,
        grid=(W // 128, 2),
        in_specs=[NATIVE, pl.BlockSpec(memory_space=pl.ANY)],
        out_specs=[TURNED, HALO_ROWS, HALO_ROWS],
        out_shape=[FULL, PART, PART],
        compiler_params=pltpu.CompilerParams(vmem_limit_bytes=VMEM_LIMIT),
        name="turn_c",
    )(c, after)


def build_mask(tiles, mask):
    row_dev, col_dev = lax.axis_index("rows"), lax.axis_index("cols")
    n_rows, n_cols = tiles.shape
    first_row, first_tile = row_dev * R, col_dev * (W // TILE)
    lane = lax.broadcasted_iota(jnp.int32, (16, 128), 1)

    def value(p, ct):
        cell = first_row + (-1, 0, R)[p]
        inside = (cell >= 0) & (cell < n_rows * TILE) & (ct >= 0) & (ct < n_cols)
        rt = jnp.clip(cell, 0, n_rows * TILE - 1) // TILE
        return jnp.where(inside, tiles[rt, jnp.clip(ct, 0, n_cols - 1)], 0)

    for p in range(3):
        for t in range(W // 128):
            cell = jnp.full((16, 128), value(p, first_tile + t), jnp.int32)
            mask[p, :, t * 128 : (t + 1) * 128] = cell.astype(F32).astype(BF16)
        right = jnp.full((16, 128), value(p, first_tile + W // TILE), jnp.int32)
        left = jnp.full((16, 128), value(p, first_tile - 1), jnp.int32)
        mask[p, :, W:E] = jnp.where(lane < 64, right, left).astype(F32).astype(BF16)


def masked(v, mask, r, at):
    if isinstance(r, int):
        p = int(r >= 0) + int(r >= R)
    else:
        p = (r >= 0).astype(jnp.int32) + (r >= R).astype(jnp.int32)
    m = mask[p, :, at]
    return v * jnp.concatenate([m] * (C // 16), axis=0)


def unpack_edges(left, right, dst, first):
    lane = lax.broadcasted_iota(jnp.int32, (C, 128), 1)
    for k in range(4):
        rv, lv = right.astype(F32), left.astype(F32)
        if k:
            rv = pltpu.roll(rv, 128 - 32 * k, 1)
        if k != 3:
            lv = pltpu.roll(lv, 96 - 32 * k, 1)
        tile = jnp.where(lane < EDGE, rv, jnp.where(lane >= 128 - EDGE, lv, 0.0))
        dst[first + k, :, W:E] = tile.astype(BF16)


def unpack_all(a, col_left, col_right, cor_top, cor_bot, dst):
    for g in range(HG):
        unpack_edges(cor_top[a, 0, g], cor_top[a, 1, g], dst, 4 * g)
        unpack_edges(cor_bot[a, 0, g], cor_bot[a, 1, g], dst, HALO + R + 4 * g)

    def own(g, _):
        unpack_edges(col_left[a, g], col_right[a, g], dst, HALO + 4 * g)
        return 0

    lax.fori_loop(0, GROUPS, own, 0)


def shifted(v, d):
    return pltpu.roll(v, (-d) % v.shape[1], 1)


def row_stack(v, d, reverse):
    ahead, behind = shifted(v, d), shifted(v, -d)
    parts = [ahead, v, behind] if reverse else [behind, v, ahead]
    return jnp.concatenate(parts, axis=0)


def col_stack(ref, r, d, at):
    return jnp.concatenate([ref[r + d, :, at], ref[r, :, at], ref[r - d, :, at]], axis=0)


def forward_matrix(w):
    return jnp.concatenate([w[j].astype(F32).T for j in range(3)], axis=0).T.astype(BF16)


def backward_matrix(w, order=(0, 1, 2)):
    return jnp.concatenate([w[j].astype(F32) for j in order], axis=0).T.astype(BF16)


def two_rows(matrix):
    none = jnp.zeros((C, C), BF16)
    return jnp.concatenate(
        [jnp.concatenate([matrix, none], axis=1), jnp.concatenate([none, matrix], axis=1)], axis=0
    )


MAIN = (slice(0, 256), slice(256, 512))
TAIL = slice(W, E)


def loop(count, step, body):
    def one(i, _):
        body(i * step)
        return 0

    lax.fori_loop(0, count // step, one, 0)


def conv_columns(ref, rows, d, matrix, post, tail=True):
    def window(r, at):
        return jnp.concatenate([ref[r + k * d, :, at] for k in (-1, 0, 1, 2)], axis=0)

    for r in rows:
        for at in MAIN:
            both = dot(matrix, window(r, at))
            post(r, at, both[:C])
            post(r + d, at, both[C:])
    if tail:
        for r, s in zip(rows[::2], rows[1::2]):
            both = dot(matrix, jnp.concatenate([window(r, TAIL), window(s, TAIL)], axis=1))
            for row, half in ((r, both[:, :128]), (s, both[:, 128:])):
                post(row, TAIL, half[:C])
                post(row + d, TAIL, half[C:])


def conv_columns_single(ref, rows, d, matrix, post):
    def window(r, at):
        return jnp.concatenate([ref[r + k * d, :, at] for k in (-1, 0, 1)], axis=0)

    for r in rows:
        for at in MAIN:
            post(r, at, dot(matrix, window(r, at)))
    for r, s in zip(rows[::2], rows[1::2]):
        both = dot(matrix, jnp.concatenate([window(r, TAIL), window(s, TAIL)], axis=1))
        post(r, TAIL, both[:, :128])
        post(s, TAIL, both[:, 128:])


def conv_rows(ref, rows, d, reverse, matrix, post, tail=True):
    stacks = []
    for r in rows:
        stack = row_stack(ref[r], d, reverse)
        stacks.append(stack)
        for at in MAIN:
            post(r, at, dot(matrix, stack[:, at]))
    if tail:
        for q in range(0, len(rows), 2):
            both = dot(matrix, jnp.concatenate([stacks[q][:, TAIL], stacks[q + 1][:, TAIL]], axis=1))
            post(rows[q], TAIL, both[:, :128])
            post(rows[q + 1], TAIL, both[:, 128:])
    return stacks


def elu(p):
    return jnp.where(p > 0, p, jnp.exp(p) - 1.0)


def turn_out(src, out):
    for i in range(R // 16):
        for t in range(W // 128):
            at = slice(t * 128, (t + 1) * 128)
            out[:, i * 16 : (i + 1) * 16, at] = turn(src[i * 16 : (i + 1) * 16, :, at])


def forward_kernel(
    tiles, x, xtop, xbot, col_left, col_right, cor_top, cor_bot, wr, wc,
    out, h1_out, b1_out, h2_out,
    xe, h1, b1, h2, flat, mask, sems,
):
    loads = [
        pltpu.make_async_copy(x, xe.at[HALO : HALO + R, :, 0:W], sems.at[0]),
        pltpu.make_async_copy(xtop, xe.at[0:HALO, :, 0:W], sems.at[1]),
        pltpu.make_async_copy(xbot, xe.at[HALO + R :, :, 0:W], sems.at[2]),
    ]
    for load in loads:
        load.start()
    build_mask(tiles, mask)
    unpack_all(0, col_left, col_right, cor_top, cor_bot, xe)
    wr1, wr2 = forward_matrix(wr[0]), forward_matrix(wr[1])
    wc1, wc2 = two_rows(forward_matrix(wc[0])), two_rows(forward_matrix(wc[1]))
    for load in loads:
        load.wait()

    d1, d2 = FIRST_SPACING, SECOND_SPACING

    def hidden_one(r):
        def post(row, at, pre):
            h1[row, :, at] = masked(elu(pre).astype(BF16), mask, row - HALO, at)

        conv_rows(xe, [r + q for q in range(STEP)], d1, False, wr1, post)

    loop(R + 2 * HALO, STEP, hidden_one)
    save_h1 = pltpu.make_async_copy(h1.at[HALO : HALO + R], h1_out, sems.at[3])
    save_h1.start()

    def block_one(r):
        def post(row, at, col):
            b1[row - d1, :, at] = xe[row, :, at] + masked(col.astype(BF16), mask, row - HALO, at)

        conv_columns(h1, [r + d1 + q for q in range(d1)], d1, wc1, post)

    loop(R + 2 * d2, 2 * d1, block_one)
    save_b1 = pltpu.make_async_copy(b1.at[d2 : d2 + R], b1_out, sems.at[4])
    save_b1.start()

    def hidden_two(r):
        def post(row, at, pre):
            h2[row, :, at] = masked(elu(pre).astype(BF16), mask, row - d2, at)

        conv_rows(b1, [r + q for q in range(STEP)], d2, False, wr2, post)

    loop(R + 2 * d2, STEP, hidden_two)
    save_h2 = pltpu.make_async_copy(h2.at[d2 - d1 : d2 + R + d1], h2_out, sems.at[5])
    save_h2.start()

    def last(i):
        r = (i // d2) * 2 * d2 + i % d2

        def post(row, at, col):
            flat[row - d2, :, at] = b1[row, :, at] + masked(col.astype(BF16), mask, row - d2, at)

        conv_columns(h2, [r + d2 + q for q in range(4)], d2, wc2, post, tail=False)

    loop(R // 2, 4, last)
    turn_out(flat, out)
    save_h1.wait()
    save_b1.wait()
    save_h2.wait()


ANY = pl.BlockSpec(memory_space=pl.ANY)
VM = pl.BlockSpec(memory_space=pltpu.VMEM)
SM = pl.BlockSpec(memory_space=pltpu.SMEM)
STEP = 8


def forward_call(tiles, x, xtop, xbot, col_left, col_right, cor_top, cor_bot, wr, wc):
    d1, d2 = FIRST_SPACING, SECOND_SPACING
    return pl.pallas_call(
        forward_kernel,
        in_specs=[SM, ANY, ANY, ANY, VM, VM, VM, VM, VM, VM],
        out_specs=[VM, ANY, ANY, ANY],
        out_shape=[
            jax.ShapeDtypeStruct((C, R, W), BF16),
            jax.ShapeDtypeStruct((R, C, E), BF16),
            jax.ShapeDtypeStruct((R, C, E), BF16),
            jax.ShapeDtypeStruct((R + 2 * d1, C, E), BF16),
        ],
        scratch_shapes=[
            pltpu.VMEM((R + 2 * HALO, C, E), BF16),
            pltpu.VMEM((R + 2 * HALO, C, E), BF16),
            pltpu.VMEM((R + 2 * d2, C, E), BF16),
            pltpu.VMEM((R + 2 * d2, C, E), BF16),
            pltpu.VMEM((R, C, W), BF16),
            pltpu.VMEM((3, 16, E), BF16),
            pltpu.SemaphoreType.DMA((6,)),
        ],
        compiler_params=pltpu.CompilerParams(vmem_limit_bytes=VMEM_LIMIT),
        cost_estimate=pl.CostEstimate(flops=20_000_000_000, bytes_accessed=20_000_000, transcendentals=0),
        name="forward",
    )(tiles, x, xtop, xbot, col_left, col_right, cor_top, cor_bot, wr, wc)


def backward_kernel(
    tiles, c, ctop, cbot, col_left, col_right, cor_top, cor_bot, wr, wc, x_in, h1_in, b1_in, h2_in,
    out, taps,
    ce, cm, h1, b1, h2, x, a2, cg1, g1, a1, flat, mask, sems,
):
    d1, d2 = FIRST_SPACING, SECOND_SPACING
    loads = [
        pltpu.make_async_copy(c, ce.at[HALO : HALO + R, :, 0:W], sems.at[0]),
        pltpu.make_async_copy(ctop, ce.at[0:HALO, :, 0:W], sems.at[1]),
        pltpu.make_async_copy(cbot, ce.at[HALO + R :, :, 0:W], sems.at[2]),
    ]
    late = [
        pltpu.make_async_copy(h2_in, h2, sems.at[3]),
        pltpu.make_async_copy(b1_in, b1, sems.at[4]),
        pltpu.make_async_copy(h1_in, h1, sems.at[5]),
        pltpu.make_async_copy(x_in, x, sems.at[6]),
    ]
    for load in loads + late:
        load.start()
    build_mask(tiles, mask)
    unpack_all(1, col_left, col_right, cor_top, cor_bot, ce)
    wr1, wr2 = backward_matrix(wr[0]), backward_matrix(wr[1])
    wc1, wc2 = backward_matrix(wc[0], (2, 1, 0)), backward_matrix(wc[1], (2, 1, 0))
    wc1w, wc2w = two_rows(wc1), two_rows(wc2)
    taps[...] = jnp.zeros_like(taps)
    for load in loads:
        load.wait()

    def mask_cot(r):
        for q in range(4):
            cm[r + q] = masked(ce[r + q], mask, r + q - HALO, slice(0, E))

    loop(R + 2 * HALO, 4, mask_cot)
    late[0].wait()

    up = HALO - d1

    def post_two(row, at, hid):
        slope = 1.0 + jnp.minimum(h2[row - up, :, at], 0).astype(F32)
        a2[row - up, :, at] = masked((hid * slope).astype(BF16), mask, row - HALO, at)

    def act_two(i):
        r = (i // d2) * 2 * d2 + i % d2
        conv_columns(cm, [r + up + q for q in range(4)], d2, wc2w, post_two)

    loop(R // 2, 4, act_two)
    conv_columns_single(cm, [R + up + q for q in range(2 * d1)], d2, wc2, post_two)
    late[1].wait()

    def add_taps(k, left, right):
        taps[k] += dot_nt(jnp.concatenate(left, axis=1), jnp.concatenate(right, axis=1))

    own = slice(0, W)

    def col_taps_two(r):
        rows = [r + q for q in range(4)]
        add_taps(0, [col_stack(cm, s + HALO, d2, own) for s in rows], [h2[s + d1, :, own] for s in rows])

    loop(R, 4, col_taps_two)

    def post_one(row, at, mixed):
        g = ce[row + up, :, at].astype(F32) + mixed
        cg1[row, :, at] = masked(g.astype(BF16), mask, row - d1, at)
        if at != TAIL:
            g1[row, :, at] = g

    def grad_one(r):
        rows = [r + q + d1 for q in range(4)]
        stacks = conv_rows(a2, rows, d2, True, wr2, post_one)
        add_taps(1, [s[:, own] for s in stacks], [b1[s - d1, :, own] for s in rows])

    for first in (0, R + d1):
        conv_rows(a2, [first + q for q in range(d1)], d2, True, wr2, post_one)
    loop(R, 4, grad_one)
    late[2].wait()
    late[3].wait()

    def act_one(r):
        def post(row, at, hid):
            slope = 1.0 + jnp.minimum(h1[row - d1, :, at], 0).astype(F32)
            a1[row - d1, :, at] = masked((hid * slope).astype(BF16), mask, row - d1, at)

        rows = [r + q for q in range(2 * d1)]
        conv_columns(cg1, [s + d1 for s in rows[:d1]], d1, wc1w, post)
        add_taps(2, [col_stack(cg1, s + d1, d1, own) for s in rows], [h1[s, :, own] for s in rows])

    loop(R, 2 * d1, act_one)

    def last(r):
        def post(row, at, mixed):
            flat[row, :, at] = (g1[row + d1, :, at] + mixed).astype(BF16)

        rows = [r + q for q in range(4)]
        stacks = conv_rows(a1, rows, d1, True, wr1, post, tail=False)
        add_taps(3, [s[:, own] for s in stacks], [x[s] for s in rows])

    loop(R, 4, last)
    turn_out(flat, out)


def backward_call(tiles, c, ctop, cbot, col_left, col_right, cor_top, cor_bot, wr, wc, x, h1, b1, h2):
    d1 = FIRST_SPACING
    return pl.pallas_call(
        backward_kernel,
        in_specs=[SM, ANY, ANY, ANY, VM, VM, VM, VM, VM, VM, ANY, ANY, ANY, ANY],
        out_specs=[VM, VM],
        out_shape=[
            jax.ShapeDtypeStruct((C, R, W), BF16),
            jax.ShapeDtypeStruct((4, 3 * C, C), F32),
        ],
        scratch_shapes=[
            pltpu.VMEM((R + 2 * HALO, C, E), BF16),
            pltpu.VMEM((R + 2 * HALO, C, E), BF16),
            pltpu.VMEM((R, C, E), BF16),
            pltpu.VMEM((R, C, E), BF16),
            pltpu.VMEM((R + 2 * d1, C, E), BF16),
            pltpu.VMEM((R, C, W), BF16),
            pltpu.VMEM((R + 2 * d1, C, E), BF16),
            pltpu.VMEM((R + 2 * d1, C, E), BF16),
            pltpu.VMEM((R + 2 * d1, C, W), F32),
            pltpu.VMEM((R, C, E), BF16),
            pltpu.VMEM((R, C, W), BF16),
            pltpu.VMEM((3, 16, E), BF16),
            pltpu.SemaphoreType.DMA((7,)),
        ],
        compiler_params=pltpu.CompilerParams(vmem_limit_bytes=VMEM_LIMIT),
        cost_estimate=pl.CostEstimate(flops=20_000_000_000, bytes_accessed=20_000_000, transcendentals=0),
        name="backward",
    )(tiles, c, ctop, cbot, col_left, col_right, cor_top, cor_bot, wr, wc, x, h1, b1, h2)


def tap_sum(taps):
    flat = taps.reshape(-1, 128)
    wide = lax.axis_size("rows")
    part = lax.all_to_all(flat, "rows", 0, 0, tiled=True).reshape(wide, -1, 128).sum(0)
    cols = lax.axis_size("cols")
    spread = jnp.broadcast_to(part[None], (cols,) + part.shape).reshape(-1, 128)
    part = lax.all_to_all(spread, "cols", 0, 0, tiled=True).reshape(cols, -1, 128).sum(0)
    spread = jnp.broadcast_to(part[None], (wide,) + part.shape).reshape(-1, 128)
    whole = lax.all_to_all(spread, "rows", 0, 0, tiled=True)
    return whole.reshape(4, 3, C, C)


def on_device(x, tile_mask, wr, wc, cot):
    n_rows, n_cols = lax.axis_size("rows"), lax.axis_size("cols")
    factor = 1.0 / math.sqrt(R * n_rows * W * n_cols)
    down = [(i, i + 1) for i in range(n_rows - 1)]
    up = [(i + 1, i) for i in range(n_rows - 1)]
    right = [(i, i + 1) for i in range(n_cols - 1)]
    left = [(i + 1, i) for i in range(n_cols - 1)]

    xt, xtop, xbot, to_left, to_right = pack_x(x, cot)
    col_right = lax.ppermute(to_left, "cols", left)
    col_left = lax.ppermute(to_right, "cols", right)
    xabove = lax.ppermute(xbot, "rows", down)
    xbelow = lax.ppermute(xtop, "rows", up)
    first = jnp.stack([col_left[:, :HG], col_right[:, :HG]], axis=1)
    last = jnp.stack([col_left[:, GROUPS - HG :], col_right[:, GROUPS - HG :]], axis=1)
    cor_bot = lax.ppermute(first, "rows", up)
    cor_top = lax.ppermute(last, "rows", down)
    ct, ctop, cbot = turn_c(cot, col_left)
    cabove = lax.ppermute(cbot, "rows", down)
    cbelow = lax.ppermute(ctop, "rows", up)

    final, h1, b1, h2 = forward_call(
        tile_mask, xt, xabove, xbelow, col_left, col_right, cor_top, cor_bot, wr, wc
    )
    map_grad, taps = backward_call(
        tile_mask, ct, cabove, cbelow, col_left, col_right, cor_top, cor_bot, wr, wc, xt, h1, b1, h2
    )
    total = tap_sum(taps) * factor
    row_grad = jnp.stack([total[3], total[1]])
    col_grad = jnp.stack([total[2], total[0]])
    return final, map_grad, row_grad, col_grad


def solution(mesh):
    placed = (P(None, "rows", "cols"), P(), P(), P(), P(None, "rows", "cols"))
    return jax.shard_map(
        on_device,
        mesh=mesh,
        in_specs=placed,
        out_specs=(P(None, "rows", "cols"), P(None, "rows", "cols"), P(), P()),
        check_vma=False,
    )
```

time: 202 us -> 151 us (0.75)
  Pallas kernels: 88.8 us -> 57.2 us
  waiting for transfers between devices: 32.5 us -> 4.7 us
  blocking collectives: 52 us -> 60.3 us
    ppermute x1, waiting for transfers between devices: 25.3 us -> 2.08 us  [on_device(): cor_top = lax.ppermute(last, 'rows', down)]
    pallas_call x1, Pallas kernels: 44 us -> 25.4 us  [backward_call(): pl.pallas_call(backward_kernel, in_specs=[SM, ANY, ANY, ANY, VM, VM, VM,...]
    pallas_call x1, Pallas kernels: 34.5 us -> 18.1 us  [forward_call(): pl.pallas_call(forward_kernel, in_specs=[SM, ANY, ANY, ANY, VM, VM, VM, V...]
    all_to_all x1, blocking collectives: 17.4 us -> 29 us  [tap_sum(): lax.all_to_all(spread, 'cols', 0, 0, tiled=True).reshape(cols, -1, 128)]
    ppermute x1, waiting for transfers between devices: 7.12 us -> 2.6 us  [on_device(): cor_bot = lax.ppermute(first, 'rows', up)]
    pallas_call x1 -> x2, Pallas kernels: 10.3 us -> 13.8 us  [the longest x1 7.37 us: pack_x(): pl.pallas_call(pack_x_kernel, grid=(W // 128, 2), in_specs=[NATIVE, NATIV...]
    all_to_all x1, blocking collectives: 22.2 us -> 18.9 us  [tap_sum(): lax.all_to_all(flat, 'rows', 0, 0, tiled=True).reshape(wide, -1, 128).sum(0)]
  transfers between devices with their start and end apart: 8 -> 8, of which waited for: 2 -> 2; matrix products, arithmetic and copies ran while one was open for 0% -> 1% of each run, Pallas kernels for 17% -> 16%
where the time goes in v1:
time: 151 us; the launch traced here: 150 us
  blocking collectives  60.3 us (40%)
  Pallas kernels  57.2 us (38%)
  starting transfers between devices  21.3 us (14%)
  waiting for transfers between devices  4.7 us (3%)
  local copies, waits for them, and re-layouts  4.53 us (3%)
    all_to_all x1, blocking collectives, tap_sum(): lax.all_to_all(spread, 'cols', 0, 0, tiled=True).reshape(cols, -1, 128)  29 us
    pallas_call x1, Pallas kernels, backward_call(): pl.pallas_call(backward_kernel, in_specs=[SM, ANY, ANY, ANY, VM, VM, VM,...  25.4 us
    all_to_all x1, blocking collectives, tap_sum(): lax.all_to_all(flat, 'rows', 0, 0, tiled=True).reshape(wide, -1, 128).sum(0)  18.9 us
    pallas_call x1, Pallas kernels, forward_call(): pl.pallas_call(forward_kernel, in_specs=[SM, ANY, ANY, ANY, VM, VM, VM, V...  18.1 us
    all_to_all x1, blocking collectives, tap_sum(): whole = lax.all_to_all(spread, 'rows', 0, 0, tiled=True)  12.4 us
    pallas_call x1, Pallas kernels, pack_x(): pl.pallas_call(pack_x_kernel, grid=(W // 128, 2), in_specs=[NATIVE, NATIV...  7.37 us
    pallas_call x1, Pallas kernels, turn_c(): pl.pallas_call(turn_c_kernel, grid=(W // 128, 2), in_specs=[NATIVE, pl.Bl...  6.4 us
    ppermute x1, starting transfers between devices, on_device(): cabove = lax.ppermute(cbot, 'rows', down)  4.58 us
  transfers between devices with their start and end apart: 8, of which 2 were waited for; matrix products, arithmetic and copies ran while one was open for 1% of the time, Pallas kernels for 16%

profile of v1, /device:TPU:0, one launch (start us, length us, event | category | flops | bytes accessed | tf_op | source)
XLA Modules:
  0.0 149.8 jit_solution(12647483523441115406)
XLA Ops:
  0.6 7.4 %pack_x.1 = (bf16[32,64,512]{2,1,0:T(8,128)(2,1)}, bf16[12,64,512]{2,1,0:T(8,128)(2,1)}, bf16[12,64,512]{2,1,0:T(8,128)(2,1)}, bf16[2,8,64,128]{3,2,1,0:T(8,128)(2,1)}, bf16[2,8,64,128]{3,2,1,0:T(8,128)(2,1)}) custom-call(bf16[64,32,512]{2,1,0:T(8,128)(2,1)} %x_ref.1, bf16[64,32,512]{2,1,0:T(8,128)(2,1)} %c_ref.3), custom_call_target="tpu_custom_call" | custom-call | tf_op jit(solution)/shard_map/pack_x/pallas_call | solution.py:96
  8.0 1.3 collective-permute-start.3
  9.3 3.0 %collective-permute-start.2 = (bf16[2,8,64,128]{3,2,1,0:T(8,128)(2,1)}, bf16[2,8,64,128]{3,2,1,0:T(8,128)(2,1)S(1)}, u32[]{:S(2)}, u32[]{:S(2)}) collective-permute-start(bf16[2,8,64,128]{3,2,1,0:T(8,128)(2,1)} %get-tuple-element.21), channel_id=1, source_target_pairs={{0,1},{1,2},{2,3},{4,5},{5,6},{6,7},{8,9},{9,10},{10,11},{12,13},{... | collective-permute-start | bytes 786440 | tf_op jit(solution)/shard_map/ppermute | solution.py:522
  12.4 4.0 %collective-permute-start = (bf16[12,64,512]{2,1,0:T(8,128)(2,1)}, bf16[12,64,512]{2,1,0:T(8,128)(2,1)S(1)}, u32[]{:S(2)}, u32[]{:S(2)}) collective-permute-start(bf16[12,64,512]{2,1,0:T(8,128)(2,1)} %get-tuple-element.19), channel_id=1, source_target_pairs={{0,4},{4,8},{8,12},{12,16},{16,20},{20,24},{24,28},{28,32},{32,36}... | collective-permute-start | bytes 2359304 | tf_op jit(solution)/shard_map/ppermute | solution.py:523
  16.3 1.3 collective-permute-start.1
  17.6 0.0 collective-permute-done.3.col_right
  17.6 0.0 copy-start.1
  17.7 0.0 collective-permute-done.2.col_left.after
  17.7 0.0 copy-start
  17.7 4.6 %collective-permute-start.4 = (bf16[2,2,3,64,128]{4,3,2,0,1:T(8,128)(2,1)S(1)}, bf16[2,2,3,64,128]{4,3,2,0,1:T(8,128)(2,1)S(1)}, u32[]{:S(2)}, u32[]{:S(2)}) collective-permute-start(bf16[2,2,3,64,128]{4,3,2,0,1:T(8,128)(2,1)S(1)} %pad_maximum_fusion), channel_id=1, source_target_pairs={{0,4},{4,8},{8,12},{12,16},{16,20},{20,24},{24,28},{28,32},{32,36}... | collective-permute-start | bytes 589832 | tf_op jit(solution)/shard_map/ppermute | solution.py:528
  22.3 1.3 collective-permute-start.5
  23.6 0.0 copy-done
  23.6 6.4 %turn_c.1 = (bf16[32,64,512]{2,1,0:T(8,128)(2,1)}, bf16[12,64,512]{2,1,0:T(8,128)(2,1)}, bf16[12,64,512]{2,1,0:T(8,128)(2,1)}) custom-call(bf16[64,32,512]{2,1,0:T(8,128)(2,1)} %c_ref.3, bf16[2,8,64,128]{3,2,1,0:T(8,128)(2,1)} %copy-done), custom_call_target="tpu_custom_call" | custom-call | tf_op jit(solution)/shard_map/turn_c/pallas_call | solution.py:108
  30.0 4.6 %collective-permute-start.6 = (bf16[12,64,512]{2,1,0:T(8,128)(2,1)}, bf16[12,64,512]{2,1,0:T(8,128)(2,1)S(1)}, u32[]{:S(2)}, u32[]{:S(2)}) collective-permute-start(bf16[12,64,512]{2,1,0:T(8,128)(2,1)} %get-tuple-element.25), channel_id=1, source_target_pairs={{0,4},{4,8},{8,12},{12,16},{16,20},{20,24},{24,28},{28,32},{32,36}... | collective-permute-start | bytes 2359304 | tf_op jit(solution)/shard_map/ppermute | solution.py:530
  34.6 2.1 %collective-permute-done.4 = bf16[2,2,3,64,128]{4,3,2,0,1:T(8,128)(2,1)S(1)} collective-permute-done((bf16[2,2,3,64,128]{4,3,2,0,1:T(8,128)(2,1)S(1)}, bf16[2,2,3,64,128]{4,3,2,0,1:T(8,128)(2,1)S(1)}, u32[]{:S(2)}, u32[]{:S(2)}) %collective-permute-start.4) | collective-permute-done | bytes 196640 | tf_op jit(solution)/shard_map/ppermute | solution.py:528
  36.7 1.3 collective-permute-start.7
  38.0 0.7 copy.19.cor_top
  38.7 0.0 copy-done.1
  38.7 2.6 %collective-permute-done.5.cor_bot = bf16[2,2,3,64,128]{4,3,2,1,0:T(8,128)(2,1)S(1)} collective-permute-done((bf16[2,2,3,64,128]{4,3,2,1,0:T(8,128)(2,1)S(1)}, bf16[2,2,3,64,128]{4,3,2,1,0:T(8,128)(2,1)S(1)}, u32[]{:S(2)}, u32[]{:S(2)}) %collective-permute-start.5) | collective-permute-done | bytes 196640 | tf_op jit(solution)/shard_map/ppermute | solution.py:527
  41.3 0.0 copy-start.6
  41.3 0.0 collective-permute-done.xtop
  41.3 0.0 copy-start.2
  41.3 0.0 collective-permute-done.1.xbot
  41.3 0.0 copy-start.3
  41.3 0.7 copy-done.6
  42.0 0.3 copy-done.2
  42.3 0.2 copy-done.3
  42.5 18.1 %forward.1 = (bf16[64,32,512]{2,1,0:T(8,128)(2,1)}, bf16[32,64,640]{2,1,0:T(8,128)(2,1)}, bf16[32,64,640]{2,1,0:T(8,128)(2,1)}, bf16[40,64,640]{2,1,0:T(8,128)(2,1)}) custom-call(s32[8,16]{1,0:T(8,128)} %tiles.3, bf16[32,64,512]{2,1,0:T(8,128)(2,1)} %get-tuple-element.18.x.x_in, bf16[12,64,512]{2,1,0:T(8,128)(2,1)} %copy-done.2, ...), custom_call_target="tpu_custom_call" | custom-call | flops 20000000000 | bytes 20000000 | tf_op jit(solution)/shard_map/forward/pallas_call | solution.py:344
  60.6 0.0 collective-permute-done.6.ctop
  60.6 0.0 copy-start.4
  60.6 0.0 collective-permute-done.7.cbot
  60.6 0.0 copy-start.5
  60.6 0.9 copy-done.4
  61.5 0.2 copy-done.5
  61.8 25.4 %backward.1 = (bf16[64,32,512]{2,1,0:T(8,128)(2,1)}, f32[4,192,64]{2,1,0:T(8,128)}) custom-call(s32[8,16]{1,0:T(8,128)} %tiles.3, bf16[32,64,512]{2,1,0:T(8,128)(2,1)} %get-tuple-element.24.c, bf16[12,64,512]{2,1,0:T(8,128)(2,1)} %copy-done.4, bf16[12,64,512]{2,1,0:T(8,128)(2,1)} %copy-done.5, bf16[2,8,64,128]{3,2,1,0:T(8,128)(2,1)} %copy-done, ...), custom_call_target="tpu_custom_call" | custom-call | flops 20000000000 | bytes 20000000 | tf_op jit(solution)/shard_map/backward/pallas_call | solution.py:471
  87.2 1.1 all_to_all.14
  88.3 18.9 %all_to_all.21 = f32[32,12,128]{2,1,0:T(8,128)S(1)} all-to-all(f32[32,12,128]{2,1,0:T(8,128)S(1)} %all_to_all.14), channel_id=1, replica_groups=mesh['rows'=32,'cols'=4] {'rows'}, dimensions={0} | all-to-all | bytes 393216 | tf_op jit(solution)/shard_map/all_to_all | solution.py:503
  107.2 29.0 %all_to_all.22 = f32[4,12,128]{2,1,0:T(8,128)S(1)} all-to-all(f32[4,12,128]{2,1,0:T(8,128)S(1)} %broadcast_in_dim.4), channel_id=1, replica_groups=mesh['rows'=32,'cols'=4] {'cols'}, dimensions={0} | all-to-all | bytes 49152 | tf_op jit(solution)/shard_map/all_to_all | solution.py:506
  136.3 12.4 %all_to_all.23 = f32[32,12,128]{2,1,0:T(8,128)S(1)} all-to-all(f32[32,12,128]{2,1,0:T(8,128)S(1)} %broadcast_in_dim.5), channel_id=1, replica_groups=mesh['rows'=32,'cols'=4] {'rows'}, dimensions={0} | all-to-all | bytes 393216 | tf_op jit(solution)/shard_map/all_to_all | solution.py:508
  148.7 0.1 slice.43
  148.8 0.1 slice.41
  148.9 0.1 slice.47
  148.9 0.1 slice.45
  149.0 0.8 pad_maximum_fusion.2
  (10 shorter events, 0.2 us)
Async XLA Ops:
  8.0 9.6 %collective-permute-start.3 = (bf16[2,8,64,128]{3,2,1,0:T(8,128)(2,1)}, bf16[2,8,64,128]{3,2,1,0:T(8,128)(2,1)S(1)}, u32[]{:S(2)}, u32[]{:S(2)}) collective-permute-start(bf16[2,8,64,128]{3,2,1,0:T(8,128)(2,1)} %get-tuple-element.22), channel_id=1, source_target_pairs={{1,0},{2,1},{3,2},{5,4},{6,5},{7,6},{9,8},{10,9},{11,10},{13,12},{... | collective-permute-start | bytes 786440 | tf_op jit(solution)/shard_map/ppermute | solution.py:521
  9.3 8.4 %collective-permute-start.2 = (bf16[2,8,64,128]{3,2,1,0:T(8,128)(2,1)}, bf16[2,8,64,128]{3,2,1,0:T(8,128)(2,1)S(1)}, u32[]{:S(2)}, u32[]{:S(2)}) collective-permute-start(bf16[2,8,64,128]{3,2,1,0:T(8,128)(2,1)} %get-tuple-element.21), channel_id=1, source_target_pairs={{0,1},{1,2},{2,3},{4,5},{5,6},{6,7},{8,9},{9,10},{10,11},{12,13},{... | collective-permute-start | bytes 786440 | tf_op jit(solution)/shard_map/ppermute | solution.py:522
  12.4 28.9 %collective-permute-start = (bf16[12,64,512]{2,1,0:T(8,128)(2,1)}, bf16[12,64,512]{2,1,0:T(8,128)(2,1)S(1)}, u32[]{:S(2)}, u32[]{:S(2)}) collective-permute-start(bf16[12,64,512]{2,1,0:T(8,128)(2,1)} %get-tuple-element.19), channel_id=1, source_target_pairs={{0,4},{4,8},{8,12},{12,16},{16,20},{20,24},{24,28},{28,32},{32,36}... | collective-permute-start | bytes 2359304 | tf_op jit(solution)/shard_map/ppermute | solution.py:523
  16.3 25.0 %collective-permute-start.1 = (bf16[12,64,512]{2,1,0:T(8,128)(2,1)}, bf16[12,64,512]{2,1,0:T(8,128)(2,1)S(1)}, u32[]{:S(2)}, u32[]{:S(2)}) collective-permute-start(bf16[12,64,512]{2,1,0:T(8,128)(2,1)} %get-tuple-element.20), channel_id=1, source_target_pairs={{4,0},{8,4},{12,8},{16,12},{20,16},{24,20},{28,24},{32,28},{36,32}... | collective-permute-start | bytes 2359304 | tf_op jit(solution)/shard_map/ppermute | solution.py:524
  17.6 21.1 %copy-start.1 = (bf16[2,8,64,128]{3,2,1,0:T(8,128)(2,1)}, bf16[2,8,64,128]{3,2,1,0:T(8,128)(2,1)S(1)}, u32[]{:S(2)}) copy-start(bf16[2,8,64,128]{3,2,1,0:T(8,128)(2,1)S(1)} %collective-permute-done.3.col_right) | copy-start | bytes 786436
  17.7 6.0 %copy-start = (bf16[2,8,64,128]{3,2,1,0:T(8,128)(2,1)}, bf16[2,8,64,128]{3,2,1,0:T(8,128)(2,1)S(1)}, u32[]{:S(2)}) copy-start(bf16[2,8,64,128]{3,2,1,0:T(8,128)(2,1)S(1)} %collective-permute-done.2.col_left.after) | copy-start | bytes 786436
  17.7 19.0 %collective-permute-start.4 = (bf16[2,2,3,64,128]{4,3,2,0,1:T(8,128)(2,1)S(1)}, bf16[2,2,3,64,128]{4,3,2,0,1:T(8,128)(2,1)S(1)}, u32[]{:S(2)}, u32[]{:S(2)}) collective-permute-start(bf16[2,2,3,64,128]{4,3,2,0,1:T(8,128)(2,1)S(1)} %pad_maximum_fusion), channel_id=1, source_target_pairs={{0,4},{4,8},{8,12},{12,16},{16,20},{20,24},{24,28},{28,32},{32,36}... | collective-permute-start | bytes 589832 | tf_op jit(solution)/shard_map/ppermute | solution.py:528
  22.3 19.0 %collective-permute-start.5 = (bf16[2,2,3,64,128]{4,3,2,1,0:T(8,128)(2,1)S(1)}, bf16[2,2,3,64,128]{4,3,2,1,0:T(8,128)(2,1)S(1)}, u32[]{:S(2)}, u32[]{:S(2)}) collective-permute-start(bf16[2,2,3,64,128]{4,3,2,1,0:T(8,128)(2,1)S(1)} %pad_maximum_fusion.1), channel_id=1, source_target_pairs={{4,0},{8,4},{12,8},{16,12},{20,16},{24,20},{28,24},{32,28},{36,32}... | collective-permute-start | bytes 589832 | tf_op jit(solution)/shard_map/ppermute | solution.py:527
  30.0 30.5 %collective-permute-start.6 = (bf16[12,64,512]{2,1,0:T(8,128)(2,1)}, bf16[12,64,512]{2,1,0:T(8,128)(2,1)S(1)}, u32[]{:S(2)}, u32[]{:S(2)}) collective-permute-start(bf16[12,64,512]{2,1,0:T(8,128)(2,1)} %get-tuple-element.25), channel_id=1, source_target_pairs={{0,4},{4,8},{8,12},{12,16},{16,20},{20,24},{24,28},{28,32},{32,36}... | collective-permute-start | bytes 2359304 | tf_op jit(solution)/shard_map/ppermute | solution.py:530
  36.7 23.9 %collective-permute-start.7 = (bf16[12,64,512]{2,1,0:T(8,128)(2,1)}, bf16[12,64,512]{2,1,0:T(8,128)(2,1)S(1)}, u32[]{:S(2)}, u32[]{:S(2)}) collective-permute-start(bf16[12,64,512]{2,1,0:T(8,128)(2,1)} %get-tuple-element.26), channel_id=1, source_target_pairs={{4,0},{8,4},{12,8},{16,12},{20,16},{24,20},{28,24},{32,28},{36,32}... | collective-permute-start | bytes 2359304 | tf_op jit(solution)/shard_map/ppermute | solution.py:531
  41.3 0.7 copy-start.6
  41.3 1.0 copy-start.2
  41.3 1.2 copy-start.3
  60.6 0.9 copy-start.4
  60.6 1.1 copy-start.5

commit v2 on v1

v2 whole, which is shorter than its diff:
```python
import functools
import math

import jax
import jax.numpy as jnp
from jax import lax
from jax.experimental import pallas as pl
from jax.experimental.pallas import tpu as pltpu
from jax.sharding import Mesh, PartitionSpec as P

FIRST_SPACING = 4
SECOND_SPACING = 8
TILE = 128
C = 64
R = 32
W = 512
E = 640
XHALO = 8
HALO = 12
XEDGE = 32
CEDGE = 16
XTILES = R * XEDGE // 128
CTILES = R * CEDGE // 128
F32 = jnp.float32
BF16 = jnp.bfloat16
VMEM_LIMIT = 60 * 1024 * 1024


def dot(a, b):
    return jnp.dot(a, b, preferred_element_type=F32)


def dot_nt(a, b):
    return lax.dot_general(a, b, (((1,), (1,)), ((), ())), preferred_element_type=F32)


def turn(block):
    return jnp.swapaxes(block, 0, 1)


def lanes(first, count, channels):
    lane = lax.broadcasted_iota(jnp.int32, (channels, 128), 1)
    return ((lane >= first) & (lane < first + count)).astype(F32).astype(BF16)


def rolled(v, shift):
    shift = shift % 128
    return pltpu.roll(v, shift, 1) if shift else v


def pack(rows, width, first):
    keep = lanes(first, width, rows[0].shape[0])
    parts = [rolled(v * keep, width * k - first) for k, v in enumerate(rows)]
    return functools.reduce(jnp.add, parts)


def unpack(left, right, k, width):
    channels = left.shape[0]
    ahead = rolled(right, -width * k) * lanes(0, width, channels)
    behind = rolled(left, 128 - width - width * k) * lanes(128 - width, width, channels)
    return ahead + behind


GC = 16


def edge_kernel(x_low, x_high, c_low, c_high, to_left, to_right):
    for src, width, at in ((x_low, XEDGE, 0), (c_low, CEDGE, XTILES)):
        for i in range(2):
            rows = turn(src[:, i * 16 : (i + 1) * 16, :])
            per = 128 // width
            for g in range(16 // per):
                tile = pack([rows[g * per + k] for k in range(per)], width, 0)
                to_left[at + (i * 16) // per + g] = tile
    for src, width, at in ((x_high, XEDGE, 0), (c_high, CEDGE, XTILES)):
        for i in range(2):
            rows = turn(src[:, i * 16 : (i + 1) * 16, :])
            per = 128 // width
            for g in range(16 // per):
                tile = pack([rows[g * per + k] for k in range(per)], width, 128 - width)
                to_right[at + (i * 16) // per + g] = tile


def pack_edges(x, c):
    low = pl.BlockSpec((GC, R, 128), lambda g: (g, 0, 0))
    high = pl.BlockSpec((GC, R, 128), lambda g: (g, 0, W // 128 - 1))
    out = pl.BlockSpec((XTILES + CTILES, GC, 128), lambda g: (0, g, 0))
    return pl.pallas_call(
        edge_kernel,
        grid=(C // GC,),
        in_specs=[low, high, low, high],
        out_specs=[out, out],
        out_shape=[jax.ShapeDtypeStruct((XTILES + CTILES, C, 128), BF16)] * 2,
        compiler_params=pltpu.CompilerParams(vmem_limit_bytes=VMEM_LIMIT),
        name="pack_edges",
    )(x, x, c, c)


def turn_block(src, dst):
    for i in range(R // 16):
        for t in range(W // 128):
            at = slice(t * 128, (t + 1) * 128)
            dst[i * 16 : (i + 1) * 16, :, at] = turn(src[:, i * 16 : (i + 1) * 16, at])


def turn_x_kernel(x_ref, xt, up, down):
    turn_block(x_ref, xt)
    up[0:XHALO] = xt[0:XHALO]
    down[0:XHALO] = xt[R - XHALO : R]


def turn_c_kernel(c_ref, left, right, ct, up, down):
    turn_block(c_ref, ct)
    up[0:HALO] = ct[0:HALO]
    down[0:HALO] = ct[R - HALO : R]
    for out, first in ((up, XTILES), (down, XTILES + CTILES - 2)):
        tiles = [left[first], left[first + 1], right[first], right[first + 1]]
        out[HALO] = jnp.concatenate(tiles, axis=1)


NATIVE = pl.BlockSpec((GC, R, W), lambda g: (g, 0, 0))
TURNED = pl.BlockSpec((R, GC, W), lambda g: (0, g, 0))


def message(rows):
    return (
        pl.BlockSpec((rows + 1, GC, W), lambda g: (0, g, 0)),
        jax.ShapeDtypeStruct((rows + 1, C, W), BF16),
    )


def turn_x(x):
    spec, shape = message(XHALO)
    return pl.pallas_call(
        turn_x_kernel,
        grid=(C // GC,),
        in_specs=[NATIVE],
        out_specs=[TURNED, spec, spec],
        out_shape=[jax.ShapeDtypeStruct((R, C, W), BF16), shape, shape],
        compiler_params=pltpu.CompilerParams(vmem_limit_bytes=VMEM_LIMIT),
        name="turn_x",
    )(x)


def turn_c(c, left, right):
    spec, shape = message(HALO)
    edges = pl.BlockSpec((XTILES + CTILES, GC, 128), lambda g: (0, g, 0))
    return pl.pallas_call(
        turn_c_kernel,
        grid=(C // GC,),
        in_specs=[NATIVE, edges, edges],
        out_specs=[TURNED, spec, spec],
        out_shape=[jax.ShapeDtypeStruct((R, C, W), BF16), shape, shape],
        compiler_params=pltpu.CompilerParams(vmem_limit_bytes=VMEM_LIMIT),
        name="turn_c",
    )(c, left, right)


def fill_kernel(up_in, down_in, left, right, up, down, rows, sems):
    copies = []
    for q, (out, first) in enumerate(((up, 0), (down, XTILES - 2))):
        tiles = [left[first], left[first + 1], right[first], right[first + 1]]
        rows[q] = jnp.concatenate(tiles, axis=1)
        copies.append(pltpu.make_async_copy(rows.at[q], out.at[XHALO], sems.at[q]))
        copies[-1].start()
    for copy in copies:
        copy.wait()


def fill_x(up, down, left, right):
    shape = jax.ShapeDtypeStruct(up.shape, BF16)
    return pl.pallas_call(
        fill_kernel,
        in_specs=[ANY, ANY, VM, VM],
        out_specs=[ANY, ANY],
        out_shape=[shape, shape],
        input_output_aliases={0: 0, 1: 1},
        scratch_shapes=[pltpu.VMEM((2, C, W), BF16), pltpu.SemaphoreType.DMA((2,))],
        name="fill_x",
    )(up, down, left, right)


ANY = pl.BlockSpec(memory_space=pl.ANY)
VM = pl.BlockSpec(memory_space=pltpu.VMEM)
SM = pl.BlockSpec(memory_space=pltpu.SMEM)
STEP = 8


def build_mask(tiles, mask):
    row_dev, col_dev = lax.axis_index("rows"), lax.axis_index("cols")
    n_rows, n_cols = tiles.shape
    first_row, first_tile = row_dev * R, col_dev * (W // TILE)
    lane = lax.broadcasted_iota(jnp.int32, (16, 128), 1)

    def value(p, ct):
        cell = first_row + (-1, 0, R)[p]
        inside = (cell >= 0) & (cell < n_rows * TILE) & (ct >= 0) & (ct < n_cols)
        rt = jnp.clip(cell, 0, n_rows * TILE - 1) // TILE
        return jnp.where(inside, tiles[rt, jnp.clip(ct, 0, n_cols - 1)], 0)

    for p in range(3):
        for t in range(W // 128):
            cell = jnp.full((16, 128), value(p, first_tile + t), jnp.int32)
            mask[p, :, t * 128 : (t + 1) * 128] = cell.astype(F32).astype(BF16)
        right = jnp.full((16, 128), value(p, first_tile + W // TILE), jnp.int32)
        left = jnp.full((16, 128), value(p, first_tile - 1), jnp.int32)
        mask[p, :, W:E] = jnp.where(lane < 64, right, left).astype(F32).astype(BF16)


def masked(v, mask, r, at):
    if isinstance(r, int):
        p = int(r >= 0) + int(r >= R)
    else:
        p = (r >= 0).astype(jnp.int32) + (r >= R).astype(jnp.int32)
    m = mask[p, :, at]
    return v * jnp.concatenate([m] * (C // 16), axis=0)


def shifted(v, d):
    return pltpu.roll(v, (-d) % v.shape[1], 1)


def row_stack(v, d, reverse):
    ahead, behind = shifted(v, d), shifted(v, -d)
    parts = [ahead, v, behind] if reverse else [behind, v, ahead]
    return jnp.concatenate(parts, axis=0)


def col_stack(ref, r, d, at):
    return jnp.concatenate([ref[r + d, :, at], ref[r, :, at], ref[r - d, :, at]], axis=0)


def forward_matrix(w):
    return jnp.concatenate([w[j].astype(F32).T for j in range(3)], axis=0).T.astype(BF16)


def backward_matrix(w, order=(0, 1, 2)):
    return jnp.concatenate([w[j].astype(F32) for j in order], axis=0).T.astype(BF16)


def two_rows(matrix):
    none = jnp.zeros((C, C), BF16)
    return jnp.concatenate(
        [jnp.concatenate([matrix, none], axis=1), jnp.concatenate([none, matrix], axis=1)], axis=0
    )


MAIN = (slice(0, 256), slice(256, 512))
TAIL = slice(W, E)


def loop(count, step, body):
    def one(i, _):
        body(i * step)
        return 0

    lax.fori_loop(0, count // step, one, 0)


def conv_columns(ref, rows, d, matrix, post, tail=True):
    def window(r, at):
        return jnp.concatenate([ref[r + k * d, :, at] for k in (-1, 0, 1, 2)], axis=0)

    for r in rows:
        for at in MAIN:
            both = dot(matrix, window(r, at))
            post(r, at, both[:C])
            post(r + d, at, both[C:])
    if tail:
        for r, s in zip(rows[::2], rows[1::2]):
            both = dot(matrix, jnp.concatenate([window(r, TAIL), window(s, TAIL)], axis=1))
            for row, half in ((r, both[:, :128]), (s, both[:, 128:])):
                post(row, TAIL, half[:C])
                post(row + d, TAIL, half[C:])


def conv_columns_single(ref, rows, d, matrix, post):
    def window(r, at):
        return jnp.concatenate([ref[r + k * d, :, at] for k in (-1, 0, 1)], axis=0)

    for r in rows:
        for at in MAIN:
            post(r, at, dot(matrix, window(r, at)))
    for r, s in zip(rows[::2], rows[1::2]):
        both = dot(matrix, jnp.concatenate([window(r, TAIL), window(s, TAIL)], axis=1))
        post(r, TAIL, both[:, :128])
        post(s, TAIL, both[:, 128:])


def conv_rows(ref, rows, d, reverse, matrix, post, tail=True):
    stacks = []
    for r in rows:
        stack = row_stack(ref[r], d, reverse)
        stacks.append(stack)
        for at in MAIN:
            post(r, at, dot(matrix, stack[:, at]))
    if tail:
        for q in range(0, len(rows), 2):
            both = dot(matrix, jnp.concatenate([stacks[q][:, TAIL], stacks[q + 1][:, TAIL]], axis=1))
            post(rows[q], TAIL, both[:, :128])
            post(rows[q + 1], TAIL, both[:, 128:])
    return stacks


def elu(p):
    return jnp.where(p > 0, p, jnp.exp(p) - 1.0)


def turn_out(src, out):
    for i in range(R // 16):
        for t in range(W // 128):
            at = slice(t * 128, (t + 1) * 128)
            out[:, i * 16 : (i + 1) * 16, at] = turn(src[i * 16 : (i + 1) * 16, :, at])


def call(kernel, name, in_specs, outs, scratch, cost, *args):
    return pl.pallas_call(
        kernel,
        in_specs=in_specs,
        out_specs=[spec for spec, _, _ in outs],
        out_shape=[jax.ShapeDtypeStruct(shape, dtype) for _, shape, dtype in outs],
        scratch_shapes=scratch,
        compiler_params=pltpu.CompilerParams(vmem_limit_bytes=VMEM_LIMIT),
        cost_estimate=pl.CostEstimate(flops=cost * 500_000_000, bytes_accessed=cost * 1_000_000, transcendentals=0),
        name=name,
    )(*args)


INNER = R - 2 * FIRST_SPACING


def inner_kernel(
    tiles, x, left, right, wr, wc,
    x_out, h1_out, b1_out, h2_out, up_out, down_out,
    xe, h1, b1, h2, mask, sems,
):
    d1, d2 = FIRST_SPACING, SECOND_SPACING
    load = pltpu.make_async_copy(x, xe.at[:, :, 0:W], sems.at[0])
    load.start()
    build_mask(tiles, mask)
    per = 128 // XEDGE

    def edges(g, _):
        for k in range(per):
            xe[g * per + k, :, TAIL] = unpack(left[g], right[g], k, XEDGE)
        return 0

    lax.fori_loop(0, XTILES, edges, 0)
    wr1, wr2 = forward_matrix(wr[0]), forward_matrix(wr[1])
    wc1 = two_rows(forward_matrix(wc[0]))
    load.wait()
    saves = [
        pltpu.make_async_copy(xe.at[0 : 2 * d1], x_out.at[0], sems.at[1]),
        pltpu.make_async_copy(xe.at[R - 2 * d1 : R], x_out.at[1], sems.at[2]),
    ]
    for save in saves:
        save.start()

    def hidden_one(r):
        def post(row, at, pre):
            h1[row, :, at] = masked(elu(pre).astype(BF16), mask, row, at)

        conv_rows(xe, [r + q for q in range(STEP)], d1, False, wr1, post)

    loop(R, STEP, hidden_one)
    saves.append(pltpu.make_async_copy(h1, h1_out, sems.at[3]))
    saves[-1].start()

    def block_one(r):
        def post(row, at, col):
            b1[row - d1, :, at] = xe[row, :, at] + masked(col.astype(BF16), mask, row, at)

        conv_columns(h1, [r + d1 + q for q in range(d1)], d1, wc1, post)

    loop(INNER, 2 * d1, block_one)
    saves.append(pltpu.make_async_copy(b1, b1_out, sems.at[4]))
    saves[-1].start()

    def hidden_two(r):
        def post(row, at, pre):
            h2[row, :, at] = masked(elu(pre).astype(BF16), mask, row + d1, at)

        conv_rows(b1, [r + q for q in range(STEP)], d2, False, wr2, post)

    loop(INNER, STEP, hidden_two)
    saves.append(pltpu.make_async_copy(h2, h2_out, sems.at[5]))
    saves.append(pltpu.make_async_copy(h2.at[0 : d2 - d1, :, 0:W], up_out, sems.at[6]))
    saves.append(pltpu.make_async_copy(h2.at[INNER - (d2 - d1) : INNER, :, 0:W], down_out, sems.at[7]))
    for save in saves[-3:]:
        save.start()
    for save in saves:
        save.wait()


def forward_inner(*args):
    d1, d2 = FIRST_SPACING, SECOND_SPACING
    return call(
        inner_kernel, "forward_inner", [SM, ANY, VM, VM, VM, VM],
        [
            (ANY, (2, 2 * d1, C, E), BF16),
            (ANY, (R, C, E), BF16),
            (ANY, (INNER, C, E), BF16),
            (ANY, (INNER, C, E), BF16),
            (ANY, (d2 - d1, C, W), BF16),
            (ANY, (d2 - d1, C, W), BF16),
        ],
        [
            pltpu.VMEM((R, C, E), BF16),
            pltpu.VMEM((R, C, E), BF16),
            pltpu.VMEM((INNER, C, E), BF16),
            pltpu.VMEM((INNER, C, E), BF16),
            pltpu.VMEM((3, 16, E), BF16),
            pltpu.SemaphoreType.DMA((8,)),
        ],
        10, *args,
    )


def outer_kernel(
    tiles, above, below, x_in, h1_in, wr, wc,
    b1_out, h2_out,
    x, h1, b1, h2, mask, sems,
):
    d1, d2 = FIRST_SPACING, SECOND_SPACING
    n = 2 * d1
    loads = [
        pltpu.make_async_copy(above.at[0:XHALO], x.at[0, 0:n, :, 0:W], sems.at[0]),
        pltpu.make_async_copy(below.at[0:XHALO], x.at[1, n : 2 * n, :, 0:W], sems.at[1]),
        pltpu.make_async_copy(x_in.at[0], x.at[0, n : 2 * n], sems.at[2]),
        pltpu.make_async_copy(x_in.at[1], x.at[1, 0:n], sems.at[3]),
        pltpu.make_async_copy(h1_in.at[0:n], h1.at[0, n : 2 * n], sems.at[4]),
        pltpu.make_async_copy(h1_in.at[R - n : R], h1.at[1, 0:n], sems.at[5]),
    ]
    edge_rows = pltpu.VMEM((2, C, W), BF16)
    for load in loads:
        load.start()
    build_mask(tiles, mask)

    def with_edges(packed, sem):
        gets = [
            pltpu.make_async_copy(above.at[XHALO], packed.at[0], sem.at[0]),
            pltpu.make_async_copy(below.at[XHALO], packed.at[1], sem.at[1]),
        ]
        for get in gets:
            get.start()
        for get in gets:
            get.wait()
        per = 128 // XEDGE
        for side in range(2):
            tile = [packed[side, :, t * 128 : (t + 1) * 128] for t in range(4)]
            for q in range(XHALO):
                x[side, side * n + q, :, TAIL] = unpack(tile[q // per], tile[2 + q // per], q % per, XEDGE)

    pl.run_scoped(with_edges, edge_rows, pltpu.SemaphoreType.DMA((2,)))
    wr1, wr2 = forward_matrix(wr[0]), forward_matrix(wr[1])
    wc1 = two_rows(forward_matrix(wc[0]))
    for load in loads:
        load.wait()

    def side_step(side, _):
        first = side * R - n

        def post_h1(row, at, pre):
            h1[side, row, :, at] = masked(elu(pre).astype(BF16), mask, row + first, at)

        conv_rows(x.at[side], [side * n + q for q in range(n)], d1, False, wr1, post_h1)
        return 0

    def side_next(side, _):
        first = side * R - n

        def post_b1(row, at, col):
            kept = masked(col.astype(BF16), mask, row + first, at)
            b1[side, row - d1, :, at] = x[side, row, :, at] + kept

        conv_columns(h1.at[side], [d1 + q for q in range(d1)], d1, wc1, post_b1)
        return 0

    def side_last(side, _):
        first = side * R - d1

        def post_h2(row, at, pre):
            h2[side, row, :, at] = masked(elu(pre).astype(BF16), mask, row + first, at)

        conv_rows(b1.at[side], [q for q in range(n)], d2, False, wr2, post_h2)
        return 0

    lax.fori_loop(0, 2, side_step, 0)
    lax.fori_loop(0, 2, side_next, 0)
    lax.fori_loop(0, 2, side_last, 0)
    saves = [pltpu.make_async_copy(b1, b1_out, sems.at[6]), pltpu.make_async_copy(h2, h2_out, sems.at[7])]
    for save in saves:
        save.start()
    for save in saves:
        save.wait()


def forward_outer(*args):
    n = 2 * FIRST_SPACING
    return call(
        outer_kernel, "forward_outer", [SM, ANY, ANY, ANY, ANY, VM, VM],
        [(ANY, (2, n, C, E), BF16), (ANY, (2, n, C, E), BF16)],
        [
            pltpu.VMEM((2, 2 * n, C, E), BF16),
            pltpu.VMEM((2, 2 * n, C, E), BF16),
            pltpu.VMEM((2, n, C, E), BF16),
            pltpu.VMEM((2, n, C, E), BF16),
            pltpu.VMEM((3, 16, E), BF16),
            pltpu.SemaphoreType.DMA((8,)),
        ],
        7, *args,
    )


def final_kernel(
    tiles, above, below, b1_in, b1_side, h2_in, h2_side, wc,
    out,
    b1, h2, flat, mask, sems,
):
    d1, d2 = FIRST_SPACING, SECOND_SPACING
    n, far, own = 2 * d1, d2 - d1, slice(0, W)
    loads = [
        pltpu.make_async_copy(above, h2.at[0:far], sems.at[0]),
        pltpu.make_async_copy(h2_side.at[0, :, :, own], h2.at[far : far + n], sems.at[1]),
        pltpu.make_async_copy(h2_in.at[:, :, own], h2.at[far + n : far + n + INNER], sems.at[2]),
        pltpu.make_async_copy(h2_side.at[1, :, :, own], h2.at[far + n + INNER : R + 2 * d2 - far], sems.at[3]),
        pltpu.make_async_copy(below, h2.at[R + 2 * d2 - far : R + 2 * d2], sems.at[4]),
        pltpu.make_async_copy(b1_side.at[0, d1:n, :, own], b1.at[0:d1], sems.at[5]),
        pltpu.make_async_copy(b1_in.at[:, :, own], b1.at[d1 : R - d1], sems.at[6]),
        pltpu.make_async_copy(b1_side.at[1, 0:d1, :, own], b1.at[R - d1 : R], sems.at[7]),
    ]
    for load in loads:
        load.start()
    build_mask(tiles, mask)
    wc2 = two_rows(forward_matrix(wc[1]))
    for load in loads:
        load.wait()

    def last(i):
        r = (i // d2) * 2 * d2 + i % d2

        def post(row, at, col):
            flat[row - d2, :, at] = b1[row - d2, :, at] + masked(col.astype(BF16), mask, row - d2, at)

        conv_columns(h2, [r + d2 + q for q in range(4)], d2, wc2, post, tail=False)

    loop(R // 2, 4, last)
    turn_out(flat, out)


def forward_final(*args):
    return call(
        final_kernel, "forward_final", [SM, ANY, ANY, ANY, ANY, ANY, ANY, VM],
        [(VM, (C, R, W), BF16)],
        [
            pltpu.VMEM((R, C, W), BF16),
            pltpu.VMEM((R + 2 * SECOND_SPACING, C, W), BF16),
            pltpu.VMEM((R, C, W), BF16),
            pltpu.VMEM((3, 16, E), BF16),
            pltpu.SemaphoreType.DMA((8,)),
        ],
        4, *args,
    )[0]


def backward_kernel(
    tiles, c, above, below, left, right, wr, wc, x_in, h1_in, b1_in, b1_side, h2_in, h2_side,
    out, taps,
    packed, ce, cm, h1, b1, h2, x, a2, cg1, g1, a1, flat, mask, sems,
):
    d1, d2 = FIRST_SPACING, SECOND_SPACING
    n = 2 * d1
    loads = [
        pltpu.make_async_copy(c, ce.at[HALO : HALO + R, :, 0:W], sems.at[0]),
        pltpu.make_async_copy(above.at[0:HALO], ce.at[0:HALO, :, 0:W], sems.at[1]),
        pltpu.make_async_copy(below.at[0:HALO], ce.at[HALO + R :, :, 0:W], sems.at[2]),
        pltpu.make_async_copy(above.at[HALO], packed.at[0], sems.at[7]),
        pltpu.make_async_copy(below.at[HALO], packed.at[1], sems.at[8]),
    ]
    late = [
        pltpu.make_async_copy(h2_side.at[0], h2.at[0:n], sems.at[3]),
        pltpu.make_async_copy(h2_in, h2.at[n : n + INNER], sems.at[9]),
        pltpu.make_async_copy(h2_side.at[1], h2.at[n + INNER : R + n], sems.at[10]),
        pltpu.make_async_copy(b1_side.at[0, d1:n], b1.at[0:d1], sems.at[4]),
        pltpu.make_async_copy(b1_in, b1.at[d1 : R - d1], sems.at[11]),
        pltpu.make_async_copy(b1_side.at[1, 0:d1], b1.at[R - d1 : R], sems.at[12]),
        pltpu.make_async_copy(h1_in, h1, sems.at[5]),
        pltpu.make_async_copy(x_in, x, sems.at[6]),
    ]
    for load in loads + late:
        load.start()
    build_mask(tiles, mask)
    per = 128 // CEDGE

    def edges(g, _):
        for k in range(per):
            ce[HALO + g * per + k, :, TAIL] = unpack(left[XTILES + g], right[XTILES + g], k, CEDGE)
        return 0

    lax.fori_loop(0, CTILES, edges, 0)
    wr1, wr2 = backward_matrix(wr[0]), backward_matrix(wr[1])
    wc1, wc2 = backward_matrix(wc[0], (2, 1, 0)), backward_matrix(wc[1], (2, 1, 0))
    wc1w, wc2w = two_rows(wc1), two_rows(wc2)
    taps[...] = jnp.zeros_like(taps)
    for load in loads:
        load.wait()
    for side, first, skip in ((0, 0, 2 * per - HALO), (1, HALO + R, 0)):
        tile = [packed[side, :, t * 128 : (t + 1) * 128] for t in range(4)]
        for q in range(HALO):
            g, k = divmod(q + skip, per)
            ce[first + q, :, TAIL] = unpack(tile[g], tile[2 + g], k, CEDGE)

    def mask_cot(r):
        for q in range(4):
            cm[r + q] = masked(ce[r + q], mask, r + q - HALO, slice(0, E))

    loop(R + 2 * HALO, 4, mask_cot)
    for load in late[0:3]:
        load.wait()

    up = HALO - d1

    def post_two(row, at, hid):
        slope = 1.0 + jnp.minimum(h2[row - up, :, at], 0).astype(F32)
        a2[row - up, :, at] = masked((hid * slope).astype(BF16), mask, row - HALO, at)

    def act_two(i):
        r = (i // d2) * 2 * d2 + i % d2
        conv_columns(cm, [r + up + q for q in range(4)], d2, wc2w, post_two)

    loop(R // 2, 4, act_two)
    conv_columns_single(cm, [R + up + q for q in range(2 * d1)], d2, wc2, post_two)
    for load in late[3:6]:
        load.wait()

    def add_taps(k, left, right):
        taps[k] += dot_nt(jnp.concatenate(left, axis=1), jnp.concatenate(right, axis=1))

    own = slice(0, W)

    def col_taps_two(r):
        rows = [r + q for q in range(4)]
        add_taps(0, [col_stack(cm, s + HALO, d2, own) for s in rows], [h2[s + d1, :, own] for s in rows])

    loop(R, 4, col_taps_two)

    def post_one(row, at, mixed):
        g = ce[row + up, :, at].astype(F32) + mixed
        cg1[row, :, at] = masked(g.astype(BF16), mask, row - d1, at)
        if at != TAIL:
            g1[row, :, at] = g

    def grad_one(r):
        rows = [r + q + d1 for q in range(4)]
        stacks = conv_rows(a2, rows, d2, True, wr2, post_one)
        add_taps(1, [s[:, own] for s in stacks], [b1[s - d1, :, own] for s in rows])

    for first in (0, R + d1):
        conv_rows(a2, [first + q for q in range(d1)], d2, True, wr2, post_one)
    loop(R, 4, grad_one)
    for load in late[6:8]:
        load.wait()

    def act_one(r):
        def post(row, at, hid):
            slope = 1.0 + jnp.minimum(h1[row - d1, :, at], 0).astype(F32)
            a1[row - d1, :, at] = masked((hid * slope).astype(BF16), mask, row - d1, at)

        rows = [r + q for q in range(2 * d1)]
        conv_columns(cg1, [s + d1 for s in rows[:d1]], d1, wc1w, post)
        add_taps(2, [col_stack(cg1, s + d1, d1, own) for s in rows], [h1[s, :, own] for s in rows])

    loop(R, 2 * d1, act_one)

    def last(r):
        def post(row, at, mixed):
            flat[row, :, at] = (g1[row + d1, :, at] + mixed).astype(BF16)

        rows = [r + q for q in range(4)]
        stacks = conv_rows(a1, rows, d1, True, wr1, post, tail=False)
        add_taps(3, [s[:, own] for s in stacks], [x[s] for s in rows])

    loop(R, 4, last)
    turn_out(flat, out)


def backward(*args):
    n = 2 * FIRST_SPACING
    return call(
        backward_kernel, "backward", [SM, ANY, ANY, ANY, VM, VM, VM, VM] + [ANY] * 6,
        [(VM, (C, R, W), BF16), (VM, (4, 3 * C, C), F32)],
        [
            pltpu.VMEM((2, C, W), BF16),
            pltpu.VMEM((R + 2 * HALO, C, E), BF16),
            pltpu.VMEM((R + 2 * HALO, C, E), BF16),
            pltpu.VMEM((R, C, E), BF16),
            pltpu.VMEM((R, C, E), BF16),
            pltpu.VMEM((R + n, C, E), BF16),
            pltpu.VMEM((R, C, W), BF16),
            pltpu.VMEM((R + n, C, E), BF16),
            pltpu.VMEM((R + n, C, E), BF16),
            pltpu.VMEM((R + n, C, W), F32),
            pltpu.VMEM((R, C, E), BF16),
            pltpu.VMEM((R, C, W), BF16),
            pltpu.VMEM((3, 16, E), BF16),
            pltpu.SemaphoreType.DMA((13,)),
        ],
        25, *args,
    )


def tap_sum(taps):
    flat = taps.reshape(-1, 128)
    wide = lax.axis_size("rows")
    part = lax.all_to_all(flat, "rows", 0, 0, tiled=True).reshape(wide, -1, 128).sum(0)
    cols = lax.axis_size("cols")
    spread = jnp.broadcast_to(part[None], (cols,) + part.shape).reshape(-1, 128)
    part = lax.all_to_all(spread, "cols", 0, 0, tiled=True).reshape(cols, -1, 128).sum(0)
    spread = jnp.broadcast_to(part[None], (wide,) + part.shape).reshape(-1, 128)
    whole = lax.all_to_all(spread, "rows", 0, 0, tiled=True)
    return whole.reshape(4, 3, C, C)


def on_device(x, tile_mask, wr, wc, cot):
    n_rows, n_cols = lax.axis_size("rows"), lax.axis_size("cols")
    factor = 1.0 / math.sqrt(R * n_rows * W * n_cols)
    down = [(i, i + 1) for i in range(n_rows - 1)]
    up = [(i + 1, i) for i in range(n_rows - 1)]
    right = [(i, i + 1) for i in range(n_cols - 1)]
    left = [(i + 1, i) for i in range(n_cols - 1)]

    to_left, to_right = pack_edges(x, cot)
    from_right = lax.ppermute(to_left, "cols", left)
    from_left = lax.ppermute(to_right, "cols", right)
    xt, x_up, x_down = turn_x(x)
    x_up, x_down = fill_x(x_up, x_down, from_left, from_right)
    x_above = lax.ppermute(x_down, "rows", down)
    x_below = lax.ppermute(x_up, "rows", up)
    ct, c_up, c_down = turn_c(cot, from_left, from_right)
    c_above = lax.ppermute(c_down, "rows", down)
    c_below = lax.ppermute(c_up, "rows", up)

    x_side, h1, b1, h2, h2_up, h2_down = forward_inner(tile_mask, xt, from_left, from_right, wr, wc)
    h2_above = lax.ppermute(h2_down, "rows", down)
    h2_below = lax.ppermute(h2_up, "rows", up)
    b1_side, h2_side = forward_outer(tile_mask, x_above, x_below, x_side, h1, wr, wc)
    map_grad, taps = backward(
        tile_mask, ct, c_above, c_below, from_left, from_right, wr, wc, xt, h1, b1, b1_side, h2, h2_side
    )
    final = forward_final(tile_mask, h2_above, h2_below, b1, b1_side, h2, h2_side, wc)
    total = tap_sum(taps) * factor
    row_grad = jnp.stack([total[3], total[1]])
    col_grad = jnp.stack([total[2], total[0]])
    return final, map_grad, row_grad, col_grad


def solution(mesh):
    placed = (P(None, "rows", "cols"), P(), P(), P(), P(None, "rows", "cols"))
    return jax.shard_map(
        on_device,
        mesh=mesh,
        in_specs=placed,
        out_specs=(P(None, "rows", "cols"), P(None, "rows", "cols"), P(), P()),
        check_vma=False,
    )
```

time: 151 us -> 137 us (0.907)
  blocking collectives: 60.3 us -> 36.3 us
  Pallas kernels: 57.2 us -> 65.6 us
  starting transfers between devices: 21.3 us -> 23.3 us
  waiting for transfers between devices: 4.7 us -> 2.75 us
  local copies, waits for them, and re-layouts: 4.53 us -> 6.26 us
    all_to_all x1, blocking collectives: 29 us -> 12.8 us  [tap_sum(): lax.all_to_all(spread, 'cols', 0, 0, tiled=True).reshape(cols, -1, 128)]
    all_to_all x1 -> x0, blocking collectives: 12.4 us -> none  [tap_sum(): whole = lax.all_to_all(spread, 'rows', 0, 0, tiled=True)]
    pallas_call x4 -> x8, Pallas kernels: 57.2 us -> 65.6 us  [the longest x4 51 us: call(): pl.pallas_call(kernel, in_specs=in_specs, out_specs=[spec for spec, _, _...]
    all_to_all x1, blocking collectives: 18.9 us -> 23.5 us  [tap_sum(): lax.all_to_all(flat, 'rows', 0, 0, tiled=True).reshape(wide, -1, 128).sum(0)]
    all_to_all x0 -> x1, starting transfers between devices: none -> 3.87 us  [tap_sum(): whole = lax.all_to_all(spread, 'rows', 0, 0, tiled=True)]
    ppermute x8, waiting for transfers between devices: 4.7 us -> 1.45 us  [the longest x1 1.43 us: on_device(): from_right = lax.ppermute(to_left, 'cols', left)]
    ppermute x8, starting transfers between devices: 21.3 us -> 19.5 us  [the longest x1 4.59 us: on_device(): c_above = lax.ppermute(c_down, 'rows', down)]
    unnamed x14 -> x16, local copies, waits for them, and re-layouts: 2.33 us -> 4.1 us
  transfers between devices with their start and end apart: 8 -> 9, of which waited for: 2 -> 2; matrix products, arithmetic and copies ran while one was open for 1% -> 1% of each run, Pallas kernels for 16% -> 44%
where the time goes in v2:
time: 137 us; the launch traced here: 136 us
  Pallas kernels  65.6 us (48%)
  blocking collectives  36.3 us (26%)
  starting transfers between devices  23.3 us (17%)
  local copies, waits for them, and re-layouts  6.26 us (5%)
  waiting for transfers between devices  2.75 us (2%)
    pallas_call x4, Pallas kernels, call(): pl.pallas_call(kernel, in_specs=in_specs, out_specs=[spec for spec, _, _...  51 us
    all_to_all x1, blocking collectives, tap_sum(): lax.all_to_all(flat, 'rows', 0, 0, tiled=True).reshape(wide, -1, 128).sum(0)  23.5 us
    all_to_all x1, blocking collectives, tap_sum(): lax.all_to_all(spread, 'cols', 0, 0, tiled=True).reshape(cols, -1, 128)  12.8 us
    ppermute x1, starting transfers between devices, on_device(): c_above = lax.ppermute(c_down, 'rows', down)  4.59 us
    ppermute x1, starting transfers between devices, on_device(): h2_above = lax.ppermute(h2_down, 'rows', down)  4.56 us
    pallas_call x1, Pallas kernels, turn_c(): pl.pallas_call(turn_c_kernel, grid=(C // GC,), in_specs=[NATIVE, edges, e...  4.51 us
    pallas_call x1, Pallas kernels, turn_x(): pl.pallas_call(turn_x_kernel, grid=(C // GC,), in_specs=[NATIVE], out_spe...  4.31 us
    unnamed x16, local copies, waits for them, and re-layouts  4.1 us
  transfers between devices with their start and end apart: 9, of which 2 were waited for; matrix products, arithmetic and copies ran while one was open for 1% of the time, Pallas kernels for 44%

profile of v2, /device:TPU:0, one launch (start us, length us, event | category | flops | bytes accessed | tf_op | source)
XLA Modules:
  0.0 135.9 jit_solution(9228118448442141429)
XLA Ops:
  0.6 4.1 %pack_edges.1 = (bf16[12,64,128]{2,1,0:T(8,128)(2,1)}, bf16[12,64,128]{2,1,0:T(8,128)(2,1)}) custom-call(bf16[64,32,512]{2,1,0:T(8,128)(2,1)} %x_high.1, bf16[64,32,512]{2,1,0:T(8,128)(2,1)} %x_high.1, bf16[64,32,512]{2,1,0:T(8,128)(2,1)} %c_ref.1, bf16[64,32,512]{2,1,0:T(8,128)(2,1)} %c_ref.1), custom_call_target="tpu_custom_call" | custom-call | tf_op jit(solution)/shard_map/pack_edges/pallas_call | solution.py:88
  4.7 1.3 collective-permute-start
  6.0 1.3 collective-permute-start.1
  7.3 4.3 %turn_x.1 = (bf16[32,64,512]{2,1,0:T(8,128)(2,1)}, bf16[9,64,512]{2,1,0:T(8,128)(2,1)}, bf16[9,64,512]{2,1,0:T(8,128)(2,1)}) custom-call(bf16[64,32,512]{2,1,0:T(8,128)(2,1)} %x_high.1), custom_call_target="tpu_custom_call" | custom-call | tf_op jit(solution)/shard_map/turn_x/pallas_call | solution.py:134
  11.6 0.0 collective-permute-done.left
  11.6 0.0 copy-start
  11.6 1.4 %collective-permute-done.1.right = bf16[12,64,128]{2,1,0:T(8,128)(2,1)S(1)} collective-permute-done((bf16[12,64,128]{2,1,0:T(8,128)(2,1)}, bf16[12,64,128]{2,1,0:T(8,128)(2,1)S(1)}, u32[]{:S(2)}, u32[]{:S(2)}) %collective-permute-start.1) | collective-permute-done | bytes 196640 | tf_op jit(solution)/shard_map/ppermute | solution.py:733
  13.1 0.0 copy-start.1
  13.1 0.0 copy-done
  13.1 0.7 copy-done.1
  13.7 1.7 %fill_x.1 = (bf16[9,64,512]{2,1,0:T(8,128)(2,1)}, bf16[9,64,512]{2,1,0:T(8,128)(2,1)}) custom-call(bf16[9,64,512]{2,1,0:T(8,128)(2,1)} %get-tuple-element.30.up_in, bf16[9,64,512]{2,1,0:T(8,128)(2,1)} %get-tuple-element.31.down_in, bf16[12,64,128]{2,1,0:T(8,128)(2,1)} %copy-done, ...), custom_call_target="tpu_custom_call", output_to_operand_aliasing={{0}: (0, {}), {1}: (1, {})} | custom-call | tf_op jit(solution)/shard_map/fill_x/pallas_call | solution.py:172
  15.4 3.9 %collective-permute-start.4 = (bf16[9,64,512]{2,1,0:T(8,128)(2,1)}, bf16[9,64,512]{2,1,0:T(8,128)(2,1)S(1)}, u32[]{:S(2)}, u32[]{:S(2)}) collective-permute-start(bf16[9,64,512]{2,1,0:T(8,128)(2,1)} %get-tuple-element.32), channel_id=1, source_target_pairs={{0,4},{4,8},{8,12},{12,16},{16,20},{20,24},{24,28},{28,32},{32,36}... | collective-permute-start | bytes 1769480 | tf_op jit(solution)/shard_map/ppermute | solution.py:737
  19.3 1.3 collective-permute-start.5
  20.6 4.5 %turn_c.1 = (bf16[32,64,512]{2,1,0:T(8,128)(2,1)}, bf16[13,64,512]{2,1,0:T(8,128)(2,1)}, bf16[13,64,512]{2,1,0:T(8,128)(2,1)}) custom-call(bf16[64,32,512]{2,1,0:T(8,128)(2,1)} %c_ref.1, bf16[12,64,128]{2,1,0:T(8,128)(2,1)} %copy-done, bf16[12,64,128]{2,1,0:T(8,128)(2,1)} %copy-done.1), custom_call_target="tpu_custom_call" | custom-call | tf_op jit(solution)/shard_map/turn_c/pallas_call | solution.py:148
  25.1 4.6 %collective-permute-start.6 = (bf16[13,64,512]{2,1,0:T(8,128)(2,1)}, bf16[13,64,512]{2,1,0:T(8,128)(2,1)S(1)}, u32[]{:S(2)}, u32[]{:S(2)}) collective-permute-start(bf16[13,64,512]{2,1,0:T(8,128)(2,1)} %get-tuple-element.40), channel_id=1, source_target_pairs={{0,4},{4,8},{8,12},{12,16},{16,20},{20,24},{24,28},{28,32},{32,36}... | collective-permute-start | bytes 2555912 | tf_op jit(solution)/shard_map/ppermute | solution.py:740
  29.7 1.3 collective-permute-start.7
  31.0 10.5 %forward_inner.1 = (bf16[2,8,64,640]{3,2,1,0:T(8,128)(2,1)}, bf16[32,64,640]{2,1,0:T(8,128)(2,1)}, bf16[24,64,640]{2,1,0:T(8,128)(2,1)}, bf16[24,64,640]{2,1,0:T...) custom-call(s32[8,16]{1,0:T(8,128)} %tiles.7, bf16[32,64,512]{2,1,0:T(8,128)(2,1)} %get-tuple-element.24.x.x_in, ...), custom_call_target="tpu_custom_call" | custom-call | flops 5000000000 | bytes 10000000 | tf_op jit(solution)/shard_map/forward_inner/pallas_call | solution.py:317
  41.5 4.6 %collective-permute-start.2 = (bf16[4,64,512]{2,1,0:T(8,128)(2,1)}, bf16[4,64,512]{2,1,0:T(8,128)(2,1)S(1)}, u32[]{:S(2)}, u32[]{:S(2)}) collective-permute-start(bf16[4,64,512]{2,1,0:T(8,128)(2,1)} %get-tuple-element.27), channel_id=1, source_target_pairs={{0,4},{4,8},{8,12},{12,16},{16,20},{20,24},{24,28},{28,32},{32,36}... | collective-permute-start | bytes 786440 | tf_op jit(solution)/shard_map/ppermute | solution.py:744
  46.0 0.0 collective-permute-done.4.above
  46.1 0.0 copy-start.6
  46.1 1.3 collective-permute-start.3
  47.4 0.0 collective-permute-done.5.below
  47.4 0.0 copy-start.7
  47.4 0.0 copy-done.6
  47.4 0.8 copy-done.7
  48.2 8.6 %forward_outer.1 = (bf16[2,8,64,640]{3,2,1,0:T(8,128)(2,1)}, bf16[2,8,64,640]{3,2,1,0:T(8,128)(2,1)}) custom-call(s32[8,16]{1,0:T(8,128)} %tiles.7, bf16[9,64,512]{2,1,0:T(8,128)(2,1)} %copy-done.6, bf16[9,64,512]{2,1,0:T(8,128)(2,1)} %copy-done.7, bf16[2,8,64,640]{3,2,1,0:T(8,128)(2,1)} %get-tuple-element.34.x_in, ...), custom_call_target="tpu_custom_call" | custom-call | flops 3500000000 | bytes 7000000 | tf_op jit(solution)/shard_map/forward_outer/pallas_call | solution.py:317
  56.8 0.0 collective-permute-done.6.above
  56.8 0.0 copy-start.4
  56.8 0.0 collective-permute-done.7.below
  56.9 0.0 copy-start.5
  56.9 0.9 copy-done.4
  57.8 0.3 copy-done.5
  58.1 25.2 %backward.1 = (bf16[64,32,512]{2,1,0:T(8,128)(2,1)}, f32[4,192,64]{2,1,0:T(8,128)}) custom-call(s32[8,16]{1,0:T(8,128)} %tiles.7, bf16[32,64,512]{2,1,0:T(8,128)(2,1)} %get-tuple-element.39.c, bf16[13,64,512]{2,1,0:T(8,128)(2,1)} %copy-done.4, bf16[13,64,512]{2,1,0:T(8,128)(2,1)} %copy-done.5, bf16[12,64,128]{2,1,0:T(8,128)(2,1)} %copy-done, ...), custom_call_target="tpu_custom_call" | custom-call | flops 12499999744 | bytes 25000000 | tf_op jit(solution)/shard_map/backward/pallas_call | solution.py:317
  83.3 1.1 all_to_all.14
  84.4 23.5 %all_to_all.21 = f32[32,12,128]{2,1,0:T(8,128)S(1)} all-to-all(f32[32,12,128]{2,1,0:T(8,128)S(1)} %all_to_all.14), channel_id=1, replica_groups=mesh['rows'=32,'cols'=4] {'rows'}, dimensions={0} | all-to-all | bytes 393216 | tf_op jit(solution)/shard_map/all_to_all | solution.py:715
  108.0 12.8 %all_to_all.22 = f32[4,12,128]{2,1,0:T(8,128)S(1)} all-to-all(f32[4,12,128]{2,1,0:T(8,128)S(1)} %broadcast_in_dim.4), channel_id=1, replica_groups=mesh['rows'=32,'cols'=4] {'cols'}, dimensions={0} | all-to-all | bytes 49152 | tf_op jit(solution)/shard_map/all_to_all | solution.py:718
  120.8 0.7 broadcast_in_dim.5
  121.5 3.9 %all-to-all-start.2 = ((f32[32,12,128]{2,1,0:T(8,128)}), f32[32,12,128]{2,1,0:T(8,128)S(1)}, u32[]{:S(2)}, u32[]{:S(2)}) async-start(f32[32,12,128]{2,1,0:T(8,128)} %broadcast_in_dim.5), calls=%async_computation.2 | async-start | bytes 524288 | tf_op jit(solution)/shard_map/all_to_all | solution.py:720
  125.4 0.0 collective-permute-done.2.above
  125.4 0.0 copy-start.2
  125.4 0.0 collective-permute-done.3.below
  125.4 0.7 copy-done.2
  126.1 0.0 copy-start.3
  126.1 0.7 copy-done.3
  126.8 6.7 %forward_final.1 = bf16[64,32,512]{2,1,0:T(8,128)(2,1)} custom-call(s32[8,16]{1,0:T(8,128)} %tiles.7, bf16[4,64,512]{2,1,0:T(8,128)(2,1)} %copy-done.2, bf16[4,64,512]{2,1,0:T(8,128)(2,1)} %copy-done.3, bf16[24,64,640]{2,1,0:T(8,128)(2,1)} %get-tuple-element.29.b1_in, bf16[2,8,64,640]{3,2,1,0:T(8,128)(2,1)} %get-tuple-element.36.b1_side, ...), custom_call_target="tpu_custom_call" | custom-call | flops 2000000000 | bytes 4000000 | tf_op jit(solution)/shard_map/forward_final/pallas_call | solution.py:317
  133.5 1.3 all-to-all-done.2
  134.8 0.1 slice.29
  134.9 0.1 slice.31
  135.0 0.1 slice.27
  135.1 0.1 slice.25
  135.2 0.8 pad_maximum_fusion
  (5 shorter events, 0.1 us)
Async XLA Ops:
  4.7 6.9 %collective-permute-start = (bf16[12,64,128]{2,1,0:T(8,128)(2,1)}, bf16[12,64,128]{2,1,0:T(8,128)(2,1)S(1)}, u32[]{:S(2)}, u32[]{:S(2)}) collective-permute-start(bf16[12,64,128]{2,1,0:T(8,128)(2,1)} %get-tuple-element.25), channel_id=1, source_target_pairs={{0,1},{1,2},{2,3},{4,5},{5,6},{6,7},{8,9},{9,10},{10,11},{12,13},{... | collective-permute-start | bytes 589832 | tf_op jit(solution)/shard_map/ppermute | solution.py:734
  6.0 7.0 %collective-permute-start.1 = (bf16[12,64,128]{2,1,0:T(8,128)(2,1)}, bf16[12,64,128]{2,1,0:T(8,128)(2,1)S(1)}, u32[]{:S(2)}, u32[]{:S(2)}) collective-permute-start(bf16[12,64,128]{2,1,0:T(8,128)(2,1)} %get-tuple-element.26), channel_id=1, source_target_pairs={{1,0},{2,1},{3,2},{5,4},{6,5},{7,6},{9,8},{10,9},{11,10},{13,12},{... | collective-permute-start | bytes 589832 | tf_op jit(solution)/shard_map/ppermute | solution.py:733
  11.6 1.4 %copy-start = (bf16[12,64,128]{2,1,0:T(8,128)(2,1)}, bf16[12,64,128]{2,1,0:T(8,128)(2,1)S(1)}, u32[]{:S(2)}) copy-start(bf16[12,64,128]{2,1,0:T(8,128)(2,1)S(1)} %collective-permute-done.left) | copy-start | bytes 589828
  13.1 0.7 copy-start.1
  15.4 30.6 %collective-permute-start.4 = (bf16[9,64,512]{2,1,0:T(8,128)(2,1)}, bf16[9,64,512]{2,1,0:T(8,128)(2,1)S(1)}, u32[]{:S(2)}, u32[]{:S(2)}) collective-permute-start(bf16[9,64,512]{2,1,0:T(8,128)(2,1)} %get-tuple-element.32), channel_id=1, source_target_pairs={{0,4},{4,8},{8,12},{12,16},{16,20},{20,24},{24,28},{28,32},{32,36}... | collective-permute-start | bytes 1769480 | tf_op jit(solution)/shard_map/ppermute | solution.py:737
  19.3 28.1 %collective-permute-start.5 = (bf16[9,64,512]{2,1,0:T(8,128)(2,1)}, bf16[9,64,512]{2,1,0:T(8,128)(2,1)S(1)}, u32[]{:S(2)}, u32[]{:S(2)}) collective-permute-start(bf16[9,64,512]{2,1,0:T(8,128)(2,1)} %get-tuple-element.33), channel_id=1, source_target_pairs={{4,0},{8,4},{12,8},{16,12},{20,16},{24,20},{28,24},{32,28},{36,32}... | collective-permute-start | bytes 1769480 | tf_op jit(solution)/shard_map/ppermute | solution.py:738
  25.1 31.7 %collective-permute-start.6 = (bf16[13,64,512]{2,1,0:T(8,128)(2,1)}, bf16[13,64,512]{2,1,0:T(8,128)(2,1)S(1)}, u32[]{:S(2)}, u32[]{:S(2)}) collective-permute-start(bf16[13,64,512]{2,1,0:T(8,128)(2,1)} %get-tuple-element.40), channel_id=1, source_target_pairs={{0,4},{4,8},{8,12},{12,16},{16,20},{20,24},{24,28},{28,32},{32,36}... | collective-permute-start | bytes 2555912 | tf_op jit(solution)/shard_map/ppermute | solution.py:740
  29.7 27.1 %collective-permute-start.7 = (bf16[13,64,512]{2,1,0:T(8,128)(2,1)}, bf16[13,64,512]{2,1,0:T(8,128)(2,1)S(1)}, u32[]{:S(2)}, u32[]{:S(2)}) collective-permute-start(bf16[13,64,512]{2,1,0:T(8,128)(2,1)} %get-tuple-element.41), channel_id=1, source_target_pairs={{4,0},{8,4},{12,8},{16,12},{20,16},{24,20},{28,24},{32,28},{36,32}... | collective-permute-start | bytes 2555912 | tf_op jit(solution)/shard_map/ppermute | solution.py:741
  41.5 83.9 %collective-permute-start.2 = (bf16[4,64,512]{2,1,0:T(8,128)(2,1)}, bf16[4,64,512]{2,1,0:T(8,128)(2,1)S(1)}, u32[]{:S(2)}, u32[]{:S(2)}) collective-permute-start(bf16[4,64,512]{2,1,0:T(8,128)(2,1)} %get-tuple-element.27), channel_id=1, source_target_pairs={{0,4},{4,8},{8,12},{12,16},{16,20},{20,24},{24,28},{28,32},{32,36}... | collective-permute-start | bytes 786440 | tf_op jit(solution)/shard_map/ppermute | solution.py:744
  46.1 1.3 copy-start.6
  46.1 79.3 %collective-permute-start.3 = (bf16[4,64,512]{2,1,0:T(8,128)(2,1)}, bf16[4,64,512]{2,1,0:T(8,128)(2,1)S(1)}, u32[]{:S(2)}, u32[]{:S(2)}) collective-permute-start(bf16[4,64,512]{2,1,0:T(8,128)(2,1)} %get-tuple-element.28), channel_id=1, source_target_pairs={{4,0},{8,4},{12,8},{16,12},{20,16},{24,20},{28,24},{32,28},{36,32}... | collective-permute-start | bytes 786440 | tf_op jit(solution)/shard_map/ppermute | solution.py:745
  47.4 0.8 copy-start.7
  56.8 0.9 copy-start.4
  56.9 1.2 copy-start.5
  121.5 13.3 %all-to-all-start.2 = ((f32[32,12,128]{2,1,0:T(8,128)}), f32[32,12,128]{2,1,0:T(8,128)S(1)}, u32[]{:S(2)}, u32[]{:S(2)}) async-start(f32[32,12,128]{2,1,0:T(8,128)} %broadcast_in_dim.5), calls=%async_computation.2 | async-start | bytes 524288 | tf_op jit(solution)/shard_map/all_to_all | solution.py:720
  125.4 0.7 copy-start.2
  126.1 0.7 copy-start.3

commit v3 on v2

--- a/solution.py
+++ b/solution.py
@@ -103,23 +103,11 @@
             dst[i * 16 : (i + 1) * 16, :, at] = turn(src[:, i * 16 : (i + 1) * 16, at])
 
 
-def turn_x_kernel(x_ref, xt, up, down):
-    turn_block(x_ref, xt)
-    up[0:XHALO] = xt[0:XHALO]
-    down[0:XHALO] = xt[R - XHALO : R]
-
-
-def turn_c_kernel(c_ref, left, right, ct, up, down):
-    turn_block(c_ref, ct)
-    up[0:HALO] = ct[0:HALO]
-    down[0:HALO] = ct[R - HALO : R]
-    for out, first in ((up, XTILES), (down, XTILES + CTILES - 2)):
-        tiles = [left[first], left[first + 1], right[first], right[first + 1]]
-        out[HALO] = jnp.concatenate(tiles, axis=1)
-
-
-NATIVE = pl.BlockSpec((GC, R, W), lambda g: (g, 0, 0))
-TURNED = pl.BlockSpec((R, GC, W), lambda g: (0, g, 0))
+def turn_kernel(x_ref, c_ref, xt, x_up, x_down, ct, c_up, c_down):
+    for src, dst, up, down, halo in ((x_ref, xt, x_up, x_down, XHALO), (c_ref, ct, c_up, c_down, HALO)):
+        turn_block(src, dst)
+        up[0:halo] = dst[0:halo]
+        down[0:halo] = dst[R - halo : R]
 
 
 def message(rows):
@@ -129,55 +117,48 @@
     )
 
 
-def turn_x(x):
-    spec, shape = message(XHALO)
+def turn_both(x, c):
+    native = pl.BlockSpec((GC, R, W), lambda g: (g, 0, 0))
+    turned = pl.BlockSpec((R, GC, W), lambda g: (0, g, 0))
+    block = jax.ShapeDtypeStruct((R, C, W), BF16)
+    (xs, x_shape), (cs, c_shape) = message(XHALO), message(HALO)
     return pl.pallas_call(
-        turn_x_kernel,
+        turn_kernel,
         grid=(C // GC,),
-        in_specs=[NATIVE],
-        out_specs=[TURNED, spec, spec],
-        out_shape=[jax.ShapeDtypeStruct((R, C, W), BF16), shape, shape],
+        in_specs=[native, native],
+        out_specs=[turned, xs, xs, turned, cs, cs],
+        out_shape=[block, x_shape, x_shape, block, c_shape, c_shape],
         compiler_params=pltpu.CompilerParams(vmem_limit_bytes=VMEM_LIMIT),
-        name="turn_x",
-    )(x)
-
-
-def turn_c(c, left, right):
-    spec, shape = message(HALO)
-    edges = pl.BlockSpec((XTILES + CTILES, GC, 128), lambda g: (0, g, 0))
-    return pl.pallas_call(
-        turn_c_kernel,
-        grid=(C // GC,),
-        in_specs=[NATIVE, edges, edges],
-        out_specs=[TURNED, spec, spec],
-        out_shape=[jax.ShapeDtypeStruct((R, C, W), BF16), shape, shape],
-        compiler_params=pltpu.CompilerParams(vmem_limit_bytes=VMEM_LIMIT),
-        name="turn_c",
-    )(c, left, right)
-
-
-def fill_kernel(up_in, down_in, left, right, up, down, rows, sems):
+        name="turn_both",
+    )(x, c)
+
+
+def fill_kernel(x_up_in, x_down_in, c_up_in, c_down_in, left, right, x_up, x_down, c_up, c_down, rows, sems):
     copies = []
-    for q, (out, first) in enumerate(((up, 0), (down, XTILES - 2))):
+    for q, (out, first, at) in enumerate((
+        (x_up, 0, XHALO),
+        (x_down, XTILES - 2, XHALO),
+        (c_up, XTILES, HALO),
+        (c_down, XTILES + CTILES - 2, HALO),
+    )):
         tiles = [left[first], left[first + 1], right[first], right[first + 1]]
         rows[q] = jnp.concatenate(tiles, axis=1)
-        copies.append(pltpu.make_async_copy(rows.at[q], out.at[XHALO], sems.at[q]))
+        copies.append(pltpu.make_async_copy(rows.at[q], out.at[at], sems.at[q]))
         copies[-1].start()
     for copy in copies:
         copy.wait()
 
 
-def fill_x(up, down, left, right):
-    shape = jax.ShapeDtypeStruct(up.shape, BF16)
+def fill(messages, left, right):
     return pl.pallas_call(
         fill_kernel,
-        in_specs=[ANY, ANY, VM, VM],
-        out_specs=[ANY, ANY],
-        out_shape=[shape, shape],
-        input_output_aliases={0: 0, 1: 1},
-        scratch_shapes=[pltpu.VMEM((2, C, W), BF16), pltpu.SemaphoreType.DMA((2,))],
-        name="fill_x",
-    )(up, down, left, right)
+        in_specs=[ANY] * 4 + [VM, VM],
+        out_specs=[ANY] * 4,
+        out_shape=[jax.ShapeDtypeStruct(m.shape, BF16) for m in messages],
+        input_output_aliases={q: q for q in range(4)},
+        scratch_shapes=[pltpu.VMEM((4, C, W), BF16), pltpu.SemaphoreType.DMA((4,))],
+        name="fill_messages",
+    )(*messages, left, right)
 
 
 ANY = pl.BlockSpec(memory_space=pl.ANY)
@@ -187,7 +168,7 @@
 
 
 def build_mask(tiles, mask):
-    row_dev, col_dev = lax.axis_index("rows"), lax.axis_index("cols")
+    row_dev, col_dev = lax.axis_index("rows"), lax.axis_index(COLS)
     n_rows, n_cols = tiles.shape
     first_row, first_tile = row_dev * R, col_dev * (W // TILE)
     lane = lax.broadcasted_iota(jnp.int32, (16, 128), 1)
@@ -224,10 +205,6 @@
     ahead, behind = shifted(v, d), shifted(v, -d)
     parts = [ahead, v, behind] if reverse else [behind, v, ahead]
     return jnp.concatenate(parts, axis=0)
-
-
-def col_stack(ref, r, d, at):
-    return jnp.concatenate([ref[r + d, :, at], ref[r, :, at], ref[r - d, :, at]], axis=0)
 
 
 def forward_matrix(w):
@@ -360,9 +337,9 @@
         def post(row, at, pre):
             h1[row, :, at] = masked(elu(pre).astype(BF16), mask, row, at)
 
-        conv_rows(xe, [r + q for q in range(STEP)], d1, False, wr1, post)
-
-    loop(R, STEP, hidden_one)
+        conv_rows(xe, [r + q for q in range(16)], d1, False, wr1, post)
+
+    loop(R, 16, hidden_one)
     saves.append(pltpu.make_async_copy(h1, h1_out, sems.at[3]))
     saves[-1].start()
 
@@ -380,9 +357,9 @@
         def post(row, at, pre):
             h2[row, :, at] = masked(elu(pre).astype(BF16), mask, row + d1, at)
 
-        conv_rows(b1, [r + q for q in range(STEP)], d2, False, wr2, post)
-
-    loop(INNER, STEP, hidden_two)
+        conv_rows(b1, [r + q for q in range(12)], d2, False, wr2, post)
+
+    loop(INNER, 12, hidden_two)
     saves.append(pltpu.make_async_copy(h2, h2_out, sems.at[5]))
     saves.append(pltpu.make_async_copy(h2.at[0 : d2 - d1, :, 0:W], up_out, sems.at[6]))
     saves.append(pltpu.make_async_copy(h2.at[INNER - (d2 - d1) : INNER, :, 0:W], down_out, sems.at[7]))
@@ -457,16 +434,14 @@
     for load in loads:
         load.wait()
 
-    def side_step(side, _):
+    for side in range(2):
         first = side * R - n
 
         def post_h1(row, at, pre):
             h1[side, row, :, at] = masked(elu(pre).astype(BF16), mask, row + first, at)
 
         conv_rows(x.at[side], [side * n + q for q in range(n)], d1, False, wr1, post_h1)
-        return 0
-
-    def side_next(side, _):
+    for side in range(2):
         first = side * R - n
 
         def post_b1(row, at, col):
@@ -474,20 +449,13 @@
             b1[side, row - d1, :, at] = x[side, row, :, at] + kept
 
         conv_columns(h1.at[side], [d1 + q for q in range(d1)], d1, wc1, post_b1)
-        return 0
-
-    def side_last(side, _):
+    for side in range(2):
         first = side * R - d1
 
         def post_h2(row, at, pre):
             h2[side, row, :, at] = masked(elu(pre).astype(BF16), mask, row + first, at)
 
         conv_rows(b1.at[side], [q for q in range(n)], d2, False, wr2, post_h2)
-        return 0
-
-    lax.fori_loop(0, 2, side_step, 0)
-    lax.fori_loop(0, 2, side_next, 0)
-    lax.fori_loop(0, 2, side_last, 0)
     saves = [pltpu.make_async_copy(b1, b1_out, sems.at[6]), pltpu.make_async_copy(h2, h2_out, sems.at[7])]
     for save in saves:
         save.start()
@@ -565,8 +533,8 @@
 
 def backward_kernel(
     tiles, c, above, below, left, right, wr, wc, x_in, h1_in, b1_in, b1_side, h2_in, h2_side,
-    out, taps,
-    packed, ce, cm, h1, b1, h2, x, a2, cg1, g1, a1, flat, mask, sems,
+    taps, a1_out, g1_out,
+    packed, ce, cm, h1, b1, h2, x, a2, cg1, g1, a1, col_acc, row_acc, mask, sems,
 ):
     d1, d2 = FIRST_SPACING, SECOND_SPACING
     n = 2 * d1
@@ -601,7 +569,6 @@
     wr1, wr2 = backward_matrix(wr[0]), backward_matrix(wr[1])
     wc1, wc2 = backward_matrix(wc[0], (2, 1, 0)), backward_matrix(wc[1], (2, 1, 0))
     wc1w, wc2w = two_rows(wc1), two_rows(wc2)
-    taps[...] = jnp.zeros_like(taps)
     for load in loads:
         load.wait()
     for side, first, skip in ((0, 0, 2 * per - HALO), (1, HALO + R, 0)):
@@ -633,16 +600,30 @@
     for load in late[3:6]:
         load.wait()
 
-    def add_taps(k, left, right):
-        taps[k] += dot_nt(jnp.concatenate(left, axis=1), jnp.concatenate(right, axis=1))
-
-    own = slice(0, W)
-
-    def col_taps_two(r):
-        rows = [r + q for q in range(4)]
-        add_taps(0, [col_stack(cm, s + HALO, d2, own) for s in rows], [h2[s + d1, :, own] for s in rows])
-
-    loop(R, 4, col_taps_two)
+    col_acc[...] = jnp.zeros_like(col_acc)
+    row_acc[...] = jnp.zeros_like(row_acc)
+
+    def add_col_taps(k, grads, g, hidden, h, d, rows):
+        acc = col_acc[k]
+        for r in rows:
+            for at in MAIN:
+                left = jnp.concatenate([hidden[r + h + q * d, :, at] for q in (0, 1)], axis=0)
+                right = jnp.concatenate([grads[r + g + q * d, :, at] for q in (-1, 0, 1, 2)], axis=0)
+                acc += dot_nt(left, right)
+        col_acc[k] = acc
+
+    def add_row_taps(k, values, stacks):
+        acc = row_acc[k]
+        for value, stack in zip(values, stacks):
+            for at in MAIN:
+                acc += dot_nt(value[:, at], stack[:, at])
+        row_acc[k] = acc
+
+    def col_taps_two(i):
+        r = (i // d2) * 2 * d2 + i % d2
+        add_col_taps(0, cm, HALO, h2, d1, d2, [r + q for q in range(4)])
+
+    loop(R // 2, 4, col_taps_two)
 
     def post_one(row, at, mixed):
         g = ce[row + up, :, at].astype(F32) + mixed
@@ -651,13 +632,15 @@
             g1[row, :, at] = g
 
     def grad_one(r):
-        rows = [r + q + d1 for q in range(4)]
+        rows = [r + q + d1 for q in range(STEP)]
         stacks = conv_rows(a2, rows, d2, True, wr2, post_one)
-        add_taps(1, [s[:, own] for s in stacks], [b1[s - d1, :, own] for s in rows])
+        add_row_taps(0, [b1[s - d1] for s in rows], stacks)
 
     for first in (0, R + d1):
         conv_rows(a2, [first + q for q in range(d1)], d2, True, wr2, post_one)
-    loop(R, 4, grad_one)
+    loop(R, STEP, grad_one)
+    save_g1 = pltpu.make_async_copy(g1.at[d1 : R + d1], g1_out, sems.at[13])
+    save_g1.start()
     for load in late[6:8]:
         load.wait()
 
@@ -668,27 +651,38 @@
 
         rows = [r + q for q in range(2 * d1)]
         conv_columns(cg1, [s + d1 for s in rows[:d1]], d1, wc1w, post)
-        add_taps(2, [col_stack(cg1, s + d1, d1, own) for s in rows], [h1[s, :, own] for s in rows])
+        add_col_taps(1, cg1, d1, h1, 0, d1, rows[:d1])
 
     loop(R, 2 * d1, act_one)
 
+    save_a1 = pltpu.make_async_copy(a1, a1_out, sems.at[14])
+    save_a1.start()
+
     def last(r):
-        def post(row, at, mixed):
-            flat[row, :, at] = (g1[row + d1, :, at] + mixed).astype(BF16)
-
-        rows = [r + q for q in range(4)]
-        stacks = conv_rows(a1, rows, d1, True, wr1, post, tail=False)
-        add_taps(3, [s[:, own] for s in stacks], [x[s] for s in rows])
-
-    loop(R, 4, last)
-    turn_out(flat, out)
+        rows = [r + q for q in range(STEP)]
+        add_row_taps(1, [x[s] for s in rows], [row_stack(a1[s], d1, True) for s in rows])
+
+    loop(R, STEP, last)
+    save_a1.wait()
+    save_g1.wait()
+    for k in range(2):
+        acc = col_acc[k]
+        low, high = acc[:C].T, acc[C:].T
+        col = [low[(2 - q) * C : (3 - q) * C] + high[(3 - q) * C : (4 - q) * C] for q in range(3)]
+        both = jnp.concatenate([jnp.concatenate(col, axis=0), row_acc[k].T], axis=1)
+        for q in range(PIECES // 2):
+            taps[k * PIECES // 2 + q] = both[q * PIECE : (q + 1) * PIECE]
+
+
+PIECES = 32
+PIECE = 6 * C // PIECES
 
 
 def backward(*args):
     n = 2 * FIRST_SPACING
     return call(
         backward_kernel, "backward", [SM, ANY, ANY, ANY, VM, VM, VM, VM] + [ANY] * 6,
-        [(VM, (C, R, W), BF16), (VM, (4, 3 * C, C), F32)],
+        [(VM, (PIECES, PIECE, 2 * C), F32), (ANY, (R, C, E), BF16), (ANY, (R, C, W), F32)],
         [
             pltpu.VMEM((2, C, W), BF16),
             pltpu.VMEM((R + 2 * HALO, C, E), BF16),
@@ -701,28 +695,67 @@
             pltpu.VMEM((R + n, C, E), BF16),
             pltpu.VMEM((R + n, C, W), F32),
             pltpu.VMEM((R, C, E), BF16),
-            pltpu.VMEM((R, C, W), BF16),
+            pltpu.VMEM((2, 2 * C, 4 * C), F32),
+            pltpu.VMEM((2, C, 3 * C), F32),
             pltpu.VMEM((3, 16, E), BF16),
-            pltpu.SemaphoreType.DMA((13,)),
+            pltpu.SemaphoreType.DMA((15,)),
         ],
         25, *args,
     )
 
 
-def tap_sum(taps):
-    flat = taps.reshape(-1, 128)
-    wide = lax.axis_size("rows")
-    part = lax.all_to_all(flat, "rows", 0, 0, tiled=True).reshape(wide, -1, 128).sum(0)
-    cols = lax.axis_size("cols")
-    spread = jnp.broadcast_to(part[None], (cols,) + part.shape).reshape(-1, 128)
-    part = lax.all_to_all(spread, "cols", 0, 0, tiled=True).reshape(cols, -1, 128).sum(0)
-    spread = jnp.broadcast_to(part[None], (wide,) + part.shape).reshape(-1, 128)
+def map_kernel(a1_in, g1_in, wr, out, a1, g1, flat, sems):
+    half = R // 2
+    loads = []
+    for q in range(2):
+        at = pl.ds(q * half, half)
+        loads.append(pltpu.make_async_copy(a1_in.at[at], a1.at[at], sems.at[2 * q]))
+        loads.append(pltpu.make_async_copy(g1_in.at[at], g1.at[at], sems.at[2 * q + 1]))
+    for load in loads:
+        load.start()
+    wr1 = backward_matrix(wr[0])
+
+    def last(r):
+        def post(row, at, mixed):
+            flat[row, :, at] = (g1[row, :, at] + mixed).astype(BF16)
+
+        conv_rows(a1, [r + q for q in range(STEP)], FIRST_SPACING, True, wr1, post, tail=False)
+
+    for q in range(2):
+        loads[2 * q].wait()
+        loads[2 * q + 1].wait()
+        loop(half, STEP, lambda r, q=q: last(q * half + r))
+    turn_out(flat, out)
+
+
+def backward_map(*args):
+    return call(
+        map_kernel, "backward_map", [ANY, ANY, VM],
+        [(VM, (C, R, W), BF16)],
+        [
+            pltpu.VMEM((R, C, E), BF16),
+            pltpu.VMEM((R, C, W), F32),
+            pltpu.VMEM((R, C, W), BF16),
+            pltpu.SemaphoreType.DMA((4,)),
+        ],
+        4, *args,
+    )[0]
+
+
+def tap_sum(taps, beside):
+    part = lax.all_to_all(taps, "rows", 0, 0, tiled=True)
+    part, beside = lax.optimization_barrier((part, beside))
+    part = lax.all_gather(part.sum(0), COLS).sum(0)
+    spread = jnp.broadcast_to(part[None], taps.shape)
     whole = lax.all_to_all(spread, "rows", 0, 0, tiled=True)
-    return whole.reshape(4, 3, C, C)
+    return whole.reshape(2, 3, C, 2 * C), beside
+
+
+COLS = ("y_hi", "core")
 
 
 def on_device(x, tile_mask, wr, wc, cot):
-    n_rows, n_cols = lax.axis_size("rows"), lax.axis_size("cols")
+    n_rows, n_cols = lax.axis_size("rows"), lax.axis_size(COLS)
     factor = 1.0 / math.sqrt(R * n_rows * W * n_cols)
     down = [(i, i + 1) for i in range(n_rows - 1)]
     up = [(i + 1, i) for i in range(n_rows - 1)]
@@ -730,13 +763,12 @@
     left = [(i + 1, i) for i in range(n_cols - 1)]
 
     to_left, to_right = pack_edges(x, cot)
-    from_right = lax.ppermute(to_left, "cols", left)
-    from_left = lax.ppermute(to_right, "cols", right)
-    xt, x_up, x_down = turn_x(x)
-    x_up, x_down = fill_x(x_up, x_down, from_left, from_right)
+    from_right = lax.ppermute(to_left, COLS, left)
+    from_left = lax.ppermute(to_right, COLS, right)
+    xt, x_up, x_down, ct, c_up, c_down = turn_both(x, cot)
+    x_up, x_down, c_up, c_down = fill((x_up, x_down, c_up, c_down), from_left, from_right)
     x_above = lax.ppermute(x_down, "rows", down)
     x_below = lax.ppermute(x_up, "rows", up)
-    ct, c_up, c_down = turn_c(cot, from_left, from_right)
     c_above = lax.ppermute(c_down, "rows", down)
     c_below = lax.ppermute(c_up, "rows", up)
 
@@ -744,22 +776,24 @@
     h2_above = lax.ppermute(h2_down, "rows", down)
     h2_below = lax.ppermute(h2_up, "rows", up)
     b1_side, h2_side = forward_outer(tile_mask, x_above, x_below, x_side, h1, wr, wc)
-    map_grad, taps = backward(
+    taps, a1, g1 = backward(
         tile_mask, ct, c_above, c_below, from_left, from_right, wr, wc, xt, h1, b1, b1_side, h2, h2_side
     )
+    taps, h2_above, h2_below = lax.optimization_barrier((taps, h2_above, h2_below))
     final = forward_final(tile_mask, h2_above, h2_below, b1, b1_side, h2, h2_side, wc)
-    total = tap_sum(taps) * factor
-    row_grad = jnp.stack([total[3], total[1]])
-    col_grad = jnp.stack([total[2], total[0]])
-    return final, map_grad, row_grad, col_grad
+    total, map_grad = tap_sum(taps, backward_map(a1, g1, wr))
+    total = total[::-1] * factor
+    return final, map_grad, total[..., C:], total[..., :C]
 
 
 def solution(mesh):
-    placed = (P(None, "rows", "cols"), P(), P(), P(), P(None, "rows", "cols"))
+    n_rows, n_cols = mesh.devices.shape
+    inner = Mesh(mesh.devices.reshape(n_rows, n_cols // 2, 2), ("rows",) + COLS)
+    blocks = P(None, "rows", COLS)
     return jax.shard_map(
         on_device,
-        mesh=mesh,
-        in_specs=placed,
-        out_specs=(P(None, "rows", "cols"), P(None, "rows", "cols"), P(), P()),
+        mesh=inner,
+        in_specs=(blocks, P(), P(), P(), blocks),
+        out_specs=(blocks, blocks, P(), P()),
         check_vma=False,
     )

time: 137 us -> 126 us (0.920)
  blocking collectives: 36.3 us -> 10.4 us
  starting transfers between devices: 23.3 us -> 38.8 us
  waiting for transfers between devices: 2.75 us -> 6.62 us
  local copies, waits for them, and re-layouts: 6.26 us -> 4.02 us
  Pallas kernels: 65.6 us -> 63.4 us
    all_to_all x2 -> x0, blocking collectives: 36.3 us -> none  [the longest x1 23.5 us: tap_sum(): lax.all_to_all(flat, 'rows', 0, 0, tiled=True).reshape(wide, -1, 128).sum(0)]
    all_to_all x0 -> x1, starting transfers between devices: none -> 12.9 us  [tap_sum(): part = lax.all_to_all(taps, 'rows', 0, 0, tiled=True)]
    all_gather x0 -> x1, blocking collectives: none -> 10.4 us  [tap_sum(): part = lax.all_gather(part.sum(0), COLS).sum(0)]
    pallas_call x3 -> x2, Pallas kernels: 10.5 us -> 7.88 us  [the longest x1 6.09 us: turn_both(): pl.pallas_call(turn_kernel, grid=(C // GC,), in_specs=[native, native], o...]
    all_to_all x1, starting transfers between devices: 3.87 us -> 5.91 us  [tap_sum(): whole = lax.all_to_all(spread, 'rows', 0, 0, tiled=True)]
    ppermute x1, waiting for transfers between devices: 0.01 us -> 1.91 us  [on_device(): c_below = lax.ppermute(c_up, 'rows', up)]
    all_to_all x1, waiting for transfers between devices: 1.3 us -> 3 us  [tap_sum(): whole = lax.all_to_all(spread, 'rows', 0, 0, tiled=True)]
    all_to_all x0 -> x1, waiting for transfers between devices: none -> 1.7 us  [tap_sum(): part = lax.all_to_all(taps, 'rows', 0, 0, tiled=True)]
  transfers between devices with their start and end apart: 9 -> 10, of which waited for: 2 -> 3; matrix products, arithmetic and copies ran while one was open for 1% -> 0% of each run, Pallas kernels for 44% -> 46%
where the time goes in v3:
time: 126 us; the launch traced here: 124 us
  Pallas kernels  63.4 us (50%)
  starting transfers between devices  38.8 us (31%)
  blocking collectives  10.4 us (8%)
  waiting for transfers between devices  6.62 us (5%)
  local copies, waits for them, and re-layouts  4.02 us (3%)
    pallas_call x5, Pallas kernels, call(): pl.pallas_call(kernel, in_specs=in_specs, out_specs=[spec for spec, _, _...  51.4 us
    all_to_all x1, starting transfers between devices, tap_sum(): part = lax.all_to_all(taps, 'rows', 0, 0, tiled=True)  12.9 us
    all_gather x1, blocking collectives, tap_sum(): part = lax.all_gather(part.sum(0), COLS).sum(0)  10.4 us
    pallas_call x1, Pallas kernels, turn_both(): pl.pallas_call(turn_kernel, grid=(C // GC,), in_specs=[native, native], o...  6.09 us
    all_to_all x1, starting transfers between devices, tap_sum(): whole = lax.all_to_all(spread, 'rows', 0, 0, tiled=True)  5.91 us
    ppermute x1, starting transfers between devices, on_device(): c_above = lax.ppermute(c_down, 'rows', down)  4.6 us
    ppermute x1, starting transfers between devices, on_device(): h2_above = lax.ppermute(h2_down, 'rows', down)  4.56 us
    ppermute x1, starting transfers between devices, on_device(): x_above = lax.ppermute(x_down, 'rows', down)  4.39 us
  transfers between devices with their start and end apart: 10, of which 3 were waited for; matrix products, arithmetic and copies ran while one was open for 0% of the time, Pallas kernels for 46%

profile of v3, /device:TPU:0, one launch (start us, length us, event | category | flops | bytes accessed | tf_op | source)
XLA Modules:
  0.0 124.2 jit_solution(6243593735830362815)
XLA Ops:
  0.6 4.1 %pack_edges.1 = (bf16[12,64,128]{2,1,0:T(8,128)(2,1)}, bf16[12,64,128]{2,1,0:T(8,128)(2,1)}) custom-call(bf16[64,32,512]{2,1,0:T(8,128)(2,1)} %x_high.1, bf16[64,32,512]{2,1,0:T(8,128)(2,1)} %x_high.1, bf16[64,32,512]{2,1,0:T(8,128)(2,1)} %c_high.1, bf16[64,32,512]{2,1,0:T(8,128)(2,1)} %c_high.1), custom_call_target="tpu_custom_call" | custom-call | tf_op jit(solution)/shard_map/pack_edges/pallas_call | solution.py:88
  4.7 1.3 %collective-permute-start = (bf16[12,64,128]{2,1,0:T(8,128)(2,1)}, bf16[12,64,128]{2,1,0:T(8,128)(2,1)S(1)}, u32[]{:S(2)}, u32[]{:S(2)}) collective-permute-start(bf16[12,64,128]{2,1,0:T(8,128)(2,1)} %get-tuple-element.37), channel_id=1, source_target_pairs={{0,1},{1,2},{2,3},{4,5},{5,6},{6,7},{8,9},{9,10},{10,11},{12,13},{... | collective-permute-start | bytes 589832 | tf_op jit(solution)/shard_map/ppermute | solution.py:767
  6.0 1.3 %collective-permute-start.1 = (bf16[12,64,128]{2,1,0:T(8,128)(2,1)}, bf16[12,64,128]{2,1,0:T(8,128)(2,1)S(1)}, u32[]{:S(2)}, u32[]{:S(2)}) collective-permute-start(bf16[12,64,128]{2,1,0:T(8,128)(2,1)} %get-tuple-element.38), channel_id=1, source_target_pairs={{1,0},{2,1},{3,2},{5,4},{6,5},{7,6},{9,8},{10,9},{11,10},{13,12},{... | collective-permute-start | bytes 589832 | tf_op jit(solution)/shard_map/ppermute | solution.py:766
  7.3 6.1 %turn_both.1 = (bf16[32,64,512]{2,1,0:T(8,128)(2,1)}, bf16[9,64,512]{2,1,0:T(8,128)(2,1)}, bf16[9,64,512]{2,1,0:T(8,128)(2,1)}, bf16[32,64,512]{2,1,0:T(8,128)(2...) custom-call(bf16[64,32,512]{2,1,0:T(8,128)(2,1)} %x_high.1, bf16[64,32,512]{2,1,0:T(8,128)(2,1)} %c_high.1), custom_call_target="tpu_custom_call" | custom-call | tf_op jit(solution)/shard_map/turn_both/pallas_call | solution.py:125
  13.4 0.0 collective-permute-done.left
  13.4 0.0 copy-start.2
  13.4 0.0 collective-permute-done.1.right
  13.4 0.0 copy-start.3
  13.4 0.6 copy-done.2
  14.1 0.1 copy-done.3
  14.1 1.8 %fill_messages.1 = (bf16[9,64,512]{2,1,0:T(8,128)(2,1)}, bf16[9,64,512]{2,1,0:T(8,128)(2,1)}, bf16[13,64,512]{2,1,0:T(8,128)(2,1)}, bf16[13,64,512]{2,1,0:T(8,128)(2,1)}) custom-call(bf16[9,64,512]{2,1,0:T(8,128)(2,1)} %get-tuple-element.33.x_up_in, ...), custom_call_target="tpu_custom_call", output_to_operand_aliasing={{0}: (0, {}), {1}: (1, {}), {2}: (2, {}), {3}: (3, {})} | custom-call | tf_op jit(solution)/shard_map/fill_messages/pallas_call | solution.py:153
  15.9 4.4 %collective-permute-start.4 = (bf16[9,64,512]{2,1,0:T(8,128)(2,1)}, bf16[9,64,512]{2,1,0:T(8,128)(2,1)S(1)}, u32[]{:S(2)}, u32[]{:S(2)}) collective-permute-start(bf16[9,64,512]{2,1,0:T(8,128)(2,1)} %get-tuple-element.44), channel_id=1, source_target_pairs={{0,4},{4,8},{8,12},{12,16},{16,20},{20,24},{24,28},{28,32},{32,36}... | collective-permute-start | bytes 1769480 | tf_op jit(solution)/shard_map/ppermute | solution.py:770
  20.3 1.3 %collective-permute-start.5 = (bf16[9,64,512]{2,1,0:T(8,128)(2,1)}, bf16[9,64,512]{2,1,0:T(8,128)(2,1)S(1)}, u32[]{:S(2)}, u32[]{:S(2)}) collective-permute-start(bf16[9,64,512]{2,1,0:T(8,128)(2,1)} %get-tuple-element.45), channel_id=1, source_target_pairs={{4,0},{8,4},{12,8},{16,12},{20,16},{24,20},{28,24},{32,28},{36,32}... | collective-permute-start | bytes 1769480 | tf_op jit(solution)/shard_map/ppermute | solution.py:771
  21.6 4.6 %collective-permute-start.2 = (bf16[13,64,512]{2,1,0:T(8,128)(2,1)}, bf16[13,64,512]{2,1,0:T(8,128)(2,1)S(1)}, u32[]{:S(2)}, u32[]{:S(2)}) collective-permute-start(bf16[13,64,512]{2,1,0:T(8,128)(2,1)} %get-tuple-element.39), channel_id=1, source_target_pairs={{0,4},{4,8},{8,12},{12,16},{16,20},{20,24},{24,28},{28,32},{32,36}... | collective-permute-start | bytes 2555912 | tf_op jit(solution)/shard_map/ppermute | solution.py:772
  26.2 1.3 %collective-permute-start.3 = (bf16[13,64,512]{2,1,0:T(8,128)(2,1)}, bf16[13,64,512]{2,1,0:T(8,128)(2,1)S(1)}, u32[]{:S(2)}, u32[]{:S(2)}) collective-permute-start(bf16[13,64,512]{2,1,0:T(8,128)(2,1)} %get-tuple-element.40), channel_id=1, source_target_pairs={{4,0},{8,4},{12,8},{16,12},{20,16},{24,20},{28,24},{32,28},{36,32}... | collective-permute-start | bytes 2555912 | tf_op jit(solution)/shard_map/ppermute | solution.py:773
  27.5 10.0 %forward_inner.1 = (bf16[2,8,64,640]{3,2,1,0:T(8,128)(2,1)}, bf16[32,64,640]{2,1,0:T(8,128)(2,1)}, bf16[24,64,640]{2,1,0:T(8,128)(2,1)}, bf16[24,64,640]{2,1,0:T...) custom-call(s32[8,16]{1,0:T(8,128)} %tiles.7, bf16[32,64,512]{2,1,0:T(8,128)(2,1)} %get-tuple-element.41.x.x_in, ...), custom_call_target="tpu_custom_call" | custom-call | flops 5000000000 | bytes 10000000 | tf_op jit(solution)/shard_map/forward_inner/pallas_call | solution.py:294
  37.6 4.6 %collective-permute-start.6 = (bf16[4,64,512]{2,1,0:T(8,128)(2,1)}, bf16[4,64,512]{2,1,0:T(8,128)(2,1)S(1)}, u32[]{:S(2)}, u32[]{:S(2)}) collective-permute-start(bf16[4,64,512]{2,1,0:T(8,128)(2,1)} %get-tuple-element.51), channel_id=1, source_target_pairs={{0,4},{4,8},{8,12},{12,16},{16,20},{20,24},{24,28},{28,32},{32,36}... | collective-permute-start | bytes 786440 | tf_op jit(solution)/shard_map/ppermute | solution.py:776
  42.1 0.0 collective-permute-done.4.above
  42.1 0.0 copy-start.6
  42.1 1.3 %collective-permute-start.7 = (bf16[4,64,512]{2,1,0:T(8,128)(2,1)}, bf16[4,64,512]{2,1,0:T(8,128)(2,1)S(1)}, u32[]{:S(2)}, u32[]{:S(2)}) collective-permute-start(bf16[4,64,512]{2,1,0:T(8,128)(2,1)} %get-tuple-element.52), channel_id=1, source_target_pairs={{4,0},{8,4},{12,8},{16,12},{20,16},{24,20},{28,24},{32,28},{36,32}... | collective-permute-start | bytes 786440 | tf_op jit(solution)/shard_map/ppermute | solution.py:777
  43.4 0.0 collective-permute-done.5.below
  43.4 0.0 copy-start.7
  43.5 0.0 copy-done.6
  43.5 0.8 copy-done.7
  44.3 7.0 %forward_outer.1 = (bf16[2,8,64,640]{3,2,1,0:T(8,128)(2,1)}, bf16[2,8,64,640]{3,2,1,0:T(8,128)(2,1)}) custom-call(s32[8,16]{1,0:T(8,128)} %tiles.7, bf16[9,64,512]{2,1,0:T(8,128)(2,1)} %copy-done.6, bf16[9,64,512]{2,1,0:T(8,128)(2,1)} %copy-done.7, bf16[2,8,64,640]{3,2,1,0:T(8,128)(2,1)} %get-tuple-element.46.x_in, ...), custom_call_target="tpu_custom_call" | custom-call | flops 3500000000 | bytes 7000000 | tf_op jit(solution)/shard_map/forward_outer/pallas_call | solution.py:294
  51.3 0.0 collective-permute-done.2.above
  51.3 0.0 copy-start.4
  51.3 1.9 %collective-permute-done.3.below = bf16[13,64,512]{2,1,0:T(8,128)(2,1)S(1)} collective-permute-done((bf16[13,64,512]{2,1,0:T(8,128)(2,1)}, bf16[13,64,512]{2,1,0:T(8,128)(2,1)S(1)}, u32[]{:S(2)}, u32[]{:S(2)}) %collective-permute-start.3) | collective-permute-done | bytes 852000 | tf_op jit(solution)/shard_map/ppermute | solution.py:773
  53.2 0.0 copy-start.5
  53.2 0.0 copy-done.4
  53.2 0.9 copy-done.5
  54.1 20.4 %backward.1 = (f32[32,12,128]{2,1,0:T(8,128)}, bf16[32,64,640]{2,1,0:T(8,128)(2,1)}, f32[32,64,512]{2,1,0:T(8,128)}) custom-call(s32[8,16]{1,0:T(8,128)} %tiles.7, bf16[32,64,512]{2,1,0:T(8,128)(2,1)} %get-tuple-element.32.c, bf16[13,64,512]{2,1,0:T(8,128)(2,1)} %copy-done.4, bf16[13,64,512]{2,1,0:T(8,128)(2,1)} %copy-done.5, ...), custom_call_target="tpu_custom_call" | custom-call | flops 12499999744 | bytes 25000000 | tf_op jit(solution)/shard_map/backward/pallas_call | solution.py:294
  74.5 0.0 collective-permute-done.6.above
  74.5 0.0 copy-start
  74.5 0.0 collective-permute-done.7.below
  74.5 0.0 copy-start.1
  74.6 12.9 %all-to-all-start = ((f32[32,12,128]{2,1,0:T(8,128)}), f32[32,12,128]{2,1,0:T(8,128)S(1)}, u32[]{:S(2)}, u32[]{:S(2)}) async-start(f32[32,12,128]{2,1,0:T(8,128)} %get-tuple-element.55), calls=%async_computation | async-start | bytes 524288 | tf_op jit(solution)/shard_map/all_to_all | solution.py:746
  87.5 7.4 %backward_map.1 = bf16[64,32,512]{2,1,0:T(8,128)(2,1)} custom-call(bf16[32,64,640]{2,1,0:T(8,128)(2,1)} %get-tuple-element.56.a1_in, f32[32,64,512]{2,1,0:T(8,128)} %get-tuple-element.57.g1_in, bf16[2,3,64,64]{3,2,1,0:T(8,128)(2,1)} %wr.7), custom_call_target="tpu_custom_call" | custom-call | flops 2000000000 | bytes 4000000 | tf_op jit(solution)/shard_map/backward_map/pallas_call | solution.py:294
  94.9 0.0 copy-done
  94.9 0.0 copy-done.1
  94.9 1.7 %all-to-all-done = f32[32,12,128]{2,1,0:T(8,128)S(1)} async-done(((f32[32,12,128]{2,1,0:T(8,128)}), f32[32,12,128]{2,1,0:T(8,128)S(1)}, u32[]{:S(2)}, u32[]{:S(2)}) %all-to-all-start) | async-done | bytes 196640 | tf_op jit(solution)/shard_map/all_to_all | solution.py:746
  96.6 10.4 %all-gather.1 = f32[4,12,128]{2,1,0:T(8,128)S(1)} all-gather(f32[1,12,128]{2,1,0:T(8,128)S(1)} %bitcast.1), channel_id=2, replica_groups=mesh['rows'=32,'y_hi'=2,'core'=2] {'y_hi','core'}, dimensions={0}, use_global_device_ids=true | all-gather | bytes 30720 | tf_op jit(solution)/shard_map/all_gather | solution.py:748
  107.0 0.7 broadcast_in_dim.2
  107.8 5.9 %all-to-all-start.1 = ((f32[32,12,128]{2,1,0:T(8,128)}), f32[32,12,128]{2,1,0:T(8,128)S(1)}, u32[]{:S(2)}, u32[]{:S(2)}) async-start(f32[32,12,128]{2,1,0:T(8,128)} %broadcast_in_dim.2), calls=%async_computation.1 | async-start | bytes 524288 | tf_op jit(solution)/shard_map/all_to_all | solution.py:750
  113.7 6.7 %forward_final.1 = bf16[64,32,512]{2,1,0:T(8,128)(2,1)} custom-call(s32[8,16]{1,0:T(8,128)} %tiles.7, bf16[4,64,512]{2,1,0:T(8,128)(2,1)} %copy-done, bf16[4,64,512]{2,1,0:T(8,128)(2,1)} %copy-done.1, bf16[24,64,640]{2,1,0:T(8,128)(2,1)} %get-tuple-element.43.b1_in, bf16[2,8,64,640]{3,2,1,0:T(8,128)(2,1)} %get-tuple-element.47.b1_side, ...), custom_call_target="tpu_custom_call" | custom-call | flops 2000000000 | bytes 4000000 | tf_op jit(solution)/shard_map/forward_final/pallas_call | solution.py:294
  120.4 3.0 %all-to-all-done.1 = f32[32,12,128]{2,1,0:T(8,128)S(1)} async-done(((f32[32,12,128]{2,1,0:T(8,128)}), f32[32,12,128]{2,1,0:T(8,128)S(1)}, u32[]{:S(2)}, u32[]{:S(2)}) %all-to-all-start.1) | async-done | bytes 196640 | tf_op jit(solution)/shard_map/all_to_all | solution.py:750
  123.4 0.8 fusion
  (4 shorter events, 0.1 us)
Async XLA Ops:
  4.7 8.7 %collective-permute-start = (bf16[12,64,128]{2,1,0:T(8,128)(2,1)}, bf16[12,64,128]{2,1,0:T(8,128)(2,1)S(1)}, u32[]{:S(2)}, u32[]{:S(2)}) collective-permute-start(bf16[12,64,128]{2,1,0:T(8,128)(2,1)} %get-tuple-element.37), channel_id=1, source_target_pairs={{0,1},{1,2},{2,3},{4,5},{5,6},{6,7},{8,9},{9,10},{10,11},{12,13},{... | collective-permute-start | bytes 589832 | tf_op jit(solution)/shard_map/ppermute | solution.py:767
  6.0 7.4 %collective-permute-start.1 = (bf16[12,64,128]{2,1,0:T(8,128)(2,1)}, bf16[12,64,128]{2,1,0:T(8,128)(2,1)S(1)}, u32[]{:S(2)}, u32[]{:S(2)}) collective-permute-start(bf16[12,64,128]{2,1,0:T(8,128)(2,1)} %get-tuple-element.38), channel_id=1, source_target_pairs={{1,0},{2,1},{3,2},{5,4},{6,5},{7,6},{9,8},{10,9},{11,10},{13,12},{... | collective-permute-start | bytes 589832 | tf_op jit(solution)/shard_map/ppermute | solution.py:766
  13.4 0.7 copy-start.2
  13.4 0.7 copy-start.3
  15.9 26.2 %collective-permute-start.4 = (bf16[9,64,512]{2,1,0:T(8,128)(2,1)}, bf16[9,64,512]{2,1,0:T(8,128)(2,1)S(1)}, u32[]{:S(2)}, u32[]{:S(2)}) collective-permute-start(bf16[9,64,512]{2,1,0:T(8,128)(2,1)} %get-tuple-element.44), channel_id=1, source_target_pairs={{0,4},{4,8},{8,12},{12,16},{16,20},{20,24},{24,28},{28,32},{32,36}... | collective-permute-start | bytes 1769480 | tf_op jit(solution)/shard_map/ppermute | solution.py:770
  20.3 23.1 %collective-permute-start.5 = (bf16[9,64,512]{2,1,0:T(8,128)(2,1)}, bf16[9,64,512]{2,1,0:T(8,128)(2,1)S(1)}, u32[]{:S(2)}, u32[]{:S(2)}) collective-permute-start(bf16[9,64,512]{2,1,0:T(8,128)(2,1)} %get-tuple-element.45), channel_id=1, source_target_pairs={{4,0},{8,4},{12,8},{16,12},{20,16},{24,20},{28,24},{32,28},{36,32}... | collective-permute-start | bytes 1769480 | tf_op jit(solution)/shard_map/ppermute | solution.py:771
  21.6 29.7 %collective-permute-start.2 = (bf16[13,64,512]{2,1,0:T(8,128)(2,1)}, bf16[13,64,512]{2,1,0:T(8,128)(2,1)S(1)}, u32[]{:S(2)}, u32[]{:S(2)}) collective-permute-start(bf16[13,64,512]{2,1,0:T(8,128)(2,1)} %get-tuple-element.39), channel_id=1, source_target_pairs={{0,4},{4,8},{8,12},{12,16},{16,20},{20,24},{24,28},{28,32},{32,36}... | collective-permute-start | bytes 2555912 | tf_op jit(solution)/shard_map/ppermute | solution.py:772
  26.2 27.0 %collective-permute-start.3 = (bf16[13,64,512]{2,1,0:T(8,128)(2,1)}, bf16[13,64,512]{2,1,0:T(8,128)(2,1)S(1)}, u32[]{:S(2)}, u32[]{:S(2)}) collective-permute-start(bf16[13,64,512]{2,1,0:T(8,128)(2,1)} %get-tuple-element.40), channel_id=1, source_target_pairs={{4,0},{8,4},{12,8},{16,12},{20,16},{24,20},{28,24},{32,28},{36,32}... | collective-permute-start | bytes 2555912 | tf_op jit(solution)/shard_map/ppermute | solution.py:773
  37.6 37.0 %collective-permute-start.6 = (bf16[4,64,512]{2,1,0:T(8,128)(2,1)}, bf16[4,64,512]{2,1,0:T(8,128)(2,1)S(1)}, u32[]{:S(2)}, u32[]{:S(2)}) collective-permute-start(bf16[4,64,512]{2,1,0:T(8,128)(2,1)} %get-tuple-element.51), channel_id=1, source_target_pairs={{0,4},{4,8},{8,12},{12,16},{16,20},{20,24},{24,28},{28,32},{32,36}... | collective-permute-start | bytes 786440 | tf_op jit(solution)/shard_map/ppermute | solution.py:776
  42.1 1.3 %copy-start.6 = (bf16[9,64,512]{2,1,0:T(8,128)(2,1)}, bf16[9,64,512]{2,1,0:T(8,128)(2,1)S(1)}, u32[]{:S(2)}) copy-start(bf16[9,64,512]{2,1,0:T(8,128)(2,1)S(1)} %collective-permute-done.4.above) | copy-start | bytes 1769476
  42.1 32.4 %collective-permute-start.7 = (bf16[4,64,512]{2,1,0:T(8,128)(2,1)}, bf16[4,64,512]{2,1,0:T(8,128)(2,1)S(1)}, u32[]{:S(2)}, u32[]{:S(2)}) collective-permute-start(bf16[4,64,512]{2,1,0:T(8,128)(2,1)} %get-tuple-element.52), channel_id=1, source_target_pairs={{4,0},{8,4},{12,8},{16,12},{20,16},{24,20},{28,24},{32,28},{36,32}... | collective-permute-start | bytes 786440 | tf_op jit(solution)/shard_map/ppermute | solution.py:777
  43.4 0.9 copy-start.7
  51.3 1.9 %copy-start.4 = (bf16[13,64,512]{2,1,0:T(8,128)(2,1)}, bf16[13,64,512]{2,1,0:T(8,128)(2,1)S(1)}, u32[]{:S(2)}) copy-start(bf16[13,64,512]{2,1,0:T(8,128)(2,1)S(1)} %collective-permute-done.2.above) | copy-start | bytes 2555908
  53.2 0.9 copy-start.5
  74.5 20.4 %copy-start = (bf16[4,64,512]{2,1,0:T(8,128)(2,1)}, bf16[4,64,512]{2,1,0:T(8,128)(2,1)S(1)}, u32[]{:S(2)}) copy-start(bf16[4,64,512]{2,1,0:T(8,128)(2,1)S(1)} %collective-permute-done.6.above) | copy-start | bytes 786436
  74.5 20.4 %copy-start.1 = (bf16[4,64,512]{2,1,0:T(8,128)(2,1)}, bf16[4,64,512]{2,1,0:T(8,128)(2,1)S(1)}, u32[]{:S(2)}) copy-start(bf16[4,64,512]{2,1,0:T(8,128)(2,1)S(1)} %collective-permute-done.7.below) | copy-start | bytes 786436
  74.6 22.0 %all-to-all-start = ((f32[32,12,128]{2,1,0:T(8,128)}), f32[32,12,128]{2,1,0:T(8,128)S(1)}, u32[]{:S(2)}, u32[]{:S(2)}) async-start(f32[32,12,128]{2,1,0:T(8,128)} %get-tuple-element.55), calls=%async_computation | async-start | bytes 524288 | tf_op jit(solution)/shard_map/all_to_all | solution.py:746
  107.8 15.6 %all-to-all-start.1 = ((f32[32,12,128]{2,1,0:T(8,128)}), f32[32,12,128]{2,1,0:T(8,128)S(1)}, u32[]{:S(2)}, u32[]{:S(2)}) async-start(f32[32,12,128]{2,1,0:T(8,128)} %broadcast_in_dim.2), calls=%async_computation.1 | async-start | bytes 524288 | tf_op jit(solution)/shard_map/all_to_all | solution.py:750

commit v4 on v3

--- a/solution.py
+++ b/solution.py
@@ -15,7 +15,6 @@
 R = 32
 W = 512
 E = 640
-XHALO = 8
 HALO = 12
 XEDGE = 32
 CEDGE = 16
@@ -23,7 +22,8 @@
 CTILES = R * CEDGE // 128
 F32 = jnp.float32
 BF16 = jnp.bfloat16
-VMEM_LIMIT = 60 * 1024 * 1024
+MIB = 1024 * 1024
+VM_INNER, VM_OUTER, VM_BACK, VM_TURN = 59, 59, 59, 59
 
 
 def dot(a, b):
@@ -91,7 +91,7 @@
         in_specs=[low, high, low, high],
         out_specs=[out, out],
         out_shape=[jax.ShapeDtypeStruct((XTILES + CTILES, C, 128), BF16)] * 2,
-        compiler_params=pltpu.CompilerParams(vmem_limit_bytes=VMEM_LIMIT),
+        compiler_params=pltpu.CompilerParams(vmem_limit_bytes=16 * MIB),
         name="pack_edges",
     )(x, x, c, c)
 
@@ -103,17 +103,24 @@
             dst[i * 16 : (i + 1) * 16, :, at] = turn(src[:, i * 16 : (i + 1) * 16, at])
 
 
+XROWS = 2 * HALO + 3
+CROWS = HALO + 1
+
+
 def turn_kernel(x_ref, c_ref, xt, x_up, x_down, ct, c_up, c_down):
-    for src, dst, up, down, halo in ((x_ref, xt, x_up, x_down, XHALO), (c_ref, ct, c_up, c_down, HALO)):
-        turn_block(src, dst)
-        up[0:halo] = dst[0:halo]
-        down[0:halo] = dst[R - halo : R]
-
-
-def message(rows):
+    turn_block(x_ref, xt)
+    for out, rows in ((x_up, slice(0, HALO)), (x_down, slice(R - HALO, R))):
+        out[0:HALO] = xt[rows, :, MAIN[0]]
+        out[HALO : 2 * HALO] = xt[rows, :, MAIN[1]]
+    turn_block(c_ref, ct)
+    c_up[0:HALO] = ct[0:HALO]
+    c_down[0:HALO] = ct[R - HALO : R]
+
+
+def message(rows, width):
     return (
-        pl.BlockSpec((rows + 1, GC, W), lambda g: (0, g, 0)),
-        jax.ShapeDtypeStruct((rows + 1, C, W), BF16),
+        pl.BlockSpec((rows, GC, width), lambda g: (0, g, 0)),
+        jax.ShapeDtypeStruct((rows, C, width), BF16),
     )
 
 
@@ -121,30 +128,33 @@
     native = pl.BlockSpec((GC, R, W), lambda g: (g, 0, 0))
     turned = pl.BlockSpec((R, GC, W), lambda g: (0, g, 0))
     block = jax.ShapeDtypeStruct((R, C, W), BF16)
-    (xs, x_shape), (cs, c_shape) = message(XHALO), message(HALO)
+    (xs, x_shape), (cs, c_shape) = message(XROWS, W // 2), message(CROWS, W)
     return pl.pallas_call(
         turn_kernel,
         grid=(C // GC,),
         in_specs=[native, native],
         out_specs=[turned, xs, xs, turned, cs, cs],
         out_shape=[block, x_shape, x_shape, block, c_shape, c_shape],
-        compiler_params=pltpu.CompilerParams(vmem_limit_bytes=VMEM_LIMIT),
+        compiler_params=pltpu.CompilerParams(vmem_limit_bytes=VM_TURN * MIB),
         name="turn_both",
     )(x, c)
 
 
-def fill_kernel(x_up_in, x_down_in, c_up_in, c_down_in, left, right, x_up, x_down, c_up, c_down, rows, sems):
+def fill_kernel(
+    x_up_in, x_down_in, c_up_in, c_down_in, left, right, x_up, x_down, c_up, c_down, x_rows, c_rows, sems
+):
     copies = []
-    for q, (out, first, at) in enumerate((
-        (x_up, 0, XHALO),
-        (x_down, XTILES - 2, XHALO),
-        (c_up, XTILES, HALO),
-        (c_down, XTILES + CTILES - 2, HALO),
-    )):
+    for q, (out, first) in enumerate(((x_up, 0), (x_down, XTILES - 3))):
+        tiles = [left[first + k] for k in range(3)] + [right[first + k] for k in range(3)]
+        for k in range(3):
+            x_rows[q, k] = jnp.concatenate(tiles[2 * k : 2 * k + 2], axis=1)
+        copies.append(pltpu.make_async_copy(x_rows.at[q], out.at[2 * HALO : XROWS], sems.at[q]))
+    for q, (out, first) in enumerate(((c_up, XTILES), (c_down, XTILES + CTILES - 2))):
         tiles = [left[first], left[first + 1], right[first], right[first + 1]]
-        rows[q] = jnp.concatenate(tiles, axis=1)
-        copies.append(pltpu.make_async_copy(rows.at[q], out.at[at], sems.at[q]))
-        copies[-1].start()
+        c_rows[q] = jnp.concatenate(tiles, axis=1)
+        copies.append(pltpu.make_async_copy(c_rows.at[q], out.at[HALO], sems.at[2 + q]))
+    for copy in copies:
+        copy.start()
     for copy in copies:
         copy.wait()
 
@@ -156,7 +166,11 @@
         out_specs=[ANY] * 4,
         out_shape=[jax.ShapeDtypeStruct(m.shape, BF16) for m in messages],
         input_output_aliases={q: q for q in range(4)},
-        scratch_shapes=[pltpu.VMEM((4, C, W), BF16), pltpu.SemaphoreType.DMA((4,))],
+        scratch_shapes=[
+            pltpu.VMEM((2, 3, C, W // 2), BF16),
+            pltpu.VMEM((2, C, W), BF16),
+            pltpu.SemaphoreType.DMA((4,)),
+        ],
         name="fill_messages",
     )(*messages, left, right)
 
@@ -165,6 +179,7 @@
 VM = pl.BlockSpec(memory_space=pltpu.VMEM)
 SM = pl.BlockSpec(memory_space=pltpu.SMEM)
 STEP = 8
+LONG = 16
 
 
 def build_mask(tiles, mask):
@@ -279,6 +294,33 @@
     return stacks
 
 
+def add_col_taps(acc_ref, grads, g, hidden, h, d, rows):
+    acc = acc_ref[...]
+    for r in rows:
+        for at in MAIN:
+            left = jnp.concatenate([hidden[r + h + q * d, :, at] for q in (0, 1)], axis=0)
+            right = jnp.concatenate([grads[r + g + q * d, :, at] for q in (-1, 0, 1, 2)], axis=0)
+            acc += dot_nt(left, right)
+    acc_ref[...] = acc
+
+
+def add_col_taps_single(acc_ref, grads, g, hidden, h, d, rows):
+    acc = acc_ref[0:C, 0 : 3 * C]
+    for r in rows:
+        for at in MAIN:
+            right = jnp.concatenate([grads[r + g + q * d, :, at] for q in (-1, 0, 1)], axis=0)
+            acc += dot_nt(hidden[r + h, :, at], right)
+    acc_ref[0:C, 0 : 3 * C] = acc
+
+
+def add_row_taps(acc_ref, values, stacks):
+    acc = acc_ref[...]
+    for value, stack in zip(values, stacks):
+        for at in MAIN:
+            acc += dot_nt(value[:, at], stack[:, at])
+    acc_ref[...] = acc
+
+
 def elu(p):
     return jnp.where(p > 0, p, jnp.exp(p) - 1.0)
 
@@ -290,14 +332,14 @@
             out[:, i * 16 : (i + 1) * 16, at] = turn(src[i * 16 : (i + 1) * 16, :, at])
 
 
-def call(kernel, name, in_specs, outs, scratch, cost, *args):
+def call(kernel, name, in_specs, outs, scratch, cost, vmem, *args):
     return pl.pallas_call(
         kernel,
         in_specs=in_specs,
         out_specs=[spec for spec, _, _ in outs],
         out_shape=[jax.ShapeDtypeStruct(shape, dtype) for _, shape, dtype in outs],
         scratch_shapes=scratch,
-        compiler_params=pltpu.CompilerParams(vmem_limit_bytes=VMEM_LIMIT),
+        compiler_params=pltpu.CompilerParams(vmem_limit_bytes=vmem * MIB),
         cost_estimate=pl.CostEstimate(flops=cost * 500_000_000, bytes_accessed=cost * 1_000_000, transcendentals=0),
         name=name,
     )(*args)
@@ -307,22 +349,25 @@
 
 
 def inner_kernel(
-    tiles, x, left, right, wr, wc,
-    x_out, h1_out, b1_out, h2_out, up_out, down_out,
-    xe, h1, b1, h2, mask, sems,
+    tiles, x, c, left, right, wr, wc,
+    x_out, h1_out, b1_out, h2_out, c_out, a2_out, cg1_out, g1_out, col_acc, row_acc,
+    xe, h1, b1, h2, ce, cm, a2, cg1, g1, mask, sems,
 ):
     d1, d2 = FIRST_SPACING, SECOND_SPACING
     load = pltpu.make_async_copy(x, xe.at[:, :, 0:W], sems.at[0])
     load.start()
+    load_c = pltpu.make_async_copy(c, ce.at[:, :, 0:W], sems.at[6])
+    load_c.start()
     build_mask(tiles, mask)
-    per = 128 // XEDGE
-
-    def edges(g, _):
-        for k in range(per):
-            xe[g * per + k, :, TAIL] = unpack(left[g], right[g], k, XEDGE)
-        return 0
-
-    lax.fori_loop(0, XTILES, edges, 0)
+    for dst, width, first, count in ((xe, XEDGE, 0, XTILES), (ce, CEDGE, XTILES, CTILES)):
+        per = 128 // width
+
+        def edges(g, _):
+            for k in range(per):
+                dst[g * per + k, :, TAIL] = unpack(left[first + g], right[first + g], k, width)
+            return 0
+
+        lax.fori_loop(0, count, edges, 0)
     wr1, wr2 = forward_matrix(wr[0]), forward_matrix(wr[1])
     wc1 = two_rows(forward_matrix(wc[0]))
     load.wait()
@@ -361,197 +406,214 @@
 
     loop(INNER, 12, hidden_two)
     saves.append(pltpu.make_async_copy(h2, h2_out, sems.at[5]))
-    saves.append(pltpu.make_async_copy(h2.at[0 : d2 - d1, :, 0:W], up_out, sems.at[6]))
-    saves.append(pltpu.make_async_copy(h2.at[INNER - (d2 - d1) : INNER, :, 0:W], down_out, sems.at[7]))
-    for save in saves[-3:]:
+    saves[-1].start()
+
+    wr2b = backward_matrix(wr[1])
+    wc2b = two_rows(backward_matrix(wc[1], (2, 1, 0)))
+    col_acc[...] = jnp.zeros_like(col_acc)
+    row_acc[...] = jnp.zeros_like(row_acc)
+    load_c.wait()
+    saves.append(pltpu.make_async_copy(ce, c_out, sems.at[7]))
+    saves[-1].start()
+
+    def mask_cot(r):
+        for q in range(4):
+            cm[r + q] = masked(ce[r + q], mask, r + q, slice(0, E))
+
+    loop(R, 4, mask_cot)
+
+    def post_two(row, at, hid):
+        slope = 1.0 + jnp.minimum(h2[row - d1, :, at], 0).astype(F32)
+        a2[row - d2, :, at] = masked((hid * slope).astype(BF16), mask, row, at)
+
+    rows = [d2 + q for q in range(d2)]
+    conv_columns(cm, rows, d2, wc2b, post_two)
+    add_col_taps(col_acc, cm, 0, h2, -d1, d2, rows)
+
+    def post_one(row, at, mixed):
+        g = ce[row + d2, :, at].astype(F32) + mixed
+        cg1[row, :, at] = masked(g.astype(BF16), mask, row + d2, at)
+        if at != TAIL:
+            g1[row, :, at] = g
+
+    rows = list(range(MIDDLE))
+    stacks = conv_rows(a2, rows, d2, True, wr2b, post_one)
+    add_row_taps(row_acc, [b1[r + d2 - d1, :, 0:W] for r in rows], stacks)
+    late = [
+        pltpu.make_async_copy(a2, a2_out, sems.at[8]),
+        pltpu.make_async_copy(cg1, cg1_out, sems.at[9]),
+        pltpu.make_async_copy(g1, g1_out, sems.at[10]),
+    ]
+    for save in late:
         save.start()
-    for save in saves:
+    for save in saves + late:
         save.wait()
 
 
+MIDDLE = R - 2 * SECOND_SPACING
+
+
 def forward_inner(*args):
-    d1, d2 = FIRST_SPACING, SECOND_SPACING
+    d1 = FIRST_SPACING
     return call(
-        inner_kernel, "forward_inner", [SM, ANY, VM, VM, VM, VM],
+        inner_kernel, "forward_inner", [SM, ANY, ANY, VM, VM, VM, VM],
         [
             (ANY, (2, 2 * d1, C, E), BF16),
             (ANY, (R, C, E), BF16),
             (ANY, (INNER, C, E), BF16),
             (ANY, (INNER, C, E), BF16),
-            (ANY, (d2 - d1, C, W), BF16),
-            (ANY, (d2 - d1, C, W), BF16),
+            (ANY, (R, C, E), BF16),
+            (ANY, (MIDDLE, C, E), BF16),
+            (ANY, (MIDDLE, C, E), BF16),
+            (ANY, (MIDDLE, C, W), F32),
+            (VM, (2 * C, 4 * C), F32),
+            (VM, (C, 3 * C), F32),
         ],
         [
             pltpu.VMEM((R, C, E), BF16),
             pltpu.VMEM((R, C, E), BF16),
             pltpu.VMEM((INNER, C, E), BF16),
             pltpu.VMEM((INNER, C, E), BF16),
+            pltpu.VMEM((R, C, E), BF16),
+            pltpu.VMEM((R, C, E), BF16),
+            pltpu.VMEM((MIDDLE, C, E), BF16),
+            pltpu.VMEM((MIDDLE, C, E), BF16),
+            pltpu.VMEM((MIDDLE, C, W), F32),
             pltpu.VMEM((3, 16, E), BF16),
-            pltpu.SemaphoreType.DMA((8,)),
+            pltpu.SemaphoreType.DMA((11,)),
         ],
-        10, *args,
+        14, VM_INNER, *args,
     )
 
 
+OUTER = HALO
+
+
 def outer_kernel(
-    tiles, above, below, x_in, h1_in, wr, wc,
-    b1_out, h2_out,
-    x, h1, b1, h2, mask, sems,
+    tiles, above, below, x_in, h1_in, b1_in, h2_in, wr, wc,
+    out, b1_out, h2_out,
+    x, h1, b1s, h2s, b1, h2, packed, flat, mask, sems,
 ):
     d1, d2 = FIRST_SPACING, SECOND_SPACING
-    n = 2 * d1
-    loads = [
-        pltpu.make_async_copy(above.at[0:XHALO], x.at[0, 0:n, :, 0:W], sems.at[0]),
-        pltpu.make_async_copy(below.at[0:XHALO], x.at[1, n : 2 * n, :, 0:W], sems.at[1]),
-        pltpu.make_async_copy(x_in.at[0], x.at[0, n : 2 * n], sems.at[2]),
-        pltpu.make_async_copy(x_in.at[1], x.at[1, 0:n], sems.at[3]),
-        pltpu.make_async_copy(h1_in.at[0:n], h1.at[0, n : 2 * n], sems.at[4]),
-        pltpu.make_async_copy(h1_in.at[R - n : R], h1.at[1, 0:n], sems.at[5]),
-    ]
-    edge_rows = pltpu.VMEM((2, C, W), BF16)
-    for load in loads:
-        load.start()
+    n, own = 2 * d1, slice(0, W)
+    size = HALO + n
+    halo_at, own_at = (slice(0, HALO), slice(n, size)), (slice(HALO, size), slice(0, n))
+    first_row = (-HALO, R - n)
+    loads = []
+
+    def load(src, dst):
+        loads.append(pltpu.make_async_copy(src, dst, sems.at[len(loads)]))
+        loads[-1].start()
+
+    for side, src in enumerate((above, below)):
+        load(src.at[2 * HALO : XROWS], packed.at[side])
+        load(src.at[0:HALO], x.at[side, halo_at[side], :, MAIN[0]])
+        load(src.at[HALO : 2 * HALO], x.at[side, halo_at[side], :, MAIN[1]])
+        load(x_in.at[side], x.at[side, own_at[side]])
+        load(h1_in.at[side * (R - n) : side * (R - n) + n], h1.at[side, own_at[side]])
+    load(b1_in.at[:, :, own], b1.at[d1 : R - d1])
+    load(h2_in.at[:, :, own], h2.at[OUTER : OUTER + INNER])
     build_mask(tiles, mask)
-
-    def with_edges(packed, sem):
-        gets = [
-            pltpu.make_async_copy(above.at[XHALO], packed.at[0], sem.at[0]),
-            pltpu.make_async_copy(below.at[XHALO], packed.at[1], sem.at[1]),
-        ]
-        for get in gets:
-            get.start()
-        for get in gets:
-            get.wait()
-        per = 128 // XEDGE
-        for side in range(2):
-            tile = [packed[side, :, t * 128 : (t + 1) * 128] for t in range(4)]
-            for q in range(XHALO):
-                x[side, side * n + q, :, TAIL] = unpack(tile[q // per], tile[2 + q // per], q % per, XEDGE)
-
-    pl.run_scoped(with_edges, edge_rows, pltpu.SemaphoreType.DMA((2,)))
     wr1, wr2 = forward_matrix(wr[0]), forward_matrix(wr[1])
-    wc1 = two_rows(forward_matrix(wc[0]))
-    for load in loads:
-        load.wait()
-
+    wc1s = forward_matrix(wc[0])
+    wc1, wc2 = two_rows(wc1s), two_rows(forward_matrix(wc[1]))
+    for copy in loads:
+        copy.wait()
+    per = 128 // XEDGE
     for side in range(2):
-        first = side * R - n
+        tile = [packed[side, k // 2, :, (k % 2) * 128 : (k % 2 + 1) * 128] for k in range(6)]
+        for q in range(HALO):
+            x[side, halo_at[side].start + q, :, TAIL] = unpack(tile[q // per], tile[3 + q // per], q % per, XEDGE)
+
+    for side in range(2):
 
         def post_h1(row, at, pre):
-            h1[side, row, :, at] = masked(elu(pre).astype(BF16), mask, row + first, at)
-
-        conv_rows(x.at[side], [side * n + q for q in range(n)], d1, False, wr1, post_h1)
+            h1[side, row, :, at] = masked(elu(pre).astype(BF16), mask, row + first_row[side], at)
+
+        conv_rows(x.at[side], [halo_at[side].start + q for q in range(HALO)], d1, False, wr1, post_h1)
     for side in range(2):
-        first = side * R - n
 
         def post_b1(row, at, col):
-            kept = masked(col.astype(BF16), mask, row + first, at)
-            b1[side, row - d1, :, at] = x[side, row, :, at] + kept
+            kept = masked(col.astype(BF16), mask, row + first_row[side], at)
+            b1s[side, row - d1, :, at] = x[side, row, :, at] + kept
 
         conv_columns(h1.at[side], [d1 + q for q in range(d1)], d1, wc1, post_b1)
+        conv_columns_single(h1.at[side], [3 * d1 + q for q in range(d1)], d1, wc1s, post_b1)
+    saves = [pltpu.make_async_copy(b1s, b1_out, sems.at[len(loads)])]
+    saves[0].start()
     for side in range(2):
-        first = side * R - d1
 
         def post_h2(row, at, pre):
-            h2[side, row, :, at] = masked(elu(pre).astype(BF16), mask, row + first, at)
-
-        conv_rows(b1.at[side], [q for q in range(n)], d2, False, wr2, post_h2)
-    saves = [pltpu.make_async_copy(b1, b1_out, sems.at[6]), pltpu.make_async_copy(h2, h2_out, sems.at[7])]
-    for save in saves:
-        save.start()
+            h2s[side, row, :, at] = masked(elu(pre).astype(BF16), mask, row + first_row[side] + d1, at)
+
+        conv_rows(b1s.at[side], list(range(OUTER)), d2, False, wr2, post_h2)
+    saves.append(pltpu.make_async_copy(h2s, h2_out, sems.at[len(loads) + 1]))
+    saves[1].start()
+    h2[0:OUTER] = h2s[0, :, :, own]
+    h2[OUTER + INNER : 2 * OUTER + INNER] = h2s[1, :, :, own]
+    b1[0:d1] = b1s[0, d2:OUTER, :, own]
+    b1[R - d1 : R] = b1s[1, 0:d1, :, own]
+
+    def last(i):
+        r = (i // d2) * 2 * d2 + i % d2
+
+        def post(row, at, col):
+            flat[row - d2, :, at] = b1[row - d2, :, at] + masked(col.astype(BF16), mask, row - d2, at)
+
+        conv_columns(h2, [r + d2 + q for q in range(4)], d2, wc2, post, tail=False)
+
+    loop(R // 2, 4, last)
+    turn_out(flat, out)
     for save in saves:
         save.wait()
 
 
 def forward_outer(*args):
-    n = 2 * FIRST_SPACING
+    size = HALO + 2 * FIRST_SPACING
     return call(
-        outer_kernel, "forward_outer", [SM, ANY, ANY, ANY, ANY, VM, VM],
-        [(ANY, (2, n, C, E), BF16), (ANY, (2, n, C, E), BF16)],
+        outer_kernel, "forward_outer", [SM, VM, VM] + [ANY] * 4 + [VM, VM],
+        [(VM, (C, R, W), BF16), (ANY, (2, OUTER, C, E), BF16), (ANY, (2, OUTER, C, E), BF16)],
         [
-            pltpu.VMEM((2, 2 * n, C, E), BF16),
-            pltpu.VMEM((2, 2 * n, C, E), BF16),
-            pltpu.VMEM((2, n, C, E), BF16),
-            pltpu.VMEM((2, n, C, E), BF16),
-            pltpu.VMEM((3, 16, E), BF16),
-            pltpu.SemaphoreType.DMA((8,)),
-        ],
-        7, *args,
-    )
-
-
-def final_kernel(
-    tiles, above, below, b1_in, b1_side, h2_in, h2_side, wc,
-    out,
-    b1, h2, flat, mask, sems,
-):
-    d1, d2 = FIRST_SPACING, SECOND_SPACING
-    n, far, own = 2 * d1, d2 - d1, slice(0, W)
-    loads = [
-        pltpu.make_async_copy(above, h2.at[0:far], sems.at[0]),
-        pltpu.make_async_copy(h2_side.at[0, :, :, own], h2.at[far : far + n], sems.at[1]),
-        pltpu.make_async_copy(h2_in.at[:, :, own], h2.at[far + n : far + n + INNER], sems.at[2]),
-        pltpu.make_async_copy(h2_side.at[1, :, :, own], h2.at[far + n + INNER : R + 2 * d2 - far], sems.at[3]),
-        pltpu.make_async_copy(below, h2.at[R + 2 * d2 - far : R + 2 * d2], sems.at[4]),
-        pltpu.make_async_copy(b1_side.at[0, d1:n, :, own], b1.at[0:d1], sems.at[5]),
-        pltpu.make_async_copy(b1_in.at[:, :, own], b1.at[d1 : R - d1], sems.at[6]),
-        pltpu.make_async_copy(b1_side.at[1, 0:d1, :, own], b1.at[R - d1 : R], sems.at[7]),
-    ]
-    for load in loads:
-        load.start()
-    build_mask(tiles, mask)
-    wc2 = two_rows(forward_matrix(wc[1]))
-    for load in loads:
-        load.wait()
-
-    def last(i):
-        r = (i // d2) * 2 * d2 + i % d2
-
-        def post(row, at, col):
-            flat[row - d2, :, at] = b1[row - d2, :, at] + masked(col.astype(BF16), mask, row - d2, at)
-
-        conv_columns(h2, [r + d2 + q for q in range(4)], d2, wc2, post, tail=False)
-
-    loop(R // 2, 4, last)
-    turn_out(flat, out)
-
-
-def forward_final(*args):
-    return call(
-        final_kernel, "forward_final", [SM, ANY, ANY, ANY, ANY, ANY, ANY, VM],
-        [(VM, (C, R, W), BF16)],
-        [
+            pltpu.VMEM((2, size, C, E), BF16),
+            pltpu.VMEM((2, size, C, E), BF16),
+            pltpu.VMEM((2, OUTER, C, E), BF16),
+            pltpu.VMEM((2, OUTER, C, E), BF16),
             pltpu.VMEM((R, C, W), BF16),
             pltpu.VMEM((R + 2 * SECOND_SPACING, C, W), BF16),
+            pltpu.VMEM((2, 3, C, W // 2), BF16),
             pltpu.VMEM((R, C, W), BF16),
             pltpu.VMEM((3, 16, E), BF16),
-            pltpu.SemaphoreType.DMA((8,)),
+            pltpu.SemaphoreType.DMA((14,)),
         ],
-        4, *args,
-    )[0]
+        14, VM_OUTER, *args,
+    )
 
 
 def backward_kernel(
-    tiles, c, above, below, left, right, wr, wc, x_in, h1_in, b1_in, b1_side, h2_in, h2_side,
+    tiles, above, below, wr, wc, c, a2_in, cg1_in, g1_in, col_in, row_in,
+    x_in, h1_in, b1_in, b1_side, h2_in, h2_side,
     taps, a1_out, g1_out,
     packed, ce, cm, h1, b1, h2, x, a2, cg1, g1, a1, col_acc, row_acc, mask, sems,
 ):
     d1, d2 = FIRST_SPACING, SECOND_SPACING
     n = 2 * d1
     loads = [
-        pltpu.make_async_copy(c, ce.at[HALO : HALO + R, :, 0:W], sems.at[0]),
+        pltpu.make_async_copy(c, ce.at[HALO : HALO + R], sems.at[0]),
         pltpu.make_async_copy(above.at[0:HALO], ce.at[0:HALO, :, 0:W], sems.at[1]),
         pltpu.make_async_copy(below.at[0:HALO], ce.at[HALO + R :, :, 0:W], sems.at[2]),
         pltpu.make_async_copy(above.at[HALO], packed.at[0], sems.at[7]),
         pltpu.make_async_copy(below.at[HALO], packed.at[1], sems.at[8]),
     ]
     late = [
-        pltpu.make_async_copy(h2_side.at[0], h2.at[0:n], sems.at[3]),
+        pltpu.make_async_copy(h2_side.at[0, OUTER - n : OUTER], h2.at[0:n], sems.at[3]),
         pltpu.make_async_copy(h2_in, h2.at[n : n + INNER], sems.at[9]),
-        pltpu.make_async_copy(h2_side.at[1], h2.at[n + INNER : R + n], sems.at[10]),
-        pltpu.make_async_copy(b1_side.at[0, d1:n], b1.at[0:d1], sems.at[4]),
+        pltpu.make_async_copy(h2_side.at[1, 0:n], h2.at[n + INNER : R + n], sems.at[10]),
+        pltpu.make_async_copy(b1_side.at[0, d2:OUTER], b1.at[0:d1], sems.at[4]),
         pltpu.make_async_copy(b1_in, b1.at[d1 : R - d1], sems.at[11]),
         pltpu.make_async_copy(b1_side.at[1, 0:d1], b1.at[R - d1 : R], sems.at[12]),
+        pltpu.make_async_copy(a2_in, a2.at[d1 + d2 : d1 + d2 + MIDDLE], sems.at[15]),
+        pltpu.make_async_copy(cg1_in, cg1.at[d1 + d2 : d1 + d2 + MIDDLE], sems.at[16]),
+        pltpu.make_async_copy(g1_in, g1.at[d1 + d2 : d1 + d2 + MIDDLE], sems.at[17]),
         pltpu.make_async_copy(h1_in, h1, sems.at[5]),
         pltpu.make_async_copy(x_in, x, sems.at[6]),
     ]
@@ -560,12 +622,6 @@
     build_mask(tiles, mask)
     per = 128 // CEDGE
 
-    def edges(g, _):
-        for k in range(per):
-            ce[HALO + g * per + k, :, TAIL] = unpack(left[XTILES + g], right[XTILES + g], k, CEDGE)
-        return 0
-
-    lax.fori_loop(0, CTILES, edges, 0)
     wr1, wr2 = backward_matrix(wr[0]), backward_matrix(wr[1])
     wc1, wc2 = backward_matrix(wc[0], (2, 1, 0)), backward_matrix(wc[1], (2, 1, 0))
     wc1w, wc2w = two_rows(wc1), two_rows(wc2)
@@ -591,39 +647,17 @@
         slope = 1.0 + jnp.minimum(h2[row - up, :, at], 0).astype(F32)
         a2[row - up, :, at] = masked((hid * slope).astype(BF16), mask, row - HALO, at)
 
-    def act_two(i):
-        r = (i // d2) * 2 * d2 + i % d2
-        conv_columns(cm, [r + up + q for q in range(4)], d2, wc2w, post_two)
-
-    loop(R // 2, 4, act_two)
-    conv_columns_single(cm, [R + up + q for q in range(2 * d1)], d2, wc2, post_two)
-    for load in late[3:6]:
+    for first in (0, d2 + MIDDLE + d1):
+        conv_columns(cm, [first + up + q for q in range(d1)], d2, wc2w, post_two)
+        conv_columns_single(cm, [first + up + d1 + q for q in range(d1)], d2, wc2, post_two)
+    col_acc[0] = col_in[...]
+    row_acc[0] = row_in[...]
+    col_acc[1] = jnp.zeros_like(col_in)
+    row_acc[1] = jnp.zeros_like(row_in)
+    edge_rows = [*range(d2), *range(R - d2, R)]
+    add_col_taps_single(col_acc.at[0], cm, HALO, h2, d1, d2, edge_rows)
+    for load in late[3:9]:
         load.wait()
-
-    col_acc[...] = jnp.zeros_like(col_acc)
-    row_acc[...] = jnp.zeros_like(row_acc)
-
-    def add_col_taps(k, grads, g, hidden, h, d, rows):
-        acc = col_acc[k]
-        for r in rows:
-            for at in MAIN:
-                left = jnp.concatenate([hidden[r + h + q * d, :, at] for q in (0, 1)], axis=0)
-                right = jnp.concatenate([grads[r + g + q * d, :, at] for q in (-1, 0, 1, 2)], axis=0)
-                acc += dot_nt(left, right)
-        col_acc[k] = acc
-
-    def add_row_taps(k, values, stacks):
-        acc = row_acc[k]
-        for value, stack in zip(values, stacks):
-            for at in MAIN:
-                acc += dot_nt(value[:, at], stack[:, at])
-        row_acc[k] = acc
-
-    def col_taps_two(i):
-        r = (i // d2) * 2 * d2 + i % d2
-        add_col_taps(0, cm, HALO, h2, d1, d2, [r + q for q in range(4)])
-
-    loop(R // 2, 4, col_taps_two)
 
     def post_one(row, at, mixed):
         g = ce[row + up, :, at].astype(F32) + mixed
@@ -631,17 +665,13 @@
         if at != TAIL:
             g1[row, :, at] = g
 
-    def grad_one(r):
-        rows = [r + q + d1 for q in range(STEP)]
-        stacks = conv_rows(a2, rows, d2, True, wr2, post_one)
-        add_row_taps(0, [b1[s - d1] for s in rows], stacks)
-
-    for first in (0, R + d1):
-        conv_rows(a2, [first + q for q in range(d1)], d2, True, wr2, post_one)
-    loop(R, STEP, grad_one)
+    rows = [*range(d1 + d2), *range(d1 + d2 + MIDDLE, 2 * d1 + R)]
+    stacks = conv_rows(a2, rows, d2, True, wr2, post_one)
+    pairs = [(b1[r - d1], stack) for r, stack in zip(rows, stacks) if d1 <= r < R + d1]
+    add_row_taps(row_acc.at[0], [p[0] for p in pairs], [p[1] for p in pairs])
     save_g1 = pltpu.make_async_copy(g1.at[d1 : R + d1], g1_out, sems.at[13])
     save_g1.start()
-    for load in late[6:8]:
+    for load in late[9:11]:
         load.wait()
 
     def act_one(r):
@@ -649,20 +679,20 @@
             slope = 1.0 + jnp.minimum(h1[row - d1, :, at], 0).astype(F32)
             a1[row - d1, :, at] = masked((hid * slope).astype(BF16), mask, row - d1, at)
 
-        rows = [r + q for q in range(2 * d1)]
-        conv_columns(cg1, [s + d1 for s in rows[:d1]], d1, wc1w, post)
-        add_col_taps(1, cg1, d1, h1, 0, d1, rows[:d1])
-
-    loop(R, 2 * d1, act_one)
+        rows = [r + q for q in (*range(d1), *range(2 * d1, 3 * d1))]
+        conv_columns(cg1, [s + d1 for s in rows], d1, wc1w, post)
+        add_col_taps(col_acc.at[1], cg1, d1, h1, 0, d1, rows)
+
+    loop(R, 4 * d1, act_one)
 
     save_a1 = pltpu.make_async_copy(a1, a1_out, sems.at[14])
     save_a1.start()
 
     def last(r):
-        rows = [r + q for q in range(STEP)]
-        add_row_taps(1, [x[s] for s in rows], [row_stack(a1[s], d1, True) for s in rows])
-
-    loop(R, STEP, last)
+        rows = [r + q for q in range(LONG)]
+        add_row_taps(row_acc.at[1], [x[s] for s in rows], [row_stack(a1[s], d1, True) for s in rows])
+
+    loop(R, LONG, last)
     save_a1.wait()
     save_g1.wait()
     for k in range(2):
@@ -681,7 +711,7 @@
 def backward(*args):
     n = 2 * FIRST_SPACING
     return call(
-        backward_kernel, "backward", [SM, ANY, ANY, ANY, VM, VM, VM, VM] + [ANY] * 6,
+        backward_kernel, "backward", [SM, VM, VM, VM, VM] + [ANY] * 4 + [VM, VM] + [ANY] * 6,
         [(VM, (PIECES, PIECE, 2 * C), F32), (ANY, (R, C, E), BF16), (ANY, (R, C, W), F32)],
         [
             pltpu.VMEM((2, C, W), BF16),
@@ -698,9 +728,9 @@
             pltpu.VMEM((2, 2 * C, 4 * C), F32),
             pltpu.VMEM((2, C, 3 * C), F32),
             pltpu.VMEM((3, 16, E), BF16),
-            pltpu.SemaphoreType.DMA((15,)),
+            pltpu.SemaphoreType.DMA((18,)),
         ],
-        25, *args,
+        20, VM_BACK, *args,
     )
 
 
@@ -738,7 +768,7 @@
             pltpu.VMEM((R, C, W), BF16),
             pltpu.SemaphoreType.DMA((4,)),
         ],
-        4, *args,
+        4, 24, *args,
     )[0]
 
 
@@ -754,6 +784,14 @@
 COLS = ("y_hi", "core")
 
 
+def in_hbm(array):
+    return pltpu.with_memory_space_constraint(array, pltpu.HBM)
+
+
+def in_vmem(array):
+    return pltpu.with_memory_space_constraint(array, pltpu.VMEM)
+
+
 def on_device(x, tile_mask, wr, wc, cot):
     n_rows, n_cols = lax.axis_size("rows"), lax.axis_size(COLS)
     factor = 1.0 / math.sqrt(R * n_rows * W * n_cols)
@@ -763,24 +801,24 @@
     left = [(i + 1, i) for i in range(n_cols - 1)]
 
     to_left, to_right = pack_edges(x, cot)
-    from_right = lax.ppermute(to_left, COLS, left)
-    from_left = lax.ppermute(to_right, COLS, right)
+    from_right = in_vmem(lax.ppermute(to_left, COLS, left))
+    from_left = in_vmem(lax.ppermute(to_right, COLS, right))
     xt, x_up, x_down, ct, c_up, c_down = turn_both(x, cot)
     x_up, x_down, c_up, c_down = fill((x_up, x_down, c_up, c_down), from_left, from_right)
-    x_above = lax.ppermute(x_down, "rows", down)
-    x_below = lax.ppermute(x_up, "rows", up)
-    c_above = lax.ppermute(c_down, "rows", down)
-    c_below = lax.ppermute(c_up, "rows", up)
-
-    x_side, h1, b1, h2, h2_up, h2_down = forward_inner(tile_mask, xt, from_left, from_right, wr, wc)
-    h2_above = lax.ppermute(h2_down, "rows", down)
-    h2_below = lax.ppermute(h2_up, "rows", up)
-    b1_side, h2_side = forward_outer(tile_mask, x_above, x_below, x_side, h1, wr, wc)
+    x_above = in_vmem(lax.ppermute(x_down, "rows", down))
+    x_below = in_vmem(lax.ppermute(x_up, "rows", up))
+    c_above = in_vmem(lax.ppermute(c_down, "rows", down))
+    c_below = in_vmem(lax.ppermute(c_up, "rows", up))
+
+    x_side, h1, b1, h2, ce, a2, cg1, g1, col_taps, row_taps = forward_inner(
+        tile_mask, xt, ct, from_left, from_right, wr, wc
+    )
+    final, b1_side, h2_side = forward_outer(tile_mask, x_above, x_below, x_side, h1, b1, h2, wr, wc)
     taps, a1, g1 = backward(
-        tile_mask, ct, c_above, c_below, from_left, from_right, wr, wc, xt, h1, b1, b1_side, h2, h2_side
+        tile_mask, c_above, c_below, wr, wc, ce, a2, cg1, g1, col_taps, row_taps,
+        xt, h1, b1, b1_side, h2, h2_side,
     )
-    taps, h2_above, h2_below = lax.optimization_barrier((taps, h2_above, h2_below))
-    final = forward_final(tile_mask, h2_above, h2_below, b1, b1_side, h2, h2_side, wc)
+    a1, g1 = in_hbm(a1), in_hbm(g1)
     total, map_grad = tap_sum(taps, backward_map(a1, g1, wr))
     total = total[::-1] * factor
     return final, map_grad, total[..., C:], total[..., :C]

time: 126 us -> 120 us (0.952)
  starting transfers between devices: 38.8 us -> 24.9 us
  blocking collectives: 10.4 us -> 23.8 us
  Pallas kernels: 63.4 us -> 54.8 us
  waiting for transfers between devices: 6.62 us -> 10.5 us
    all_to_all x0 -> x1, blocking collectives: none -> 14.5 us  [tap_sum(): whole = lax.all_to_all(spread, 'rows', 0, 0, tiled=True)]
    all_to_all x1 -> x0, starting transfers between devices: 5.91 us -> none  [tap_sum(): whole = lax.all_to_all(spread, 'rows', 0, 0, tiled=True)]
    ppermute x8 -> x6, starting transfers between devices: 20 us -> 14.2 us  [the longest x1 4.6 us: on_device(): c_above = in_vmem(lax.ppermute(c_down, 'rows', down))]
    ppermute x8 -> x6, waiting for transfers between devices: 1.92 us -> 7.68 us  [the longest x1 4.49 us: on_device(): c_below = in_vmem(lax.ppermute(c_up, 'rows', up))]
    pallas_call x5 -> x4, Pallas kernels: 51.4 us -> 46.1 us  [call(): pl.pallas_call(kernel, in_specs=in_specs, out_specs=[spec for spec, _, _...]
    all_to_all x1 -> x0, waiting for transfers between devices: 3 us -> none  [tap_sum(): whole = lax.all_to_all(spread, 'rows', 0, 0, tiled=True)]
    pallas_call x1, Pallas kernels: 4.08 us -> 1.63 us  [pack_edges(): pl.pallas_call(edge_kernel, grid=(C // GC,), in_specs=[low, high, low, hi...]
    all_to_all x1, starting transfers between devices: 12.9 us -> 10.7 us  [tap_sum(): part = lax.all_to_all(taps, 'rows', 0, 0, tiled=True)]
  transfers between devices with their start and end apart: 10 -> 7, of which waited for: 3 -> 4; matrix products, arithmetic and copies ran while one was open for 0% -> 0% of each run, Pallas kernels for 46% -> 32%
where the time goes in v4:
time: 120 us; the launch traced here: 119 us
  Pallas kernels  54.8 us (46%)
  starting transfers between devices  24.9 us (21%)
  blocking collectives  23.8 us (20%)
  waiting for transfers between devices  10.5 us (9%)
  local copies, waits for them, and re-layouts  4.02 us (3%)
    pallas_call x4, Pallas kernels, call(): pl.pallas_call(kernel, in_specs=in_specs, out_specs=[spec for spec, _, _...  46.1 us
    all_to_all x1, blocking collectives, tap_sum(): whole = lax.all_to_all(spread, 'rows', 0, 0, tiled=True)  14.5 us
    all_to_all x1, starting transfers between devices, tap_sum(): part = lax.all_to_all(taps, 'rows', 0, 0, tiled=True)  10.7 us
    all_gather x1, blocking collectives, tap_sum(): part = lax.all_gather(part.sum(0), COLS).sum(0)  9.28 us
    pallas_call x1, Pallas kernels, turn_both(): pl.pallas_call(turn_kernel, grid=(C // GC,), in_specs=[native, native], o...  6.27 us
    ppermute x1, starting transfers between devices, on_device(): c_above = in_vmem(lax.ppermute(c_down, 'rows', down))  4.6 us
    ppermute x1, waiting for transfers between devices, on_device(): c_below = in_vmem(lax.ppermute(c_up, 'rows', up))  4.49 us
    ppermute x1, starting transfers between devices, on_device(): x_above = in_vmem(lax.ppermute(x_down, 'rows', down))  4.41 us
  transfers between devices with their start and end apart: 7, of which 4 were waited for; matrix products, arithmetic and copies ran while one was open for 0% of the time, Pallas kernels for 32%

profile of v4, /device:TPU:0, one launch (start us, length us, event | category | flops | bytes accessed | tf_op | source)
XLA Modules:
  0.0 118.8 jit_solution(17909430085181247613)
XLA Ops:
  0.6 0.0 copy-start
  0.6 1.6 %copy-done = bf16[64,32,512]{2,1,0:T(8,128)(2,1)S(1)} copy-done((bf16[64,32,512]{2,1,0:T(8,128)(2,1)S(1)}, bf16[64,32,512]{2,1,0:T(8,128)(2,1)}, u32[]{:S(2)}) %copy-start) | copy-done | bytes 2097176
  2.2 0.0 copy-start.1
  2.2 1.6 %copy-done.1 = bf16[64,32,512]{2,1,0:T(8,128)(2,1)S(1)} copy-done((bf16[64,32,512]{2,1,0:T(8,128)(2,1)S(1)}, bf16[64,32,512]{2,1,0:T(8,128)(2,1)}, u32[]{:S(2)}) %copy-start.1) | copy-done | bytes 2097176
  3.8 1.6 %pack_edges.1 = (bf16[12,64,128]{2,1,0:T(8,128)(2,1)S(1)}, bf16[12,64,128]{2,1,0:T(8,128)(2,1)S(1)}) custom-call(bf16[64,32,512]{2,1,0:T(8,128)(2,1)S(1)} %copy-done, bf16[64,32,512]{2,1,0:T(8,128)(2,1)S(1)} %copy-done, bf16[64,32,512]{2,1,0:T(8,128)(2,1)S(1)} %copy-done.1, bf16[64,32,512]{2,1,0:T(8,128)(2,1)S(1)} %copy-done.1), custom_call_target="tpu_custom_call" | custom-call | tf_op jit(solution)/shard_map/pack_edges/pallas_call | solution.py:88
  5.5 1.3 %collective-permute-start = (bf16[12,64,128]{2,1,0:T(8,128)(2,1)S(1)}, bf16[12,64,128]{2,1,0:T(8,128)(2,1)S(1)}, u32[]{:S(2)}, u32[]{:S(2)}) collective-permute-start(bf16[12,64,128]{2,1,0:T(8,128)(2,1)S(1)} %get-tuple-element.38), channel_id=1, source_target_pairs={{0,1},{1,2},{2,3},{4,5},{5,6},{6,7},{8,9},{9,10},{10,11},{12,13},{... | collective-permute-start | bytes 589832 | tf_op jit(solution)/shard_map/ppermute | solution.py:805
  6.8 1.3 %collective-permute-start.1 = (bf16[12,64,128]{2,1,0:T(8,128)(2,1)S(1)}, bf16[12,64,128]{2,1,0:T(8,128)(2,1)S(1)}, u32[]{:S(2)}, u32[]{:S(2)}) collective-permute-start(bf16[12,64,128]{2,1,0:T(8,128)(2,1)S(1)} %get-tuple-element.39), channel_id=1, source_target_pairs={{1,0},{2,1},{3,2},{5,4},{6,5},{7,6},{9,8},{10,9},{11,10},{13,12},{... | collective-permute-start | bytes 589832 | tf_op jit(solution)/shard_map/ppermute | solution.py:804
  8.1 6.3 %turn_both.1 = (bf16[32,64,512]{2,1,0:T(8,128)(2,1)}, bf16[27,64,256]{2,1,0:T(8,128)(2,1)}, bf16[27,64,256]{2,1,0:T(8,128)(2,1)}, bf16[32,64,512]{2,1,0:T(8,128)...) custom-call(bf16[64,32,512]{2,1,0:T(8,128)(2,1)} %x_high.1, bf16[64,32,512]{2,1,0:T(8,128)(2,1)} %c_high.1), custom_call_target="tpu_custom_call" | custom-call | tf_op jit(solution)/shard_map/turn_both/pallas_call | solution.py:132
  14.3 0.0 collective-permute-done.left
  14.3 0.0 collective-permute-done.1.right
  14.3 0.8 fill_messages.1
  15.1 4.4 %collective-permute-start.2 = (bf16[27,64,256]{2,1,0:T(8,128)(2,1)}, bf16[27,64,256]{2,1,0:T(8,128)(2,1)S(1)}, u32[]{:S(2)}, u32[]{:S(2)}) collective-permute-start(bf16[27,64,256]{2,1,0:T(8,128)(2,1)} %get-tuple-element.40), channel_id=1, source_target_pairs={{0,4},{4,8},{8,12},{12,16},{16,20},{20,24},{24,28},{28,32},{32,36}... | collective-permute-start | bytes 2654216 | tf_op jit(solution)/shard_map/ppermute | solution.py:808
  19.6 1.3 %collective-permute-start.3 = (bf16[27,64,256]{2,1,0:T(8,128)(2,1)}, bf16[27,64,256]{2,1,0:T(8,128)(2,1)S(1)}, u32[]{:S(2)}, u32[]{:S(2)}) collective-permute-start(bf16[27,64,256]{2,1,0:T(8,128)(2,1)} %get-tuple-element.41), channel_id=1, source_target_pairs={{4,0},{8,4},{12,8},{16,12},{20,16},{24,20},{28,24},{32,28},{36,32}... | collective-permute-start | bytes 2654216 | tf_op jit(solution)/shard_map/ppermute | solution.py:809
  20.9 4.6 %collective-permute-start.4 = (bf16[13,64,512]{2,1,0:T(8,128)(2,1)}, bf16[13,64,512]{2,1,0:T(8,128)(2,1)S(1)}, u32[]{:S(2)}, u32[]{:S(2)}) collective-permute-start(bf16[13,64,512]{2,1,0:T(8,128)(2,1)} %get-tuple-element.49), channel_id=1, source_target_pairs={{0,4},{4,8},{8,12},{12,16},{16,20},{20,24},{24,28},{28,32},{32,36}... | collective-permute-start | bytes 2555912 | tf_op jit(solution)/shard_map/ppermute | solution.py:810
  25.5 1.3 %collective-permute-start.5 = (bf16[13,64,512]{2,1,0:T(8,128)(2,1)}, bf16[13,64,512]{2,1,0:T(8,128)(2,1)S(1)}, u32[]{:S(2)}, u32[]{:S(2)}) collective-permute-start(bf16[13,64,512]{2,1,0:T(8,128)(2,1)} %get-tuple-element.50), channel_id=1, source_target_pairs={{4,0},{8,4},{12,8},{16,12},{20,16},{24,20},{28,24},{32,28},{36,32}... | collective-permute-start | bytes 2555912 | tf_op jit(solution)/shard_map/ppermute | solution.py:811
  26.8 13.2 %forward_inner.1 = (bf16[2,8,64,640]{3,2,1,0:T(8,128)(2,1)}, bf16[32,64,640]{2,1,0:T(8,128)(2,1)}, bf16[24,64,640]{2,1,0:T(8,128)(2,1)}, bf16[24,64,640]{2,1,0:T...) custom-call(s32[8,16]{1,0:T(8,128)} %tiles.5, ...), custom_call_target="tpu_custom_call" | custom-call | flops 7000000000 | bytes 14000000 | tf_op jit(solution)/shard_map/forward_inner/pallas_call | solution.py:336
  40.0 0.0 collective-permute-done.2.above
  40.0 0.9 collective-permute-done.3.below
  40.9 11.4 %forward_outer.1 = (bf16[64,32,512]{2,1,0:T(8,128)(2,1)}, bf16[2,12,64,640]{3,2,1,0:T(8,128)(2,1)}, bf16[2,12,64,640]{3,2,1,0:T(8,128)(2,1)}) custom-call(s32[8,16]{1,0:T(8,128)} %tiles.5, bf16[27,64,256]{2,1,0:T(8,128)(2,1)S(1)} %collective-permute-done.2.above, bf16[27,64,256]{2,1,0:T(8,128)(2,1)S(1)} %collective-permute-done.3.below, ...), custom_call_target="tpu_custom_call" | custom-call | flops 7000000000 | bytes 14000000 | tf_op jit(solution)/shard_map/forward_outer/pallas_call | solution.py:336
  52.3 2.3 %collective-permute-done.4.above = bf16[13,64,512]{2,1,0:T(8,128)(2,1)S(1)} collective-permute-done((bf16[13,64,512]{2,1,0:T(8,128)(2,1)}, bf16[13,64,512]{2,1,0:T(8,128)(2,1)S(1)}, u32[]{:S(2)}, u32[]{:S(2)}) %collective-permute-start.4) | collective-permute-done | bytes 852000 | tf_op jit(solution)/shard_map/ppermute | solution.py:810
  54.6 4.5 %collective-permute-done.5.below = bf16[13,64,512]{2,1,0:T(8,128)(2,1)S(1)} collective-permute-done((bf16[13,64,512]{2,1,0:T(8,128)(2,1)}, bf16[13,64,512]{2,1,0:T(8,128)(2,1)S(1)}, u32[]{:S(2)}, u32[]{:S(2)}) %collective-permute-start.5) | collective-permute-done | bytes 852000 | tf_op jit(solution)/shard_map/ppermute | solution.py:811
  59.1 0.0 copy-start.2
  59.1 14.9 %backward.1 = (f32[32,12,128]{2,1,0:T(8,128)}, bf16[32,64,640]{2,1,0:T(8,128)(2,1)}, f32[32,64,512]{2,1,0:T(8,128)}) custom-call(s32[8,16]{1,0:T(8,128)} %tiles.5, bf16[13,64,512]{2,1,0:T(8,128)(2,1)S(1)} %collective-permute-done.4.above, bf16[13,64,512]{2,1,0:T(8,128)(2,1)S(1)} %collective-permute-done.5.below, bf16[2,3,64,64]{3,2,1,0:T(8,128)(2,1)} %wr.7, ...), custom_call_target="tpu_custom_call" | custom-call | flops 10000000000 | bytes 20000000 | tf_op jit(solution)/shard_map/backward/pallas_call | solution.py:336
  74.1 10.7 %all-to-all-start = ((f32[32,12,128]{2,1,0:T(8,128)}), f32[32,12,128]{2,1,0:T(8,128)S(1)}, u32[]{:S(2)}, u32[]{:S(2)}) async-start(f32[32,12,128]{2,1,0:T(8,128)} %get-tuple-element.59), calls=%async_computation | async-start | bytes 524288 | tf_op jit(solution)/shard_map/all_to_all | solution.py:776
  84.7 0.0 copy-done.2
  84.7 6.5 %backward_map.1 = bf16[64,32,512]{2,1,0:T(8,128)(2,1)} custom-call(bf16[32,64,640]{2,1,0:T(8,128)(2,1)} %get-tuple-element.60.a1_in, f32[32,64,512]{2,1,0:T(8,128)} %get-tuple-element.61.g1_in, bf16[2,3,64,64]{3,2,1,0:T(8,128)(2,1)S(1)} %copy-done.2), custom_call_target="tpu_custom_call" | custom-call | flops 2000000000 | bytes 4000000 | tf_op jit(solution)/shard_map/backward_map/pallas_call | solution.py:336
  91.3 2.8 %all-to-all-done = f32[32,12,128]{2,1,0:T(8,128)S(1)} async-done(((f32[32,12,128]{2,1,0:T(8,128)}), f32[32,12,128]{2,1,0:T(8,128)S(1)}, u32[]{:S(2)}, u32[]{:S(2)}) %all-to-all-start) | async-done | bytes 196640 | tf_op jit(solution)/shard_map/all_to_all | solution.py:776
  94.1 9.3 %all-gather.1 = f32[4,12,128]{2,1,0:T(8,128)S(1)} all-gather(f32[1,12,128]{2,1,0:T(8,128)S(1)} %bitcast.1), channel_id=2, replica_groups=mesh['rows'=32,'y_hi'=2,'core'=2] {'y_hi','core'}, dimensions={0}, use_global_device_ids=true | all-gather | bytes 30720 | tf_op jit(solution)/shard_map/all_gather | solution.py:778
  103.4 14.5 %all_to_all.10 = f32[32,12,128]{2,1,0:T(8,128)S(1)} all-to-all(f32[32,12,128]{2,1,0:T(8,128)S(1)} %broadcast_in_dim.2), channel_id=1, replica_groups=mesh['rows'=32,'y_hi'=2,'core'=2] {'rows'}, dimensions={0} | all-to-all | bytes 393216 | tf_op jit(solution)/shard_map/all_to_all | solution.py:780
  118.0 0.8 fusion
  (5 shorter events, 0.1 us)
Async XLA Ops:
  0.6 1.6 %copy-start = (bf16[64,32,512]{2,1,0:T(8,128)(2,1)S(1)}, bf16[64,32,512]{2,1,0:T(8,128)(2,1)}, u32[]{:S(2)}) copy-start(bf16[64,32,512]{2,1,0:T(8,128)(2,1)} %x_high.1) | copy-start | bytes 6291460
  2.2 1.6 %copy-start.1 = (bf16[64,32,512]{2,1,0:T(8,128)(2,1)S(1)}, bf16[64,32,512]{2,1,0:T(8,128)(2,1)}, u32[]{:S(2)}) copy-start(bf16[64,32,512]{2,1,0:T(8,128)(2,1)} %c_high.1) | copy-start | bytes 6291460
  5.5 8.9 %collective-permute-start = (bf16[12,64,128]{2,1,0:T(8,128)(2,1)S(1)}, bf16[12,64,128]{2,1,0:T(8,128)(2,1)S(1)}, u32[]{:S(2)}, u32[]{:S(2)}) collective-permute-start(bf16[12,64,128]{2,1,0:T(8,128)(2,1)S(1)} %get-tuple-element.38), channel_id=1, source_target_pairs={{0,1},{1,2},{2,3},{4,5},{5,6},{6,7},{8,9},{9,10},{10,11},{12,13},{... | collective-permute-start | bytes 589832 | tf_op jit(solution)/shard_map/ppermute | solution.py:805
  6.8 7.6 %collective-permute-start.1 = (bf16[12,64,128]{2,1,0:T(8,128)(2,1)S(1)}, bf16[12,64,128]{2,1,0:T(8,128)(2,1)S(1)}, u32[]{:S(2)}, u32[]{:S(2)}) collective-permute-start(bf16[12,64,128]{2,1,0:T(8,128)(2,1)S(1)} %get-tuple-element.39), channel_id=1, source_target_pairs={{1,0},{2,1},{3,2},{5,4},{6,5},{7,6},{9,8},{10,9},{11,10},{13,12},{... | collective-permute-start | bytes 589832 | tf_op jit(solution)/shard_map/ppermute | solution.py:804
  15.1 24.9 %collective-permute-start.2 = (bf16[27,64,256]{2,1,0:T(8,128)(2,1)}, bf16[27,64,256]{2,1,0:T(8,128)(2,1)S(1)}, u32[]{:S(2)}, u32[]{:S(2)}) collective-permute-start(bf16[27,64,256]{2,1,0:T(8,128)(2,1)} %get-tuple-element.40), channel_id=1, source_target_pairs={{0,4},{4,8},{8,12},{12,16},{16,20},{20,24},{24,28},{28,32},{32,36}... | collective-permute-start | bytes 2654216 | tf_op jit(solution)/shard_map/ppermute | solution.py:808
  19.6 21.3 %collective-permute-start.3 = (bf16[27,64,256]{2,1,0:T(8,128)(2,1)}, bf16[27,64,256]{2,1,0:T(8,128)(2,1)S(1)}, u32[]{:S(2)}, u32[]{:S(2)}) collective-permute-start(bf16[27,64,256]{2,1,0:T(8,128)(2,1)} %get-tuple-element.41), channel_id=1, source_target_pairs={{4,0},{8,4},{12,8},{16,12},{20,16},{24,20},{28,24},{32,28},{36,32}... | collective-permute-start | bytes 2654216 | tf_op jit(solution)/shard_map/ppermute | solution.py:809
  20.9 33.8 %collective-permute-start.4 = (bf16[13,64,512]{2,1,0:T(8,128)(2,1)}, bf16[13,64,512]{2,1,0:T(8,128)(2,1)S(1)}, u32[]{:S(2)}, u32[]{:S(2)}) collective-permute-start(bf16[13,64,512]{2,1,0:T(8,128)(2,1)} %get-tuple-element.49), channel_id=1, source_target_pairs={{0,4},{4,8},{8,12},{12,16},{16,20},{20,24},{24,28},{28,32},{32,36}... | collective-permute-start | bytes 2555912 | tf_op jit(solution)/shard_map/ppermute | solution.py:810
  25.5 33.7 %collective-permute-start.5 = (bf16[13,64,512]{2,1,0:T(8,128)(2,1)}, bf16[13,64,512]{2,1,0:T(8,128)(2,1)S(1)}, u32[]{:S(2)}, u32[]{:S(2)}) collective-permute-start(bf16[13,64,512]{2,1,0:T(8,128)(2,1)} %get-tuple-element.50), channel_id=1, source_target_pairs={{4,0},{8,4},{12,8},{16,12},{20,16},{24,20},{28,24},{32,28},{36,32}... | collective-permute-start | bytes 2555912 | tf_op jit(solution)/shard_map/ppermute | solution.py:811
  59.1 25.6 %copy-start.2 = (bf16[2,3,64,64]{3,2,1,0:T(8,128)(2,1)S(1)}, bf16[2,3,64,64]{3,2,1,0:T(8,128)(2,1)}, u32[]{:S(2)}) copy-start(bf16[2,3,64,64]{3,2,1,0:T(8,128)(2,1)} %wr.7) | copy-start | bytes 147460
  74.1 20.0 %all-to-all-start = ((f32[32,12,128]{2,1,0:T(8,128)}), f32[32,12,128]{2,1,0:T(8,128)S(1)}, u32[]{:S(2)}, u32[]{:S(2)}) async-start(f32[32,12,128]{2,1,0:T(8,128)} %get-tuple-element.59), calls=%async_computation | async-start | bytes 524288 | tf_op jit(solution)/shard_map/all_to_all | solution.py:776

commit v5 on v4

v5 whole, which is shorter than its diff:
```python
import functools
import math

import jax
import jax.numpy as jnp
from jax import lax
from jax.experimental import pallas as pl
from jax.experimental.pallas import tpu as pltpu
from jax.sharding import Mesh, PartitionSpec as P

FIRST_SPACING = 4
SECOND_SPACING = 8
TILE = 128
C = 64
R = 32
W = 512
E = 640
HALO = 12
XEDGE = 32
CEDGE = 16
XTILES = R * XEDGE // 128
CTILES = R * CEDGE // 128
F32 = jnp.float32
BF16 = jnp.bfloat16
MIB = 1024 * 1024


def dot(a, b):
    return jnp.dot(a, b, preferred_element_type=F32)


def dot_nt(a, b):
    return lax.dot_general(a, b, (((1,), (1,)), ((), ())), preferred_element_type=F32)


def turn(block):
    return jnp.swapaxes(block, 0, 1)


def lanes(first, count, channels):
    lane = lax.broadcasted_iota(jnp.int32, (channels, 128), 1)
    return ((lane >= first) & (lane < first + count)).astype(F32).astype(BF16)


def rolled(v, shift):
    shift = shift % 128
    return pltpu.roll(v, shift, 1) if shift else v


def pack(rows, width, first):
    keep = lanes(first, width, rows[0].shape[0])
    parts = [rolled(v * keep, width * k - first) for k, v in enumerate(rows)]
    return functools.reduce(jnp.add, parts)


def unpack(left, right, k, width):
    channels = left.shape[0]
    ahead = rolled(right, -width * k) * lanes(0, width, channels)
    behind = rolled(left, 128 - width - width * k) * lanes(128 - width, width, channels)
    return ahead + behind


GC = 16


def edge_kernel(x_low, x_high, c_low, c_high, to_left, to_right):
    for src, width, at in ((x_low, XEDGE, 0), (c_low, CEDGE, XTILES)):
        for i in range(2):
            rows = turn(src[:, i * 16 : (i + 1) * 16, :])
            per = 128 // width
            for g in range(16 // per):
                tile = pack([rows[g * per + k] for k in range(per)], width, 0)
                to_left[at + (i * 16) // per + g] = tile
    for src, width, at in ((x_high, XEDGE, 0), (c_high, CEDGE, XTILES)):
        for i in range(2):
            rows = turn(src[:, i * 16 : (i + 1) * 16, :])
            per = 128 // width
            for g in range(16 // per):
                tile = pack([rows[g * per + k] for k in range(per)], width, 128 - width)
                to_right[at + (i * 16) // per + g] = tile


def pack_edges(x, c):
    low = pl.BlockSpec((GC, R, 128), lambda g: (g, 0, 0))
    high = pl.BlockSpec((GC, R, 128), lambda g: (g, 0, W // 128 - 1))
    out = pl.BlockSpec((XTILES + CTILES, GC, 128), lambda g: (0, g, 0))
    return pl.pallas_call(
        edge_kernel,
        grid=(C // GC,),
        in_specs=[low, high, low, high],
        out_specs=[out, out],
        out_shape=[jax.ShapeDtypeStruct((XTILES + CTILES, C, 128), BF16)] * 2,
        compiler_params=pltpu.CompilerParams(vmem_limit_bytes=16 * MIB),
        name="pack_edges",
    )(x, x, c, c)


def turn_block(src, dst):
    for i in range(R // 16):
        for t in range(W // 128):
            at = slice(t * 128, (t + 1) * 128)
            dst[i * 16 : (i + 1) * 16, :, at] = turn(src[:, i * 16 : (i + 1) * 16, at])


XROWS = 2 * HALO + 3
CROWS = HALO + 1


def turn_kernel(x_ref, c_ref, xt, x_up, x_down, ct, c_up, c_down):
    turn_block(x_ref, xt)
    for out, rows in ((x_up, slice(0, HALO)), (x_down, slice(R - HALO, R))):
        out[0:HALO] = xt[rows, :, MAIN[0]]
        out[HALO : 2 * HALO] = xt[rows, :, MAIN[1]]
    turn_block(c_ref, ct)
    c_up[0:HALO] = ct[0:HALO]
    c_down[0:HALO] = ct[R - HALO : R]


def message(rows, width):
    return (
        pl.BlockSpec((rows, GC, width), lambda g: (0, g, 0)),
        pltpu.HBM((rows, C, width), BF16),
    )


def turn_both(x, c):
    native = pl.BlockSpec((GC, R, W), lambda g: (g, 0, 0))
    turned = pl.BlockSpec((R, GC, W), lambda g: (0, g, 0))
    block = pltpu.VMEM((R, C, W), BF16)
    (xs, x_shape), (cs, c_shape) = message(XROWS, W // 2), message(CROWS, W)
    return pl.pallas_call(
        turn_kernel,
        grid=(C // GC,),
        in_specs=[native, native],
        out_specs=[turned, xs, xs, turned, cs, cs],
        out_shape=[block, x_shape, x_shape, block, c_shape, c_shape],
        compiler_params=pltpu.CompilerParams(vmem_limit_bytes=16 * MIB),
        name="turn_both",
    )(x, c)


def fill_kernel(
    x_up_in, x_down_in, c_up_in, c_down_in, left, right, x_up, x_down, c_up, c_down, x_rows, c_rows, sems
):
    copies = []
    for q, (out, first) in enumerate(((x_up, 0), (x_down, XTILES - 3))):
        tiles = [left[first + k] for k in range(3)] + [right[first + k] for k in range(3)]
        for k in range(3):
            x_rows[q, k] = jnp.concatenate(tiles[2 * k : 2 * k + 2], axis=1)
        copies.append(pltpu.make_async_copy(x_rows.at[q], out.at[2 * HALO : XROWS], sems.at[q]))
    for q, (out, first) in enumerate(((c_up, XTILES), (c_down, XTILES + CTILES - 2))):
        tiles = [left[first], left[first + 1], right[first], right[first + 1]]
        c_rows[q] = jnp.concatenate(tiles, axis=1)
        copies.append(pltpu.make_async_copy(c_rows.at[q], out.at[HALO], sems.at[2 + q]))
    for copy in copies:
        copy.start()
    for copy in copies:
        copy.wait()


def fill(messages, left, right):
    return pl.pallas_call(
        fill_kernel,
        in_specs=[ANY] * 4 + [VM, VM],
        out_specs=[ANY] * 4,
        out_shape=[pltpu.HBM(m.shape, BF16) for m in messages],
        input_output_aliases={q: q for q in range(4)},
        scratch_shapes=[
            pltpu.VMEM((2, 3, C, W // 2), BF16),
            pltpu.VMEM((2, C, W), BF16),
            pltpu.SemaphoreType.DMA((4,)),
        ],
        name="fill_messages",
    )(*map(in_hbm, messages), left, right)


ANY = pl.BlockSpec(memory_space=pl.ANY)
VM = pl.BlockSpec(memory_space=pltpu.VMEM)
SM = pl.BlockSpec(memory_space=pltpu.SMEM)
STEP = 8
LONG = 16


def build_mask(tiles, mask):
    row_dev, col_dev = lax.axis_index("rows"), lax.axis_index(COLS)
    n_rows, n_cols = tiles.shape
    first_row, first_tile = row_dev * R, col_dev * (W // TILE)
    lane = lax.broadcasted_iota(jnp.int32, (16, 128), 1)

    def value(p, ct):
        cell = first_row + (-1, 0, R)[p]
        inside = (cell >= 0) & (cell < n_rows * TILE) & (ct >= 0) & (ct < n_cols)
        rt = jnp.clip(cell, 0, n_rows * TILE - 1) // TILE
        return jnp.where(inside, tiles[rt, jnp.clip(ct, 0, n_cols - 1)], 0)

    for p in range(3):
        for t in range(W // 128):
            cell = jnp.full((16, 128), value(p, first_tile + t), jnp.int32)
            mask[p, :, t * 128 : (t + 1) * 128] = cell.astype(F32).astype(BF16)
        right = jnp.full((16, 128), value(p, first_tile + W // TILE), jnp.int32)
        left = jnp.full((16, 128), value(p, first_tile - 1), jnp.int32)
        mask[p, :, W:E] = jnp.where(lane < 64, right, left).astype(F32).astype(BF16)


def masked(v, mask, r, at):
    if isinstance(r, int):
        p = int(r >= 0) + int(r >= R)
    else:
        p = (r >= 0).astype(jnp.int32) + (r >= R).astype(jnp.int32)
    m = mask[p, :, at]
    return v * jnp.concatenate([m] * (C // 16), axis=0)


def shifted(v, d):
    return pltpu.roll(v, (-d) % v.shape[1], 1)


def row_stack(v, d, reverse):
    ahead, behind = shifted(v, d), shifted(v, -d)
    parts = [ahead, v, behind] if reverse else [behind, v, ahead]
    return jnp.concatenate(parts, axis=0)


def forward_matrix(w):
    return jnp.concatenate([w[j].astype(F32).T for j in range(3)], axis=0).T.astype(BF16)


def backward_matrix(w, order=(0, 1, 2)):
    return jnp.concatenate([w[j].astype(F32) for j in order], axis=0).T.astype(BF16)


def two_rows(matrix):
    none = jnp.zeros((C, C), BF16)
    return jnp.concatenate(
        [jnp.concatenate([matrix, none], axis=1), jnp.concatenate([none, matrix], axis=1)], axis=0
    )


MAIN = (slice(0, 256), slice(256, 512))
TAIL = slice(W, E)


class Rows:
    def __init__(self, *parts):
        self.parts = parts

    def __call__(self, r, at):
        for first, count, get in self.parts:
            if first <= r < first + count:
                return get(r - first, at)
        raise IndexError(r)

    def row(self, r):
        return jnp.concatenate([self(r, at) for at in (*MAIN, TAIL)], axis=1)


def held(ref, *index):
    return lambda q, at: ref[(*index, q, slice(None), at)]


def with_tail(main, tail):
    return lambda q, at: tail[q] if at == TAIL else main[q, :, at]


def conv_columns(get, rows, d, matrix, post, tail=True, taps=(-1, 0, 1, 2)):
    def window(r, at):
        return jnp.concatenate([get(r + k * d, at) for k in taps], axis=0)

    def put(r, at, both):
        post(r, at, both[:C])
        if len(taps) == 4:
            post(r + d, at, both[C:])

    for r in rows:
        for at in MAIN:
            put(r, at, dot(matrix, window(r, at)))
    if tail:
        for r, s in zip(rows[::2], rows[1::2]):
            both = dot(matrix, jnp.concatenate([window(r, TAIL), window(s, TAIL)], axis=1))
            put(r, TAIL, both[:, :128])
            put(s, TAIL, both[:, 128:])


SINGLE = (-1, 0, 1)


def conv_rows(get, rows, d, reverse, matrix, post, tail=True):
    stacks = []
    for r in rows:
        stack = row_stack(get.row(r), d, reverse)
        stacks.append(stack)
        for at in MAIN:
            post(r, at, dot(matrix, stack[:, at]))
    if tail:
        for q in range(0, len(rows), 2):
            both = dot(matrix, jnp.concatenate([stacks[q][:, TAIL], stacks[q + 1][:, TAIL]], axis=1))
            post(rows[q], TAIL, both[:, :128])
            post(rows[q + 1], TAIL, both[:, 128:])
    return stacks


def add_col_taps(acc_ref, grads, hidden, d, rows):
    acc = acc_ref[...]
    for r in rows:
        for at in MAIN:
            left = jnp.concatenate([hidden(r + q * d, at) for q in (0, 1)], axis=0)
            right = jnp.concatenate([grads(r + q * d, at) for q in (-1, 0, 1, 2)], axis=0)
            acc += dot_nt(left, right)
    acc_ref[...] = acc


def add_col_taps_single(acc_ref, grads, hidden, d, rows):
    acc = acc_ref[0:C, 0 : 3 * C]
    for r in rows:
        for at in MAIN:
            right = jnp.concatenate([grads(r + q * d, at) for q in (-1, 0, 1)], axis=0)
            acc += dot_nt(hidden(r, at), right)
    acc_ref[0:C, 0 : 3 * C] = acc


def add_row_taps(acc_ref, values, rows, stacks):
    acc = acc_ref[...]
    for r, stack in zip(rows, stacks):
        for at in MAIN:
            acc += dot_nt(values(r, at), stack[:, at])
    acc_ref[...] = acc


def elu(p):
    return jnp.where(p > 0, p, jnp.exp(p) - 1.0)


def turn_out(src, out):
    for i in range(R // 16):
        for t in range(W // 128):
            at = slice(t * 128, (t + 1) * 128)
            out[:, i * 16 : (i + 1) * 16, at] = turn(src[i * 16 : (i + 1) * 16, :, at])


def call(kernel, name, in_specs, outs, scratch, cost, vmem, *args):
    return pl.pallas_call(
        kernel,
        in_specs=in_specs,
        out_specs=[VM for _ in outs],
        out_shape=outs,
        scratch_shapes=scratch,
        compiler_params=pltpu.CompilerParams(vmem_limit_bytes=vmem * MIB),
        cost_estimate=pl.CostEstimate(flops=cost * 500_000_000, bytes_accessed=cost * 1_000_000, transcendentals=0),
        name=name,
    )(*args)


INNER = R - 2 * FIRST_SPACING
MIDDLE = R - 2 * SECOND_SPACING
OUTER = HALO
D1, D2 = FIRST_SPACING, SECOND_SPACING


def inner_kernel(
    tiles, x, c, left, right, wr, wc,
    xt, h1, b1, h2, ct, cm, a2, cg1, g1, col_acc, row_acc,
    mask,
):
    build_mask(tiles, mask)
    for dst, width, first, count in ((xt, XEDGE, 0, XTILES), (ct, CEDGE, XTILES, CTILES)):
        per = 128 // width

        def edges(g, _):
            for k in range(per):
                dst[g * per + k] = unpack(left[first + g], right[first + g], k, width)
            return 0

        lax.fori_loop(0, count, edges, 0)
    wr1, wr2 = forward_matrix(wr[0]), forward_matrix(wr[1])
    wc1 = two_rows(forward_matrix(wc[0]))
    wr2b = backward_matrix(wr[1])
    wc2b = two_rows(backward_matrix(wc[1], (2, 1, 0)))
    get_x = Rows((0, R, with_tail(x, xt)))
    get_c = Rows((0, R, with_tail(c, ct)))
    get_h1 = Rows((0, R, held(h1)))
    get_b1 = Rows((D1, INNER, held(b1)))
    get_h2 = Rows((D1, INNER, held(h2)))
    get_cm = Rows((0, R, held(cm)))
    get_a2 = Rows((D2, MIDDLE, held(a2)))

    def hidden_one(first):
        def post(row, at, pre):
            h1[row, :, at] = masked(elu(pre).astype(BF16), mask, row, at)

        conv_rows(get_x, [first + q for q in range(8)], D1, False, wr1, post)

    def block_one(first):
        def post(row, at, col):
            b1[row - D1, :, at] = get_x(row, at) + masked(col.astype(BF16), mask, row, at)

        conv_columns(get_h1, [first + q for q in range(D1)], D1, wc1, post)

    def hidden_two(first):
        def post(row, at, pre):
            h2[row - D1, :, at] = masked(elu(pre).astype(BF16), mask, row, at)

        conv_rows(get_b1, [first + q for q in range(8)], D2, False, wr2, post)

    def mask_cot(first):
        for r in range(first, first + 8):
            for at in (*MAIN, TAIL):
                cm[r, :, at] = masked(get_c(r, at), mask, r, at)

    hidden_one(0)
    mask_cot(0)
    hidden_one(8)
    mask_cot(8)
    block_one(4)
    hidden_one(16)
    mask_cot(16)
    block_one(12)
    hidden_two(4)
    hidden_one(24)
    mask_cot(24)
    block_one(20)
    hidden_two(12)
    hidden_two(20)

    def post_two(row, at, hid):
        slope = 1.0 + jnp.minimum(get_h2(row, at), 0).astype(F32)
        a2[row - D2, :, at] = masked((hid * slope).astype(BF16), mask, row, at)

    rows = [D2 + q for q in range(D2)]
    conv_columns(get_cm, rows, D2, wc2b, post_two)
    col_acc[...] = jnp.zeros_like(col_acc)
    row_acc[...] = jnp.zeros_like(row_acc)
    add_col_taps(col_acc, get_cm, get_h2, D2, rows)

    def post_one(row, at, mixed):
        g = get_c(row, at).astype(F32) + mixed
        cg1[row - D2, :, at] = masked(g.astype(BF16), mask, row, at)
        if at != TAIL:
            g1[row - D2, :, at] = g

    for first in range(D2, R - D2, 8):
        rows = list(range(first, first + 8))
        stacks = conv_rows(get_a2, rows, D2, True, wr2b, post_one)
        add_row_taps(row_acc, get_b1, rows, stacks)


def forward_inner(*args):
    return call(
        inner_kernel, "forward_inner", [SM] + [VM] * 6,
        [
            pltpu.VMEM((R, C, 128), BF16),
            pltpu.VMEM((R, C, E), BF16),
            pltpu.VMEM((INNER, C, E), BF16),
            pltpu.VMEM((INNER, C, E), BF16),
            pltpu.VMEM((R, C, 128), BF16),
            pltpu.VMEM((R, C, E), BF16),
            pltpu.VMEM((MIDDLE, C, E), BF16),
            pltpu.VMEM((MIDDLE, C, E), BF16),
            pltpu.VMEM((MIDDLE, C, W), F32),
            pltpu.VMEM((2 * C, 4 * C), F32),
            pltpu.VMEM((C, 3 * C), F32),
        ],
        [pltpu.VMEM((3, 16, E), BF16)],
        14, 8, *args,
    )


def outer_kernel(
    tiles, above, below, x, xt, h1, b1, h2, wr, wc,
    out, b1s, h2s,
    xe, h1e, flat, mask,
):
    build_mask(tiles, mask)
    wr1, wr2 = forward_matrix(wr[0]), forward_matrix(wr[1])
    wc1s = forward_matrix(wc[0])
    wc1, wc2 = two_rows(wc1s), two_rows(forward_matrix(wc[1]))
    per = 128 // XEDGE

    def message(side, ref):
        def get(q, at):
            if at == TAIL:
                return xe[side, q]
            return ref[q if at == MAIN[0] else HALO + q]

        return get

    for side, ref in enumerate((above, below)):
        tile = [ref[2 * HALO + k // 2, :, (k % 2) * 128 : (k % 2 + 1) * 128] for k in range(6)]
        for q in range(HALO):
            xe[side, q] = unpack(tile[q // per], tile[3 + q // per], q % per, XEDGE)
    get_x = Rows((-HALO, HALO, message(0, above)), (0, R, with_tail(x, xt)), (R, HALO, message(1, below)))
    get_h1 = Rows((-HALO, HALO, held(h1e, 0)), (0, R, held(h1)), (R, HALO, held(h1e, 1)))
    get_b1 = Rows((-D2, OUTER, held(b1s, 0)), (D1, INNER, held(b1)), (R - D1, OUTER, held(b1s, 1)))
    get_h2 = Rows((-D2, OUTER, held(h2s, 0)), (D1, INNER, held(h2)), (R - D1, OUTER, held(h2s, 1)))

    def hidden_one(side):
        first = (-HALO, R)[side]

        def post(row, at, pre):
            h1e[side, row - first, :, at] = masked(elu(pre).astype(BF16), mask, row, at)

        conv_rows(get_x, [first + q for q in range(HALO)], D1, False, wr1, post)

    def block_one(side):
        first = (-D2, R - D1)[side]

        def post(row, at, col):
            b1s[side, row - first, :, at] = get_x(row, at) + masked(col.astype(BF16), mask, row, at)

        conv_columns(get_h1, [first + q for q in range(D1)], D1, wc1, post)
        conv_columns(get_h1, [first + 2 * D1 + q for q in range(D1)], D1, wc1s, post, taps=SINGLE)

    def hidden_two(side):
        first = (-D2, R - D1)[side]

        def post(row, at, pre):
            h2s[side, row - first, :, at] = masked(elu(pre).astype(BF16), mask, row, at)

        conv_rows(get_b1, [first + q for q in range(OUTER)], D2, False, wr2, post)

    def last(first):
        def post(row, at, col):
            flat[row, :, at] = get_b1(row, at) + masked(col.astype(BF16), mask, row, at)

        conv_columns(get_h2, [first + q for q in range(D2)], D2, wc2, post, tail=False)

    hidden_one(0)
    block_one(0)
    hidden_one(1)
    hidden_two(0)
    block_one(1)
    last(0)
    hidden_two(1)
    last(2 * D2)
    turn_out(flat, out)


def forward_outer(*args):
    return call(
        outer_kernel, "forward_outer", [SM] + [VM] * 9,
        [
            jax.ShapeDtypeStruct((C, R, W), BF16),
            pltpu.VMEM((2, OUTER, C, E), BF16),
            pltpu.VMEM((2, OUTER, C, E), BF16),
        ],
        [
            pltpu.VMEM((2, HALO, C, 128), BF16),
            pltpu.VMEM((2, HALO, C, E), BF16),
            pltpu.VMEM((R, C, W), BF16),
            pltpu.VMEM((3, 16, E), BF16),
        ],
        14, 16, *args,
    )


PIECES = 32
PIECE = 6 * C // PIECES
REST = D1 + D2


def backward_kernel(
    tiles, above, below, wr, wc, c, ct, cm, a2, cg1, col_in, row_in, x, h1, b1, b1s, h2, h2s,
    taps, a1, g1s,
    cmh, a2s, cg1s, col_acc, row_acc, mask,
):
    build_mask(tiles, mask)
    wr1, wr2 = backward_matrix(wr[0]), backward_matrix(wr[1])
    wc1, wc2 = backward_matrix(wc[0], (2, 1, 0)), backward_matrix(wc[1], (2, 1, 0))
    wc1w, wc2w = two_rows(wc1), two_rows(wc2)
    per = 128 // CEDGE
    for side, ref, skip in ((0, above, 2 * per - HALO), (1, below, 0)):
        first = (-HALO, R)[side]
        tile = [ref[HALO, :, t * 128 : (t + 1) * 128] for t in range(4)]
        for q in range(HALO):
            g, k = divmod(q + skip, per)
            for at in MAIN:
                cmh[side, q, :, at] = masked(ref[q, :, at], mask, first + q, at)
            cmh[side, q, :, TAIL] = masked(unpack(tile[g], tile[2 + g], k, CEDGE), mask, first + q, TAIL)
    get_c = Rows((-HALO, HALO, held(cmh, 0)), (0, R, with_tail(c, ct)), (R, HALO, held(cmh, 1)))
    get_cm = Rows((-HALO, HALO, held(cmh, 0)), (0, R, held(cm)), (R, HALO, held(cmh, 1)))
    get_b1 = Rows((-D2, OUTER, held(b1s, 0)), (D1, INNER, held(b1)), (R - D1, OUTER, held(b1s, 1)))
    get_h2 = Rows((-D2, OUTER, held(h2s, 0)), (D1, INNER, held(h2)), (R - D1, OUTER, held(h2s, 1)))
    get_a2 = Rows((-D1, REST, held(a2s, 0)), (D2, MIDDLE, held(a2)), (R - D2, REST, held(a2s, 1)))
    get_cg1 = Rows((-D1, REST, held(cg1s, 0)), (D2, MIDDLE, held(cg1)), (R - D2, REST, held(cg1s, 1)))
    get_h1 = Rows((0, R, held(h1)))
    get_a1 = Rows((0, R, held(a1)))
    get_x = Rows((0, R, held(x)))
    firsts = (-D1, R - D2)

    col_acc[0] = col_in[...]
    row_acc[0] = row_in[...]
    col_acc[1] = jnp.zeros_like(col_in)
    row_acc[1] = jnp.zeros_like(row_in)
    for side, first in enumerate(firsts):

        def post_two(row, at, hid):
            slope = 1.0 + jnp.minimum(get_h2(row, at), 0).astype(F32)
            a2s[side, row - first, :, at] = masked((hid * slope).astype(BF16), mask, row, at)

        conv_columns(get_cm, [first + q for q in range(D1)], D2, wc2w, post_two)
        conv_columns(get_cm, [first + D1 + q for q in range(D1)], D2, wc2, post_two, taps=SINGLE)
    for side, first in enumerate(firsts):
        own = [r for r in range(first, first + REST) if 0 <= r < R]
        add_col_taps_single(col_acc.at[0], get_cm, get_h2, D2, own)

        def post_one(row, at, mixed):
            g = get_c(row, at).astype(F32) + mixed
            cg1s[side, row - first, :, at] = masked(g.astype(BF16), mask, row, at)
            if at != TAIL and row in own:
                g1s[side, row - own[0], :, at] = g

        rows = list(range(first, first + REST))
        stacks = conv_rows(get_a2, rows, D2, True, wr2, post_one)
        kept = [(r, stack) for r, stack in zip(rows, stacks) if r in own]
        add_row_taps(row_acc.at[0], get_b1, [k[0] for k in kept], [k[1] for k in kept])

    for first in range(0, R, 2 * D1):

        def post(row, at, hid):
            slope = 1.0 + jnp.minimum(h1[row, :, at], 0).astype(F32)
            a1[row, :, at] = masked((hid * slope).astype(BF16), mask, row, at)

        rows = [first + q for q in range(D1)]
        conv_columns(get_cg1, rows, D1, wc1w, post)
        add_col_taps(col_acc.at[1], get_cg1, get_h1, D1, rows)
        rows = list(range(first, first + 2 * D1))
        add_row_taps(row_acc.at[1], get_x, rows, [row_stack(get_a1.row(r), D1, True) for r in rows])

    for k in range(2):
        acc = col_acc[k]
        low, high = acc[:C].T, acc[C:].T
        col = [low[(2 - q) * C : (3 - q) * C] + high[(3 - q) * C : (4 - q) * C] for q in range(3)]
        both = jnp.concatenate([jnp.concatenate(col, axis=0), row_acc[k].T], axis=1)
        for q in range(PIECES // 2):
            taps[k * PIECES // 2 + q] = both[q * PIECE : (q + 1) * PIECE]


def backward(*args):
    return call(
        backward_kernel, "backward", [SM] + [VM] * 17,
        [
            jax.ShapeDtypeStruct((PIECES, PIECE, 2 * C), F32),
            pltpu.VMEM((R, C, E), BF16),
            pltpu.VMEM((2, D2, C, W), F32),
        ],
        [
            pltpu.VMEM((2, HALO, C, E), BF16),
            pltpu.VMEM((2, REST, C, E), BF16),
            pltpu.VMEM((2, REST, C, E), BF16),
            pltpu.VMEM((2, 2 * C, 4 * C), F32),
            pltpu.VMEM((2, C, 3 * C), F32),
            pltpu.VMEM((3, 16, E), BF16),
        ],
        16, 20, *args,
    )


def map_kernel(a1, g1, g1s, wr, out, flat):
    wr1 = backward_matrix(wr[0])
    get_a1 = Rows((0, R, held(a1)))
    get_g1 = Rows((0, D2, held(g1s, 0)), (D2, MIDDLE, held(g1)), (R - D2, D2, held(g1s, 1)))

    def post(row, at, mixed):
        flat[row, :, at] = (get_g1(row, at) + mixed).astype(BF16)

    for first in range(0, R, 8):
        conv_rows(get_a1, [first + q for q in range(8)], D1, True, wr1, post, tail=False)
    turn_out(flat, out)


def backward_map(*args):
    return call(
        map_kernel, "backward_map", [VM] * 4,
        [jax.ShapeDtypeStruct((C, R, W), BF16)],
        [pltpu.VMEM((R, C, W), BF16)],
        4, 10, *args,
    )[0]


def tap_sum(taps, beside):
    part = lax.all_to_all(taps, "rows", 0, 0, tiled=True)
    part = lax.all_gather(part.sum(0), COLS).sum(0)
    spread = jnp.broadcast_to(part[None], taps.shape)
    whole = lax.all_to_all(spread, "rows", 0, 0, tiled=True)
    return whole.reshape(2, 3, C, 2 * C), beside


COLS = ("y_hi", "core")


def in_hbm(array):
    return pltpu.with_memory_space_constraint(array, pltpu.HBM)


def in_vmem(array):
    return pltpu.with_memory_space_constraint(array, pltpu.VMEM)


def on_device(x, tile_mask, wr, wc, cot):
    n_rows, n_cols = lax.axis_size("rows"), lax.axis_size(COLS)
    factor = 1.0 / math.sqrt(R * n_rows * W * n_cols)
    down = [(i, i + 1) for i in range(n_rows - 1)]
    up = [(i + 1, i) for i in range(n_rows - 1)]
    right = [(i, i + 1) for i in range(n_cols - 1)]
    left = [(i + 1, i) for i in range(n_cols - 1)]

    to_left, to_right = pack_edges(x, cot)
    from_right = in_vmem(lax.ppermute(to_left, COLS, left))
    from_left = in_vmem(lax.ppermute(to_right, COLS, right))
    xt, x_up, x_down, ct, c_up, c_down = turn_both(x, cot)
    x_up, x_down, c_up, c_down = fill((x_up, x_down, c_up, c_down), from_left, from_right)
    x_above = in_vmem(lax.ppermute(x_down, "rows", down))
    x_below = in_vmem(lax.ppermute(x_up, "rows", up))
    c_above = in_vmem(lax.ppermute(c_down, "rows", down))
    c_below = in_vmem(lax.ppermute(c_up, "rows", up))

    xt, ct = in_vmem(xt), in_vmem(ct)
    x_tail, h1, b1, h2, c_tail, cm, a2, cg1, g1, col_taps, row_taps = map(
        in_vmem, forward_inner(tile_mask, xt, ct, from_left, from_right, wr, wc)
    )
    final, b1s, h2s = forward_outer(tile_mask, x_above, x_below, xt, x_tail, h1, b1, h2, wr, wc)
    b1s, h2s = in_vmem(b1s), in_vmem(h2s)
    taps, a1, g1s = backward(
        tile_mask, c_above, c_below, wr, wc, ct, c_tail, cm, a2, cg1, col_taps, row_taps,
        xt, h1, b1, b1s, h2, h2s,
    )
    total, map_grad = tap_sum(taps, backward_map(in_vmem(a1), g1, in_vmem(g1s), wr))
    total = total[::-1] * factor
    return final, map_grad, total[..., C:], total[..., :C]


def solution(mesh):
    n_rows, n_cols = mesh.devices.shape
    inner = Mesh(mesh.devices.reshape(n_rows, n_cols // 2, 2), ("rows",) + COLS)
    blocks = P(None, "rows", COLS)
    return jax.shard_map(
        on_device,
        mesh=inner,
        in_specs=(blocks, P(), P(), P(), blocks),
        out_specs=(blocks, blocks, P(), P()),
        check_vma=False,
    )
```

time: 120 us -> 115 us (0.958)
  Pallas kernels: 54.8 us -> 36.2 us
  local copies, waits for them, and re-layouts: 4.02 us -> 16.4 us
  starting transfers between devices: 24.9 us -> 18.1 us
  blocking collectives: 23.8 us -> 29.4 us
  waiting for transfers between devices: 10.5 us -> 13.1 us
    pallas_call x4, Pallas kernels: 46.1 us -> 30.6 us  [call(): pl.pallas_call(kernel, in_specs=in_specs, out_specs=[VM for _ in outs], o...]
    unnamed x6 -> x30, local copies, waits for them, and re-layouts: 3.18 us -> 14.8 us
    all_to_all x1, starting transfers between devices: 10.7 us -> 3.87 us  [tap_sum(): whole = lax.all_to_all(spread, 'rows', 0, 0, tiled=True)]
    all_to_all x1, blocking collectives: 14.5 us -> 19.7 us  [tap_sum(): part = lax.all_to_all(taps, 'rows', 0, 0, tiled=True)]
    ppermute x1, waiting for transfers between devices: 2.33 us -> 5.57 us  [on_device(): c_above = in_vmem(lax.ppermute(c_down, 'rows', down))]
    pallas_call x1, Pallas kernels: 6.27 us -> 3.26 us  [turn_both(): pl.pallas_call(turn_kernel, grid=(C // GC,), in_specs=[native, native], o...]
  transfers between devices with their start and end apart: 7 -> 7, of which waited for: 4 -> 3; matrix products, arithmetic and copies ran while one was open for 0% -> 0% of each run, Pallas kernels for 32% -> 21%
where the time goes in v5:
time: 115 us; the launch traced here: 114 us
  Pallas kernels  36.2 us (31%)
  blocking collectives  29.4 us (26%)
  starting transfers between devices  18.1 us (16%)
  local copies, waits for them, and re-layouts  16.4 us (14%)
  waiting for transfers between devices  13.1 us (11%)
    pallas_call x4, Pallas kernels, call(): pl.pallas_call(kernel, in_specs=in_specs, out_specs=[VM for _ in outs], o...  30.6 us
    all_to_all x1, blocking collectives, tap_sum(): part = lax.all_to_all(taps, 'rows', 0, 0, tiled=True)  19.7 us
    unnamed x30, local copies, waits for them, and re-layouts  14.8 us
    all_gather x1, blocking collectives, tap_sum(): part = lax.all_gather(part.sum(0), COLS).sum(0)  9.68 us
    ppermute x1, waiting for transfers between devices, on_device(): c_above = in_vmem(lax.ppermute(c_down, 'rows', down))  5.57 us
    ppermute x1, starting transfers between devices, on_device(): c_above = in_vmem(lax.ppermute(c_down, 'rows', down))  4.6 us
    ppermute x1, waiting for transfers between devices, on_device(): c_below = in_vmem(lax.ppermute(c_up, 'rows', up))  4.49 us
    ppermute x1, starting transfers between devices, on_device(): x_above = in_vmem(lax.ppermute(x_down, 'rows', down))  4.41 us
  transfers between devices with their start and end apart: 7, of which 3 were waited for; matrix products, arithmetic and copies ran while one was open for 0% of the time, Pallas kernels for 21%

profile of v5, /device:TPU:0, one launch (start us, length us, event | category | flops | bytes accessed | tf_op | source)
XLA Modules:
  0.0 114.1 jit_solution(3561815958558760226)
XLA Ops:
  0.6 0.0 copy-start
  0.6 1.6 %copy-done = bf16[64,32,512]{2,1,0:T(8,128)(2,1)S(1)} copy-done((bf16[64,32,512]{2,1,0:T(8,128)(2,1)S(1)}, bf16[64,32,512]{2,1,0:T(8,128)(2,1)}, u32[]{:S(2)}) %copy-start) | copy-done | bytes 2097176
  2.2 0.0 copy-start.1
  2.2 1.6 %copy-done.1 = bf16[64,32,512]{2,1,0:T(8,128)(2,1)S(1)} copy-done((bf16[64,32,512]{2,1,0:T(8,128)(2,1)S(1)}, bf16[64,32,512]{2,1,0:T(8,128)(2,1)}, u32[]{:S(2)}) %copy-start.1) | copy-done | bytes 2097176
  3.8 1.6 %pack_edges.1 = (bf16[12,64,128]{2,1,0:T(8,128)(2,1)S(1)}, bf16[12,64,128]{2,1,0:T(8,128)(2,1)S(1)}) custom-call(bf16[64,32,512]{2,1,0:T(8,128)(2,1)S(1)} %copy-done, bf16[64,32,512]{2,1,0:T(8,128)(2,1)S(1)} %copy-done, bf16[64,32,512]{2,1,0:T(8,128)(2,1)S(1)} %copy-done.1, bf16[64,32,512]{2,1,0:T(8,128)(2,1)S(1)} %copy-done.1), custom_call_target="tpu_custom_call" | custom-call | tf_op jit(solution)/shard_map/pack_edges/pallas_call | solution.py:87
  5.5 1.3 %collective-permute-start = (bf16[12,64,128]{2,1,0:T(8,128)(2,1)S(1)}, bf16[12,64,128]{2,1,0:T(8,128)(2,1)S(1)}, u32[]{:S(2)}, u32[]{:S(2)}) collective-permute-start(bf16[12,64,128]{2,1,0:T(8,128)(2,1)S(1)} %get-tuple-element.37), channel_id=1, source_target_pairs={{0,1},{1,2},{2,3},{4,5},{5,6},{6,7},{8,9},{9,10},{10,11},{12,13},{... | collective-permute-start | bytes 589832 | tf_op jit(solution)/shard_map/ppermute | solution.py:708
  6.8 1.3 %collective-permute-start.1 = (bf16[12,64,128]{2,1,0:T(8,128)(2,1)S(1)}, bf16[12,64,128]{2,1,0:T(8,128)(2,1)S(1)}, u32[]{:S(2)}, u32[]{:S(2)}) collective-permute-start(bf16[12,64,128]{2,1,0:T(8,128)(2,1)S(1)} %get-tuple-element.38), channel_id=1, source_target_pairs={{1,0},{2,1},{3,2},{5,4},{6,5},{7,6},{9,8},{10,9},{11,10},{13,12},{... | collective-permute-start | bytes 589832 | tf_op jit(solution)/shard_map/ppermute | solution.py:707
  8.1 3.3 %turn_both.1 = (bf16[32,64,512]{2,1,0:T(8,128)(2,1)S(1)}, bf16[27,64,256]{2,1,0:T(8,128)(2,1)}, bf16[27,64,256]{2,1,0:T(8,128)(2,1)}, bf16[32,64,512]{2,1,0:T(8,...) custom-call(bf16[64,32,512]{2,1,0:T(8,128)(2,1)S(1)} %copy-done, bf16[64,32,512]{2,1,0:T(8,128)(2,1)S(1)} %copy-done.1), custom_call_target="tpu_custom_call" | custom-call | tf_op jit(solution)/shard_map/turn_both/pallas_call | solution.py:131
  11.3 0.0 copy-start.7
  11.3 1.3 %copy-done.7 = bf16[32,64,512]{2,1,0:T(8,128)(2,1)} copy-done((bf16[32,64,512]{2,1,0:T(8,128)(2,1)}, bf16[32,64,512]{2,1,0:T(8,128)(2,1)S(1)}, u32[]{:S(2)}) %copy-start.7) | copy-done | bytes 2097176
  12.6 0.0 copy-start.10
  12.6 1.3 %copy-done.10 = bf16[32,64,512]{2,1,0:T(8,128)(2,1)} copy-done((bf16[32,64,512]{2,1,0:T(8,128)(2,1)}, bf16[32,64,512]{2,1,0:T(8,128)(2,1)S(1)}, u32[]{:S(2)}) %copy-start.10) | copy-done | bytes 2097176
  14.0 0.0 copy-start.6
  14.0 0.0 copy-start.13
  14.0 0.0 copy-start.14
  14.0 0.0 collective-permute-done.left
  14.0 0.0 collective-permute-done.1.right
  14.0 0.8 fill_messages.1
  14.8 4.4 %collective-permute-start.2 = (bf16[27,64,256]{2,1,0:T(8,128)(2,1)}, bf16[27,64,256]{2,1,0:T(8,128)(2,1)S(1)}, u32[]{:S(2)}, u32[]{:S(2)}) collective-permute-start(bf16[27,64,256]{2,1,0:T(8,128)(2,1)} %get-tuple-element.39), channel_id=1, source_target_pairs={{0,4},{4,8},{8,12},{12,16},{16,20},{20,24},{24,28},{28,32},{32,36}... | collective-permute-start | bytes 2654216 | tf_op jit(solution)/shard_map/ppermute | solution.py:711
  19.2 1.3 %collective-permute-start.3 = (bf16[27,64,256]{2,1,0:T(8,128)(2,1)}, bf16[27,64,256]{2,1,0:T(8,128)(2,1)S(1)}, u32[]{:S(2)}, u32[]{:S(2)}) collective-permute-start(bf16[27,64,256]{2,1,0:T(8,128)(2,1)} %get-tuple-element.40), channel_id=1, source_target_pairs={{4,0},{8,4},{12,8},{16,12},{20,16},{24,20},{28,24},{32,28},{36,32}... | collective-permute-start | bytes 2654216 | tf_op jit(solution)/shard_map/ppermute | solution.py:712
  20.5 4.6 %collective-permute-start.4 = (bf16[13,64,512]{2,1,0:T(8,128)(2,1)}, bf16[13,64,512]{2,1,0:T(8,128)(2,1)S(1)}, u32[]{:S(2)}, u32[]{:S(2)}) collective-permute-start(bf16[13,64,512]{2,1,0:T(8,128)(2,1)} %get-tuple-element.48), channel_id=1, source_target_pairs={{0,4},{4,8},{8,12},{12,16},{16,20},{20,24},{24,28},{28,32},{32,36}... | collective-permute-start | bytes 2555912 | tf_op jit(solution)/shard_map/ppermute | solution.py:713
  25.1 1.3 %collective-permute-start.5 = (bf16[13,64,512]{2,1,0:T(8,128)(2,1)}, bf16[13,64,512]{2,1,0:T(8,128)(2,1)S(1)}, u32[]{:S(2)}, u32[]{:S(2)}) collective-permute-start(bf16[13,64,512]{2,1,0:T(8,128)(2,1)} %get-tuple-element.49), channel_id=1, source_target_pairs={{4,0},{8,4},{12,8},{16,12},{20,16},{24,20},{28,24},{32,28},{36,32}... | collective-permute-start | bytes 2555912 | tf_op jit(solution)/shard_map/ppermute | solution.py:714
  26.4 0.0 copy-done.6
  26.4 0.0 copy-done.13
  26.4 0.0 copy-done.14
  26.4 0.0 copy-start.8
  26.4 1.6 %copy-done.8 = bf16[32,64,512]{2,1,0:T(8,128)(2,1)S(1)} copy-done((bf16[32,64,512]{2,1,0:T(8,128)(2,1)S(1)}, bf16[32,64,512]{2,1,0:T(8,128)(2,1)}, u32[]{:S(2)}) %copy-start.8) | copy-done | bytes 2097176
  28.0 0.0 copy-start.11
  28.0 1.6 %copy-done.11 = bf16[32,64,512]{2,1,0:T(8,128)(2,1)S(1)} copy-done((bf16[32,64,512]{2,1,0:T(8,128)(2,1)S(1)}, bf16[32,64,512]{2,1,0:T(8,128)(2,1)}, u32[]{:S(2)}) %copy-start.11) | copy-done | bytes 2097176
  29.6 0.0 copy-start.9
  29.6 9.4 %forward_inner.1 = (bf16[32,64,128]{2,1,0:T(8,128)(2,1)S(1)}, bf16[32,64,640]{2,1,0:T(8,128)(2,1)S(1)}, bf16[24,64,640]{2,1,0:T(8,128)(2,1)S(1)}, bf16[24,64,640...) custom-call(s32[8,16]{1,0:T(8,128)S(1)} %copy-done.14, ...), custom_call_target="tpu_custom_call" | custom-call | flops 7000000000 | bytes 14000000 | tf_op jit(solution)/shard_map/forward_inner/pallas_call | solution.py:341
  39.0 0.0 copy-start.2
  39.0 1.3 %copy-done.2 = f32[16,64,512]{2,1,0:T(8,128)} copy-done((f32[16,64,512]{2,1,0:T(8,128)}, f32[16,64,512]{2,1,0:T(8,128)S(1)}, u32[]{:S(2)}) %copy-start.2) | copy-done | bytes 2097176
  40.3 0.0 collective-permute-done.2.above
  40.3 0.0 collective-permute-done.3.below
  40.3 0.0 copy-done.9
  40.3 0.0 copy-start.12
  40.3 8.0 %forward_outer.1 = (bf16[64,32,512]{2,1,0:T(8,128)(2,1)}, bf16[2,12,64,640]{3,2,1,0:T(8,128)(2,1)S(1)}, bf16[2,12,64,640]{3,2,1,0:T(8,128)(2,1)S(1)}) custom-call(s32[8,16]{1,0:T(8,128)S(1)} %copy-done.14, bf16[27,64,256]{2,1,0:T(8,128)(2,1)S(1)} %collective-permute-done.2.above, bf16[27,64,256]{2,1,0:T(8,128)(2,1)S(1)} %collective-permute-done.3.below, ...), custom_call_target="tpu_custom_call" | custom-call | flops 7000000000 | bytes 14000000 | tf_op jit(solution)/shard_map/forward_outer/pallas_call | solution.py:341
  48.4 5.6 %collective-permute-done.4.above = bf16[13,64,512]{2,1,0:T(8,128)(2,1)S(1)} collective-permute-done((bf16[13,64,512]{2,1,0:T(8,128)(2,1)}, bf16[13,64,512]{2,1,0:T(8,128)(2,1)S(1)}, u32[]{:S(2)}, u32[]{:S(2)}) %collective-permute-start.4) | collective-permute-done | bytes 852000 | tf_op jit(solution)/shard_map/ppermute | solution.py:713
  53.9 4.5 %collective-permute-done.5.below = bf16[13,64,512]{2,1,0:T(8,128)(2,1)S(1)} collective-permute-done((bf16[13,64,512]{2,1,0:T(8,128)(2,1)}, bf16[13,64,512]{2,1,0:T(8,128)(2,1)S(1)}, u32[]{:S(2)}, u32[]{:S(2)}) %collective-permute-start.5) | collective-permute-done | bytes 852000 | tf_op jit(solution)/shard_map/ppermute | solution.py:714
  58.4 0.0 copy-done.12
  58.4 9.4 %backward.1 = (f32[32,12,128]{2,1,0:T(8,128)S(1)}, bf16[32,64,640]{2,1,0:T(8,128)(2,1)S(1)}, f32[2,8,64,512]{3,2,1,0:T(8,128)S(1)}) custom-call(s32[8,16]{1,0:T(8,128)S(1)} %copy-done.14, bf16[13,64,512]{2,1,0:T(8,128)(2,1)S(1)} %collective-permute-done.4.above, bf16[13,64,512]{2,1,0:T(8,128)(2,1)S(1)} %collective-permute-done.5.below, ...), custom_call_target="tpu_custom_call" | custom-call | flops 8000000000 | bytes 16000000 | tf_op jit(solution)/shard_map/backward/pallas_call | solution.py:341
  67.9 0.0 copy-start.4
  67.9 1.3 %copy-done.4 = f32[2,8,64,512]{3,2,1,0:T(8,128)} copy-done((f32[2,8,64,512]{3,2,1,0:T(8,128)}, f32[2,8,64,512]{3,2,1,0:T(8,128)S(1)}, u32[]{:S(2)}) %copy-start.4) | copy-done | bytes 2097176
  69.2 19.7 %all_to_all.10 = f32[32,12,128]{2,1,0:T(8,128)S(1)} all-to-all(f32[32,12,128]{2,1,0:T(8,128)S(1)} %get-tuple-element.61), channel_id=1, replica_groups=mesh['rows'=32,'y_hi'=2,'core'=2] {'rows'}, dimensions={0} | all-to-all | bytes 393216 | tf_op jit(solution)/shard_map/all_to_all | solution.py:680
  88.9 9.7 %all-gather.1 = f32[4,12,128]{2,1,0:T(8,128)S(1)} all-gather(f32[1,12,128]{2,1,0:T(8,128)S(1)} %bitcast.1), channel_id=2, replica_groups=mesh['rows'=32,'y_hi'=2,'core'=2] {'y_hi','core'}, dimensions={0}, use_global_device_ids=true | all-gather | bytes 30720 | tf_op jit(solution)/shard_map/all_gather | solution.py:681
  98.6 0.7 broadcast_in_dim.2
  99.3 3.9 %all-to-all-start.1 = ((f32[32,12,128]{2,1,0:T(8,128)}), f32[32,12,128]{2,1,0:T(8,128)S(1)}, u32[]{:S(2)}, u32[]{:S(2)}) async-start(f32[32,12,128]{2,1,0:T(8,128)} %broadcast_in_dim.2), calls=%async_computation.1 | async-start | bytes 524288 | tf_op jit(solution)/shard_map/all_to_all | solution.py:683
  103.2 0.0 copy-start.3
  103.2 1.6 %copy-done.3 = f32[16,64,512]{2,1,0:T(8,128)S(1)} copy-done((f32[16,64,512]{2,1,0:T(8,128)S(1)}, f32[16,64,512]{2,1,0:T(8,128)}, u32[]{:S(2)}) %copy-start.3) | copy-done | bytes 2097176
  104.8 0.0 copy-start.5
  104.8 1.6 %copy-done.5 = f32[2,8,64,512]{3,2,1,0:T(8,128)S(1)} copy-done((f32[2,8,64,512]{3,2,1,0:T(8,128)S(1)}, f32[2,8,64,512]{3,2,1,0:T(8,128)}, u32[]{:S(2)}) %copy-start.5) | copy-done | bytes 2097176
  106.4 3.7 %backward_map.1 = bf16[64,32,512]{2,1,0:T(8,128)(2,1)} custom-call(bf16[32,64,640]{2,1,0:T(8,128)(2,1)S(1)} %get-tuple-element.58.a1, f32[16,64,512]{2,1,0:T(8,128)S(1)} %copy-done.3, f32[2,8,64,512]{3,2,1,0:T(8,128)S(1)} %copy-done.5, bf16[2,3,64,64]{3,2,1,0:T(8,128)(2,1)S(1)} %copy-done.6), custom_call_target="tpu_custom_call" | custom-call | flops 2000000000 | bytes 4000000 | tf_op jit(solution)/shard_map/backward_map/pallas_call | solution.py:341
  110.1 3.1 %all-to-all-done.1 = f32[32,12,128]{2,1,0:T(8,128)S(1)} async-done(((f32[32,12,128]{2,1,0:T(8,128)}), f32[32,12,128]{2,1,0:T(8,128)S(1)}, u32[]{:S(2)}, u32[]{:S(2)}) %all-to-all-start.1) | async-done | bytes 196640 | tf_op jit(solution)/shard_map/all_to_all | solution.py:683
  113.3 0.8 fusion
  (4 shorter events, 0.1 us)
Async XLA Ops:
  0.6 1.6 %copy-start = (bf16[64,32,512]{2,1,0:T(8,128)(2,1)S(1)}, bf16[64,32,512]{2,1,0:T(8,128)(2,1)}, u32[]{:S(2)}) copy-start(bf16[64,32,512]{2,1,0:T(8,128)(2,1)} %x_high.1) | copy-start | bytes 6291460
  2.2 1.6 %copy-start.1 = (bf16[64,32,512]{2,1,0:T(8,128)(2,1)S(1)}, bf16[64,32,512]{2,1,0:T(8,128)(2,1)}, u32[]{:S(2)}) copy-start(bf16[64,32,512]{2,1,0:T(8,128)(2,1)} %c_high.1) | copy-start | bytes 6291460
  5.5 8.5 %collective-permute-start = (bf16[12,64,128]{2,1,0:T(8,128)(2,1)S(1)}, bf16[12,64,128]{2,1,0:T(8,128)(2,1)S(1)}, u32[]{:S(2)}, u32[]{:S(2)}) collective-permute-start(bf16[12,64,128]{2,1,0:T(8,128)(2,1)S(1)} %get-tuple-element.37), channel_id=1, source_target_pairs={{0,1},{1,2},{2,3},{4,5},{5,6},{6,7},{8,9},{9,10},{10,11},{12,13},{... | collective-permute-start | bytes 589832 | tf_op jit(solution)/shard_map/ppermute | solution.py:708
  6.8 7.2 %collective-permute-start.1 = (bf16[12,64,128]{2,1,0:T(8,128)(2,1)S(1)}, bf16[12,64,128]{2,1,0:T(8,128)(2,1)S(1)}, u32[]{:S(2)}, u32[]{:S(2)}) collective-permute-start(bf16[12,64,128]{2,1,0:T(8,128)(2,1)S(1)} %get-tuple-element.38), channel_id=1, source_target_pairs={{1,0},{2,1},{3,2},{5,4},{6,5},{7,6},{9,8},{10,9},{11,10},{13,12},{... | collective-permute-start | bytes 589832 | tf_op jit(solution)/shard_map/ppermute | solution.py:707
  11.3 1.3 %copy-start.7 = (bf16[32,64,512]{2,1,0:T(8,128)(2,1)}, bf16[32,64,512]{2,1,0:T(8,128)(2,1)S(1)}, u32[]{:S(2)}) copy-start(bf16[32,64,512]{2,1,0:T(8,128)(2,1)S(1)} %get-tuple-element.41.x) | copy-start | bytes 6291460
  12.6 1.3 %copy-start.10 = (bf16[32,64,512]{2,1,0:T(8,128)(2,1)}, bf16[32,64,512]{2,1,0:T(8,128)(2,1)S(1)}, u32[]{:S(2)}) copy-start(bf16[32,64,512]{2,1,0:T(8,128)(2,1)S(1)} %get-tuple-element.42.c) | copy-start | bytes 6291460
  14.0 12.4 %copy-start.6 = (bf16[2,3,64,64]{3,2,1,0:T(8,128)(2,1)S(1)}, bf16[2,3,64,64]{3,2,1,0:T(8,128)(2,1)}, u32[]{:S(2)}) copy-start(bf16[2,3,64,64]{3,2,1,0:T(8,128)(2,1)} %wr.7) | copy-start | bytes 147460
  14.0 12.4 %copy-start.13 = (bf16[2,3,64,64]{3,2,1,0:T(8,128)(2,1)S(1)}, bf16[2,3,64,64]{3,2,1,0:T(8,128)(2,1)}, u32[]{:S(2)}) copy-start(bf16[2,3,64,64]{3,2,1,0:T(8,128)(2,1)} %wc.5) | copy-start | bytes 147460
  14.0 12.4 %copy-start.14 = (s32[8,16]{1,0:T(8,128)S(1)}, s32[8,16]{1,0:T(8,128)}, u32[]{:S(2)}) copy-start(s32[8,16]{1,0:T(8,128)} %tiles.5) | copy-start | bytes 1540
  14.8 25.5 %collective-permute-start.2 = (bf16[27,64,256]{2,1,0:T(8,128)(2,1)}, bf16[27,64,256]{2,1,0:T(8,128)(2,1)S(1)}, u32[]{:S(2)}, u32[]{:S(2)}) collective-permute-start(bf16[27,64,256]{2,1,0:T(8,128)(2,1)} %get-tuple-element.39), channel_id=1, source_target_pairs={{0,4},{4,8},{8,12},{12,16},{16,20},{20,24},{24,28},{28,32},{32,36}... | collective-permute-start | bytes 2654216 | tf_op jit(solution)/shard_map/ppermute | solution.py:711
  19.2 21.1 %collective-permute-start.3 = (bf16[27,64,256]{2,1,0:T(8,128)(2,1)}, bf16[27,64,256]{2,1,0:T(8,128)(2,1)S(1)}, u32[]{:S(2)}, u32[]{:S(2)}) collective-permute-start(bf16[27,64,256]{2,1,0:T(8,128)(2,1)} %get-tuple-element.40), channel_id=1, source_target_pairs={{4,0},{8,4},{12,8},{16,12},{20,16},{24,20},{28,24},{32,28},{36,32}... | collective-permute-start | bytes 2654216 | tf_op jit(solution)/shard_map/ppermute | solution.py:712
  20.5 33.4 %collective-permute-start.4 = (bf16[13,64,512]{2,1,0:T(8,128)(2,1)}, bf16[13,64,512]{2,1,0:T(8,128)(2,1)S(1)}, u32[]{:S(2)}, u32[]{:S(2)}) collective-permute-start(bf16[13,64,512]{2,1,0:T(8,128)(2,1)} %get-tuple-element.48), channel_id=1, source_target_pairs={{0,4},{4,8},{8,12},{12,16},{16,20},{20,24},{24,28},{28,32},{32,36}... | collective-permute-start | bytes 2555912 | tf_op jit(solution)/shard_map/ppermute | solution.py:713
  25.1 33.3 %collective-permute-start.5 = (bf16[13,64,512]{2,1,0:T(8,128)(2,1)}, bf16[13,64,512]{2,1,0:T(8,128)(2,1)S(1)}, u32[]{:S(2)}, u32[]{:S(2)}) collective-permute-start(bf16[13,64,512]{2,1,0:T(8,128)(2,1)} %get-tuple-element.49), channel_id=1, source_target_pairs={{4,0},{8,4},{12,8},{16,12},{20,16},{24,20},{28,24},{32,28},{36,32}... | collective-permute-start | bytes 2555912 | tf_op jit(solution)/shard_map/ppermute | solution.py:714
  26.4 1.6 %copy-start.8 = (bf16[32,64,512]{2,1,0:T(8,128)(2,1)S(1)}, bf16[32,64,512]{2,1,0:T(8,128)(2,1)}, u32[]{:S(2)}) copy-start(bf16[32,64,512]{2,1,0:T(8,128)(2,1)} %copy-done.7) | copy-start | bytes 6291460
  28.0 1.6 %copy-start.11 = (bf16[32,64,512]{2,1,0:T(8,128)(2,1)S(1)}, bf16[32,64,512]{2,1,0:T(8,128)(2,1)}, u32[]{:S(2)}) copy-start(bf16[32,64,512]{2,1,0:T(8,128)(2,1)} %copy-done.10) | copy-start | bytes 6291460
  29.6 10.7 %copy-start.9 = (bf16[32,64,512]{2,1,0:T(8,128)(2,1)S(1)}, bf16[32,64,512]{2,1,0:T(8,128)(2,1)}, u32[]{:S(2)}) copy-start(bf16[32,64,512]{2,1,0:T(8,128)(2,1)} %copy-done.7) | copy-start | bytes 6291460
  39.0 1.3 %copy-start.2 = (f32[16,64,512]{2,1,0:T(8,128)}, f32[16,64,512]{2,1,0:T(8,128)S(1)}, u32[]{:S(2)}) copy-start(f32[16,64,512]{2,1,0:T(8,128)S(1)} %get-tuple-element.59.g1) | copy-start | bytes 6291460
  40.3 18.1 %copy-start.12 = (bf16[32,64,512]{2,1,0:T(8,128)(2,1)S(1)}, bf16[32,64,512]{2,1,0:T(8,128)(2,1)}, u32[]{:S(2)}) copy-start(bf16[32,64,512]{2,1,0:T(8,128)(2,1)} %copy-done.10) | copy-start | bytes 6291460
  67.9 1.3 %copy-start.4 = (f32[2,8,64,512]{3,2,1,0:T(8,128)}, f32[2,8,64,512]{3,2,1,0:T(8,128)S(1)}, u32[]{:S(2)}) copy-start(f32[2,8,64,512]{3,2,1,0:T(8,128)S(1)} %get-tuple-element.60.g1s) | copy-start | bytes 6291460
  99.3 13.9 %all-to-all-start.1 = ((f32[32,12,128]{2,1,0:T(8,128)}), f32[32,12,128]{2,1,0:T(8,128)S(1)}, u32[]{:S(2)}, u32[]{:S(2)}) async-start(f32[32,12,128]{2,1,0:T(8,128)} %broadcast_in_dim.2), calls=%async_computation.1 | async-start | bytes 524288 | tf_op jit(solution)/shard_map/all_to_all | solution.py:683
  103.2 1.6 %copy-start.3 = (f32[16,64,512]{2,1,0:T(8,128)S(1)}, f32[16,64,512]{2,1,0:T(8,128)}, u32[]{:S(2)}) copy-start(f32[16,64,512]{2,1,0:T(8,128)} %copy-done.2) | copy-start | bytes 6291460
  104.8 1.6 %copy-start.5 = (f32[2,8,64,512]{3,2,1,0:T(8,128)S(1)}, f32[2,8,64,512]{3,2,1,0:T(8,128)}, u32[]{:S(2)}) copy-start(f32[2,8,64,512]{3,2,1,0:T(8,128)} %copy-done.4) | copy-start | bytes 6291460

commit v6 on v5

--- a/solution.py
+++ b/solution.py
@@ -170,6 +170,7 @@
             pltpu.VMEM((2, C, W), BF16),
             pltpu.SemaphoreType.DMA((4,)),
         ],
+        compiler_params=pltpu.CompilerParams(vmem_limit_bytes=8 * MIB),
         name="fill_messages",
     )(*map(in_hbm, messages), left, right)
 
@@ -341,7 +342,7 @@
     return pl.pallas_call(
         kernel,
         in_specs=in_specs,
-        out_specs=[VM for _ in outs],
+        out_specs=[ANY if getattr(out, "memory_space", None) == pltpu.HBM else VM for out in outs],
         out_shape=outs,
         scratch_shapes=scratch,
         compiler_params=pltpu.CompilerParams(vmem_limit_bytes=vmem * MIB),
@@ -558,10 +559,12 @@
 
 
 def backward_kernel(
-    tiles, above, below, wr, wc, c, ct, cm, a2, cg1, col_in, row_in, x, h1, b1, b1s, h2, h2s,
-    taps, a1, g1s,
-    cmh, a2s, cg1s, col_acc, row_acc, mask,
+    tiles, above, below, wr, wc, c, ct, cm, a2, cg1, g1, col_in, row_in, x, h1, b1, b1s, h2, h2s,
+    taps, a1, g1_out,
+    cmh, a2s, cg1s, g1s, col_acc, row_acc, mask, sems,
 ):
+    saves = [pltpu.make_async_copy(g1, g1_out.at[D2 : R - D2], sems.at[0])]
+    saves[0].start()
     build_mask(tiles, mask)
     wr1, wr2 = backward_matrix(wr[0]), backward_matrix(wr[1])
     wc1, wc2 = backward_matrix(wc[0], (2, 1, 0)), backward_matrix(wc[1], (2, 1, 0))
@@ -612,6 +615,8 @@
         stacks = conv_rows(get_a2, rows, D2, True, wr2, post_one)
         kept = [(r, stack) for r, stack in zip(rows, stacks) if r in own]
         add_row_taps(row_acc.at[0], get_b1, [k[0] for k in kept], [k[1] for k in kept])
+        saves.append(pltpu.make_async_copy(g1s.at[side], g1_out.at[own[0] : own[0] + D2], sems.at[1 + side]))
+        saves[-1].start()
 
     for first in range(0, R, 2 * D1):
 
@@ -632,47 +637,54 @@
         both = jnp.concatenate([jnp.concatenate(col, axis=0), row_acc[k].T], axis=1)
         for q in range(PIECES // 2):
             taps[k * PIECES // 2 + q] = both[q * PIECE : (q + 1) * PIECE]
+    for save in saves:
+        save.wait()
 
 
 def backward(*args):
     return call(
-        backward_kernel, "backward", [SM] + [VM] * 17,
+        backward_kernel, "backward", [SM] + [VM] * 18,
         [
             jax.ShapeDtypeStruct((PIECES, PIECE, 2 * C), F32),
             pltpu.VMEM((R, C, E), BF16),
-            pltpu.VMEM((2, D2, C, W), F32),
+            pltpu.HBM((R, C, W), F32),
         ],
         [
             pltpu.VMEM((2, HALO, C, E), BF16),
             pltpu.VMEM((2, REST, C, E), BF16),
             pltpu.VMEM((2, REST, C, E), BF16),
+            pltpu.VMEM((2, D2, C, W), F32),
             pltpu.VMEM((2, 2 * C, 4 * C), F32),
             pltpu.VMEM((2, C, 3 * C), F32),
             pltpu.VMEM((3, 16, E), BF16),
+            pltpu.SemaphoreType.DMA((3,)),
         ],
         16, 20, *args,
     )
 
 
-def map_kernel(a1, g1, g1s, wr, out, flat):
+def map_kernel(a1, g1_in, wr, out, g1, flat, sems):
+    loads = [pltpu.make_async_copy(g1_in.at[r : r + 8], g1.at[r : r + 8], sems.at[r // 8]) for r in range(0, R, 8)]
+    for load in loads:
+        load.start()
     wr1 = backward_matrix(wr[0])
     get_a1 = Rows((0, R, held(a1)))
-    get_g1 = Rows((0, D2, held(g1s, 0)), (D2, MIDDLE, held(g1)), (R - D2, D2, held(g1s, 1)))
 
     def post(row, at, mixed):
-        flat[row, :, at] = (get_g1(row, at) + mixed).astype(BF16)
-
-    for first in range(0, R, 8):
+        flat[row, :, at] = (g1[row, :, at] + mixed).astype(BF16)
+
+    for load, first in zip(loads, range(0, R, 8)):
+        load.wait()
         conv_rows(get_a1, [first + q for q in range(8)], D1, True, wr1, post, tail=False)
     turn_out(flat, out)
 
 
 def backward_map(*args):
     return call(
-        map_kernel, "backward_map", [VM] * 4,
+        map_kernel, "backward_map", [VM, ANY, VM],
         [jax.ShapeDtypeStruct((C, R, W), BF16)],
-        [pltpu.VMEM((R, C, W), BF16)],
-        4, 10, *args,
+        [pltpu.VMEM((R, C, W), F32), pltpu.VMEM((R, C, W), BF16), pltpu.SemaphoreType.DMA((R // 8,))],
+        4, 14, *args,
     )[0]
 
 
@@ -719,11 +731,11 @@
     )
     final, b1s, h2s = forward_outer(tile_mask, x_above, x_below, xt, x_tail, h1, b1, h2, wr, wc)
     b1s, h2s = in_vmem(b1s), in_vmem(h2s)
-    taps, a1, g1s = backward(
-        tile_mask, c_above, c_below, wr, wc, ct, c_tail, cm, a2, cg1, col_taps, row_taps,
+    taps, a1, g1 = backward(
+        tile_mask, c_above, c_below, wr, wc, ct, c_tail, cm, a2, cg1, g1, col_taps, row_taps,
         xt, h1, b1, b1s, h2, h2s,
     )
-    total, map_grad = tap_sum(taps, backward_map(in_vmem(a1), g1, in_vmem(g1s), wr))
+    total, map_grad = tap_sum(taps, backward_map(in_vmem(a1), in_hbm(g1), wr))
     total = total[::-1] * factor
     return final, map_grad, total[..., C:], total[..., :C]
 

time: 115 us -> 111 us (0.965)
  local copies, waits for them, and re-layouts: 16.4 us -> 4.73 us
  waiting for transfers between devices: 13.1 us -> 19.8 us
  Pallas kernels: 36.2 us -> 38.6 us
    unnamed x30 -> x10, local copies, waits for them, and re-layouts: 14.8 us -> 3.19 us
    ppermute x1, waiting for transfers between devices: 0.01 us -> 3.26 us  [on_device(): x_below = in_vmem(lax.ppermute(x_up, 'rows', up))]
    pallas_call x4, Pallas kernels: 30.6 us -> 32.9 us  [call(): pl.pallas_call(kernel, in_specs=in_specs, out_specs=[ANY if getattr(out,...]
    ppermute x1, waiting for transfers between devices: 0.01 us -> 2.26 us  [on_device(): from_right = in_vmem(lax.ppermute(to_left, COLS, left))]
  transfers between devices with their start and end apart: 7 -> 7, of which waited for: 3 -> 5; matrix products, arithmetic and copies ran while one was open for 0% -> 0% of each run, Pallas kernels for 21% -> 24%
where the time goes in v6:
time: 111 us; the launch traced here: 110 us
  Pallas kernels  38.6 us (35%)
  blocking collectives  28.6 us (26%)
  waiting for transfers between devices  19.8 us (18%)
  starting transfers between devices  17.5 us (16%)
  local copies, waits for them, and re-layouts  4.73 us (4%)
    pallas_call x4, Pallas kernels, call(): pl.pallas_call(kernel, in_specs=in_specs, out_specs=[ANY if getattr(out,...  32.9 us
    all_to_all x1, blocking collectives, tap_sum(): part = lax.all_to_all(taps, 'rows', 0, 0, tiled=True)  19.1 us
    all_gather x1, blocking collectives, tap_sum(): part = lax.all_gather(part.sum(0), COLS).sum(0)  9.51 us
    ppermute x1, waiting for transfers between devices, on_device(): c_above = in_vmem(lax.ppermute(c_down, 'rows', down))  5.73 us
    ppermute x1, starting transfers between devices, on_device(): c_above = in_vmem(lax.ppermute(c_down, 'rows', down))  4.6 us
    ppermute x1, waiting for transfers between devices, on_device(): c_below = in_vmem(lax.ppermute(c_up, 'rows', up))  4.49 us
    all_to_all x1, waiting for transfers between devices, tap_sum(): whole = lax.all_to_all(spread, 'rows', 0, 0, tiled=True)  4.07 us
    ppermute x1, starting transfers between devices, on_device(): x_above = in_vmem(lax.ppermute(x_down, 'rows', down))  3.88 us
  transfers between devices with their start and end apart: 7, of which 5 were waited for; matrix products, arithmetic and copies ran while one was open for 0% of the time, Pallas kernels for 24%

profile of v6, /device:TPU:0, one launch (start us, length us, event | category | flops | bytes accessed | tf_op | source)
XLA Modules:
  0.0 110.1 jit_solution(17637771004124115560)
XLA Ops:
  0.6 0.0 copy-start
  0.6 1.6 %copy-done = bf16[64,32,512]{2,1,0:T(8,128)(2,1)S(1)} copy-done((bf16[64,32,512]{2,1,0:T(8,128)(2,1)S(1)}, bf16[64,32,512]{2,1,0:T(8,128)(2,1)}, u32[]{:S(2)}) %copy-start) | copy-done | bytes 2097176
  2.2 0.0 copy-start.1
  2.2 1.6 %copy-done.1 = bf16[64,32,512]{2,1,0:T(8,128)(2,1)S(1)} copy-done((bf16[64,32,512]{2,1,0:T(8,128)(2,1)S(1)}, bf16[64,32,512]{2,1,0:T(8,128)(2,1)}, u32[]{:S(2)}) %copy-start.1) | copy-done | bytes 2097176
  3.8 1.6 %pack_edges.1 = (bf16[12,64,128]{2,1,0:T(8,128)(2,1)S(1)}, bf16[12,64,128]{2,1,0:T(8,128)(2,1)S(1)}) custom-call(bf16[64,32,512]{2,1,0:T(8,128)(2,1)S(1)} %copy-done, bf16[64,32,512]{2,1,0:T(8,128)(2,1)S(1)} %copy-done, bf16[64,32,512]{2,1,0:T(8,128)(2,1)S(1)} %copy-done.1, bf16[64,32,512]{2,1,0:T(8,128)(2,1)S(1)} %copy-done.1), custom_call_target="tpu_custom_call" | custom-call | tf_op jit(solution)/shard_map/pack_edges/pallas_call | solution.py:87
  5.5 1.3 %collective-permute-start = (bf16[12,64,128]{2,1,0:T(8,128)(2,1)S(1)}, bf16[12,64,128]{2,1,0:T(8,128)(2,1)S(1)}, u32[]{:S(2)}, u32[]{:S(2)}) collective-permute-start(bf16[12,64,128]{2,1,0:T(8,128)(2,1)S(1)} %get-tuple-element.37), channel_id=1, source_target_pairs={{0,1},{1,2},{2,3},{4,5},{5,6},{6,7},{8,9},{9,10},{10,11},{12,13},{... | collective-permute-start | bytes 589832 | tf_op jit(solution)/shard_map/ppermute | solution.py:720
  6.8 1.3 %collective-permute-start.1 = (bf16[12,64,128]{2,1,0:T(8,128)(2,1)S(1)}, bf16[12,64,128]{2,1,0:T(8,128)(2,1)S(1)}, u32[]{:S(2)}, u32[]{:S(2)}) collective-permute-start(bf16[12,64,128]{2,1,0:T(8,128)(2,1)S(1)} %get-tuple-element.38), channel_id=1, source_target_pairs={{1,0},{2,1},{3,2},{5,4},{6,5},{7,6},{9,8},{10,9},{11,10},{13,12},{... | collective-permute-start | bytes 589832 | tf_op jit(solution)/shard_map/ppermute | solution.py:719
  8.1 3.3 %turn_both.1 = (bf16[32,64,512]{2,1,0:T(8,128)(2,1)S(1)}, bf16[27,64,256]{2,1,0:T(8,128)(2,1)}, bf16[27,64,256]{2,1,0:T(8,128)(2,1)}, bf16[32,64,512]{2,1,0:T(8,...) custom-call(bf16[64,32,512]{2,1,0:T(8,128)(2,1)S(1)} %copy-done, bf16[64,32,512]{2,1,0:T(8,128)(2,1)S(1)} %copy-done.1), custom_call_target="tpu_custom_call" | custom-call | tf_op jit(solution)/shard_map/turn_both/pallas_call | solution.py:131
  11.3 0.0 copy-start.2
  11.3 0.0 copy-start.3
  11.3 0.0 copy-start.4
  11.3 0.0 collective-permute-done.left
  11.3 2.3 %collective-permute-done.1.right = bf16[12,64,128]{2,1,0:T(8,128)(2,1)S(1)} collective-permute-done((bf16[12,64,128]{2,1,0:T(8,128)(2,1)S(1)}, bf16[12,64,128]{2,1,0:T(8,128)(2,1)S(1)}, u32[]{:S(2)}, u32[]{:S(2)}) %collective-permute-start.1) | collective-permute-done | bytes 196640 | tf_op jit(solution)/shard_map/ppermute | solution.py:719
  13.6 0.8 fill_messages.1
  14.4 3.9 %collective-permute-start.2 = (bf16[27,64,256]{2,1,0:T(8,128)(2,1)}, bf16[27,64,256]{2,1,0:T(8,128)(2,1)S(1)}, u32[]{:S(2)}, u32[]{:S(2)}) collective-permute-start(bf16[27,64,256]{2,1,0:T(8,128)(2,1)} %get-tuple-element.39), channel_id=1, source_target_pairs={{0,4},{4,8},{8,12},{12,16},{16,20},{20,24},{24,28},{28,32},{32,36}... | collective-permute-start | bytes 2654216 | tf_op jit(solution)/shard_map/ppermute | solution.py:723
  18.3 1.3 %collective-permute-start.3 = (bf16[27,64,256]{2,1,0:T(8,128)(2,1)}, bf16[27,64,256]{2,1,0:T(8,128)(2,1)S(1)}, u32[]{:S(2)}, u32[]{:S(2)}) collective-permute-start(bf16[27,64,256]{2,1,0:T(8,128)(2,1)} %get-tuple-element.40), channel_id=1, source_target_pairs={{4,0},{8,4},{12,8},{16,12},{20,16},{24,20},{28,24},{32,28},{36,32}... | collective-permute-start | bytes 2654216 | tf_op jit(solution)/shard_map/ppermute | solution.py:724
  19.6 4.6 %collective-permute-start.4 = (bf16[13,64,512]{2,1,0:T(8,128)(2,1)}, bf16[13,64,512]{2,1,0:T(8,128)(2,1)S(1)}, u32[]{:S(2)}, u32[]{:S(2)}) collective-permute-start(bf16[13,64,512]{2,1,0:T(8,128)(2,1)} %get-tuple-element.48), channel_id=1, source_target_pairs={{0,4},{4,8},{8,12},{12,16},{16,20},{20,24},{24,28},{28,32},{32,36}... | collective-permute-start | bytes 2555912 | tf_op jit(solution)/shard_map/ppermute | solution.py:725
  24.2 1.3 %collective-permute-start.5 = (bf16[13,64,512]{2,1,0:T(8,128)(2,1)}, bf16[13,64,512]{2,1,0:T(8,128)(2,1)S(1)}, u32[]{:S(2)}, u32[]{:S(2)}) collective-permute-start(bf16[13,64,512]{2,1,0:T(8,128)(2,1)} %get-tuple-element.49), channel_id=1, source_target_pairs={{4,0},{8,4},{12,8},{16,12},{20,16},{24,20},{28,24},{32,28},{36,32}... | collective-permute-start | bytes 2555912 | tf_op jit(solution)/shard_map/ppermute | solution.py:726
  25.5 0.0 copy-done.2
  25.5 0.0 copy-done.3
  25.5 0.0 copy-done.4
  25.5 9.5 %forward_inner.1 = (bf16[32,64,128]{2,1,0:T(8,128)(2,1)S(1)}, bf16[32,64,640]{2,1,0:T(8,128)(2,1)S(1)}, bf16[24,64,640]{2,1,0:T(8,128)(2,1)S(1)}, bf16[24,64,640...) custom-call(s32[8,16]{1,0:T(8,128)S(1)} %copy-done.4, ...), custom_call_target="tpu_custom_call" | custom-call | flops 7000000000 | bytes 14000000 | tf_op jit(solution)/shard_map/forward_inner/pallas_call | solution.py:342
  35.0 0.0 collective-permute-done.2.above
  35.0 3.3 %collective-permute-done.3.below = bf16[27,64,256]{2,1,0:T(8,128)(2,1)S(1)} collective-permute-done((bf16[27,64,256]{2,1,0:T(8,128)(2,1)}, bf16[27,64,256]{2,1,0:T(8,128)(2,1)S(1)}, u32[]{:S(2)}, u32[]{:S(2)}) %collective-permute-start.3) | collective-permute-done | bytes 884768 | tf_op jit(solution)/shard_map/ppermute | solution.py:724
  38.3 8.0 %forward_outer.1 = (bf16[64,32,512]{2,1,0:T(8,128)(2,1)}, bf16[2,12,64,640]{3,2,1,0:T(8,128)(2,1)S(1)}, bf16[2,12,64,640]{3,2,1,0:T(8,128)(2,1)S(1)}) custom-call(s32[8,16]{1,0:T(8,128)S(1)} %copy-done.4, bf16[27,64,256]{2,1,0:T(8,128)(2,1)S(1)} %collective-permute-done.2.above, bf16[27,64,256]{2,1,0:T(8,128)(2,1)S(1)} %collective-permute-done.3.below, ...), custom_call_target="tpu_custom_call" | custom-call | flops 7000000000 | bytes 14000000 | tf_op jit(solution)/shard_map/forward_outer/pallas_call | solution.py:342
  46.3 5.7 %collective-permute-done.4.above = bf16[13,64,512]{2,1,0:T(8,128)(2,1)S(1)} collective-permute-done((bf16[13,64,512]{2,1,0:T(8,128)(2,1)}, bf16[13,64,512]{2,1,0:T(8,128)(2,1)S(1)}, u32[]{:S(2)}, u32[]{:S(2)}) %collective-permute-start.4) | collective-permute-done | bytes 852000 | tf_op jit(solution)/shard_map/ppermute | solution.py:725
  52.0 4.5 %collective-permute-done.5.below = bf16[13,64,512]{2,1,0:T(8,128)(2,1)S(1)} collective-permute-done((bf16[13,64,512]{2,1,0:T(8,128)(2,1)}, bf16[13,64,512]{2,1,0:T(8,128)(2,1)S(1)}, u32[]{:S(2)}, u32[]{:S(2)}) %collective-permute-start.5) | collective-permute-done | bytes 852000 | tf_op jit(solution)/shard_map/ppermute | solution.py:726
  56.5 9.5 %backward.1 = (f32[32,12,128]{2,1,0:T(8,128)S(1)}, bf16[32,64,640]{2,1,0:T(8,128)(2,1)S(1)}, f32[32,64,512]{2,1,0:T(8,128)}) custom-call(s32[8,16]{1,0:T(8,128)S(1)} %copy-done.4, bf16[13,64,512]{2,1,0:T(8,128)(2,1)S(1)} %collective-permute-done.4.above, bf16[13,64,512]{2,1,0:T(8,128)(2,1)S(1)} %collective-permute-done.5.below, ...), custom_call_target="tpu_custom_call" | custom-call | flops 8000000000 | bytes 16000000 | tf_op jit(solution)/shard_map/backward/pallas_call | solution.py:342
  66.0 19.1 %all_to_all.10 = f32[32,12,128]{2,1,0:T(8,128)S(1)} all-to-all(f32[32,12,128]{2,1,0:T(8,128)S(1)} %get-tuple-element.61), channel_id=1, replica_groups=mesh['rows'=32,'y_hi'=2,'core'=2] {'rows'}, dimensions={0} | all-to-all | bytes 393216 | tf_op jit(solution)/shard_map/all_to_all | solution.py:692
  85.2 9.5 %all-gather.1 = f32[4,12,128]{2,1,0:T(8,128)S(1)} all-gather(f32[1,12,128]{2,1,0:T(8,128)S(1)} %bitcast.1), channel_id=2, replica_groups=mesh['rows'=32,'y_hi'=2,'core'=2] {'y_hi','core'}, dimensions={0}, use_global_device_ids=true | all-gather | bytes 30720 | tf_op jit(solution)/shard_map/all_gather | solution.py:693
  94.7 0.7 broadcast_in_dim.2
  95.4 3.9 %all-to-all-start.1 = ((f32[32,12,128]{2,1,0:T(8,128)}), f32[32,12,128]{2,1,0:T(8,128)S(1)}, u32[]{:S(2)}, u32[]{:S(2)}) async-start(f32[32,12,128]{2,1,0:T(8,128)} %broadcast_in_dim.2), calls=%async_computation.1 | async-start | bytes 524288 | tf_op jit(solution)/shard_map/all_to_all | solution.py:695
  99.3 5.9 %backward_map.1 = bf16[64,32,512]{2,1,0:T(8,128)(2,1)} custom-call(bf16[32,64,640]{2,1,0:T(8,128)(2,1)S(1)} %get-tuple-element.59.a1, f32[32,64,512]{2,1,0:T(8,128)} %get-tuple-element.60.g1_in, bf16[2,3,64,64]{3,2,1,0:T(8,128)(2,1)S(1)} %copy-done.2), custom_call_target="tpu_custom_call" | custom-call | flops 2000000000 | bytes 4000000 | tf_op jit(solution)/shard_map/backward_map/pallas_call | solution.py:342
  105.2 4.1 %all-to-all-done.1 = f32[32,12,128]{2,1,0:T(8,128)S(1)} async-done(((f32[32,12,128]{2,1,0:T(8,128)}), f32[32,12,128]{2,1,0:T(8,128)S(1)}, u32[]{:S(2)}, u32[]{:S(2)}) %all-to-all-start.1) | async-done | bytes 196640 | tf_op jit(solution)/shard_map/all_to_all | solution.py:695
  109.3 0.8 fusion
  (4 shorter events, 0.1 us)
Async XLA Ops:
  0.6 1.6 %copy-start = (bf16[64,32,512]{2,1,0:T(8,128)(2,1)S(1)}, bf16[64,32,512]{2,1,0:T(8,128)(2,1)}, u32[]{:S(2)}) copy-start(bf16[64,32,512]{2,1,0:T(8,128)(2,1)} %x_high.1) | copy-start | bytes 6291460
  2.2 1.6 %copy-start.1 = (bf16[64,32,512]{2,1,0:T(8,128)(2,1)S(1)}, bf16[64,32,512]{2,1,0:T(8,128)(2,1)}, u32[]{:S(2)}) copy-start(bf16[64,32,512]{2,1,0:T(8,128)(2,1)} %c_high.1) | copy-start | bytes 6291460
  5.5 5.9 %collective-permute-start = (bf16[12,64,128]{2,1,0:T(8,128)(2,1)S(1)}, bf16[12,64,128]{2,1,0:T(8,128)(2,1)S(1)}, u32[]{:S(2)}, u32[]{:S(2)}) collective-permute-start(bf16[12,64,128]{2,1,0:T(8,128)(2,1)S(1)} %get-tuple-element.37), channel_id=1, source_target_pairs={{0,1},{1,2},{2,3},{4,5},{5,6},{6,7},{8,9},{9,10},{10,11},{12,13},{... | collective-permute-start | bytes 589832 | tf_op jit(solution)/shard_map/ppermute | solution.py:720
  6.8 6.8 %collective-permute-start.1 = (bf16[12,64,128]{2,1,0:T(8,128)(2,1)S(1)}, bf16[12,64,128]{2,1,0:T(8,128)(2,1)S(1)}, u32[]{:S(2)}, u32[]{:S(2)}) collective-permute-start(bf16[12,64,128]{2,1,0:T(8,128)(2,1)S(1)} %get-tuple-element.38), channel_id=1, source_target_pairs={{1,0},{2,1},{3,2},{5,4},{6,5},{7,6},{9,8},{10,9},{11,10},{13,12},{... | collective-permute-start | bytes 589832 | tf_op jit(solution)/shard_map/ppermute | solution.py:719
  11.3 14.2 %copy-start.2 = (bf16[2,3,64,64]{3,2,1,0:T(8,128)(2,1)S(1)}, bf16[2,3,64,64]{3,2,1,0:T(8,128)(2,1)}, u32[]{:S(2)}) copy-start(bf16[2,3,64,64]{3,2,1,0:T(8,128)(2,1)} %wr.7) | copy-start | bytes 147460
  11.3 14.2 %copy-start.3 = (bf16[2,3,64,64]{3,2,1,0:T(8,128)(2,1)S(1)}, bf16[2,3,64,64]{3,2,1,0:T(8,128)(2,1)}, u32[]{:S(2)}) copy-start(bf16[2,3,64,64]{3,2,1,0:T(8,128)(2,1)} %wc.5) | copy-start | bytes 147460
  11.3 14.2 %copy-start.4 = (s32[8,16]{1,0:T(8,128)S(1)}, s32[8,16]{1,0:T(8,128)}, u32[]{:S(2)}) copy-start(s32[8,16]{1,0:T(8,128)} %tiles.5) | copy-start | bytes 1540
  14.4 20.6 %collective-permute-start.2 = (bf16[27,64,256]{2,1,0:T(8,128)(2,1)}, bf16[27,64,256]{2,1,0:T(8,128)(2,1)S(1)}, u32[]{:S(2)}, u32[]{:S(2)}) collective-permute-start(bf16[27,64,256]{2,1,0:T(8,128)(2,1)} %get-tuple-element.39), channel_id=1, source_target_pairs={{0,4},{4,8},{8,12},{12,16},{16,20},{20,24},{24,28},{28,32},{32,36}... | collective-permute-start | bytes 2654216 | tf_op jit(solution)/shard_map/ppermute | solution.py:723
  18.3 20.0 %collective-permute-start.3 = (bf16[27,64,256]{2,1,0:T(8,128)(2,1)}, bf16[27,64,256]{2,1,0:T(8,128)(2,1)S(1)}, u32[]{:S(2)}, u32[]{:S(2)}) collective-permute-start(bf16[27,64,256]{2,1,0:T(8,128)(2,1)} %get-tuple-element.40), channel_id=1, source_target_pairs={{4,0},{8,4},{12,8},{16,12},{20,16},{24,20},{28,24},{32,28},{36,32}... | collective-permute-start | bytes 2654216 | tf_op jit(solution)/shard_map/ppermute | solution.py:724
  19.6 32.5 %collective-permute-start.4 = (bf16[13,64,512]{2,1,0:T(8,128)(2,1)}, bf16[13,64,512]{2,1,0:T(8,128)(2,1)S(1)}, u32[]{:S(2)}, u32[]{:S(2)}) collective-permute-start(bf16[13,64,512]{2,1,0:T(8,128)(2,1)} %get-tuple-element.48), channel_id=1, source_target_pairs={{0,4},{4,8},{8,12},{12,16},{16,20},{20,24},{24,28},{28,32},{32,36}... | collective-permute-start | bytes 2555912 | tf_op jit(solution)/shard_map/ppermute | solution.py:725
  24.2 32.4 %collective-permute-start.5 = (bf16[13,64,512]{2,1,0:T(8,128)(2,1)}, bf16[13,64,512]{2,1,0:T(8,128)(2,1)S(1)}, u32[]{:S(2)}, u32[]{:S(2)}) collective-permute-start(bf16[13,64,512]{2,1,0:T(8,128)(2,1)} %get-tuple-element.49), channel_id=1, source_target_pairs={{4,0},{8,4},{12,8},{16,12},{20,16},{24,20},{28,24},{32,28},{36,32}... | collective-permute-start | bytes 2555912 | tf_op jit(solution)/shard_map/ppermute | solution.py:726
  95.4 13.9 %all-to-all-start.1 = ((f32[32,12,128]{2,1,0:T(8,128)}), f32[32,12,128]{2,1,0:T(8,128)S(1)}, u32[]{:S(2)}, u32[]{:S(2)}) async-start(f32[32,12,128]{2,1,0:T(8,128)} %broadcast_in_dim.2), calls=%async_computation.1 | async-start | bytes 524288 | tf_op jit(solution)/shard_map/all_to_all | solution.py:695

commit v7 on v6

--- a/solution.py
+++ b/solution.py
@@ -715,7 +715,7 @@
     right = [(i, i + 1) for i in range(n_cols - 1)]
     left = [(i + 1, i) for i in range(n_cols - 1)]
 
-    to_left, to_right = pack_edges(x, cot)
+    to_left, to_right = pack_edges(in_hbm(x), in_hbm(cot))
     from_right = in_vmem(lax.ppermute(to_left, COLS, left))
     from_left = in_vmem(lax.ppermute(to_right, COLS, right))
     xt, x_up, x_down, ct, c_up, c_down = turn_both(x, cot)

time: 111 us -> 109 us (0.982)
  local copies, waits for them, and re-layouts: 4.73 us -> 1.57 us
  Pallas kernels: 38.6 us -> 40.4 us
    unnamed x10, local copies, waits for them, and re-layouts: 3.19 us -> 0.02 us
    pallas_call x1, Pallas kernels: 1.63 us -> 3.43 us  [pack_edges(): pl.pallas_call(edge_kernel, grid=(C // GC,), in_specs=[low, high, low, hi...]
  transfers between devices with their start and end apart: 7 -> 7, of which waited for: 5 -> 5; matrix products, arithmetic and copies ran while one was open for 0% -> 0% of each run, Pallas kernels for 24% -> 25%
where the time goes in v7:
time: 109 us
  Pallas kernels  40.4 us (37%)
  blocking collectives  28.6 us (26%)
  waiting for transfers between devices  19.8 us (18%)
  starting transfers between devices  17.5 us (16%)
  local copies, waits for them, and re-layouts  1.57 us (1%)
    pallas_call x4, Pallas kernels, call(): pl.pallas_call(kernel, in_specs=in_specs, out_specs=[ANY if getattr(out,...  32.9 us
    all_to_all x1, blocking collectives, tap_sum(): part = lax.all_to_all(taps, 'rows', 0, 0, tiled=True)  19.1 us
    all_gather x1, blocking collectives, tap_sum(): part = lax.all_gather(part.sum(0), COLS).sum(0)  9.53 us
    ppermute x1, waiting for transfers between devices, on_device(): c_above = in_vmem(lax.ppermute(c_down, 'rows', down))  5.74 us
    ppermute x1, starting transfers between devices, on_device(): c_above = in_vmem(lax.ppermute(c_down, 'rows', down))  4.6 us
    ppermute x1, waiting for transfers between devices, on_device(): c_below = in_vmem(lax.ppermute(c_up, 'rows', up))  4.49 us
    all_to_all x1, waiting for transfers between devices, tap_sum(): whole = lax.all_to_all(spread, 'rows', 0, 0, tiled=True)  4.07 us
    ppermute x1, starting transfers between devices, on_device(): x_above = in_vmem(lax.ppermute(x_down, 'rows', down))  3.88 us
  transfers between devices with their start and end apart: 7, of which 5 were waited for; matrix products, arithmetic and copies ran while one was open for 0% of the time, Pallas kernels for 25%

profile of v7, /device:TPU:0, one launch (start us, length us, event | category | flops | bytes accessed | tf_op | source)
XLA Modules:
  0.0 108.8 jit_solution(6868631896276372976)
XLA Ops:
  0.6 0.0 copy-start
  0.6 0.0 copy-start.1
  0.7 3.4 %pack_edges.1 = (bf16[12,64,128]{2,1,0:T(8,128)(2,1)S(1)}, bf16[12,64,128]{2,1,0:T(8,128)(2,1)S(1)}) custom-call(bf16[64,32,512]{2,1,0:T(8,128)(2,1)} %x_high.1, bf16[64,32,512]{2,1,0:T(8,128)(2,1)} %x_high.1, bf16[64,32,512]{2,1,0:T(8,128)(2,1)} %c_high.1, bf16[64,32,512]{2,1,0:T(8,128)(2,1)} %c_high.1), custom_call_target="tpu_custom_call" | custom-call | tf_op jit(solution)/shard_map/pack_edges/pallas_call | solution.py:87
  4.1 1.3 %collective-permute-start = (bf16[12,64,128]{2,1,0:T(8,128)(2,1)S(1)}, bf16[12,64,128]{2,1,0:T(8,128)(2,1)S(1)}, u32[]{:S(2)}, u32[]{:S(2)}) collective-permute-start(bf16[12,64,128]{2,1,0:T(8,128)(2,1)S(1)} %get-tuple-element.37), channel_id=1, source_target_pairs={{0,1},{1,2},{2,3},{4,5},{5,6},{6,7},{8,9},{9,10},{10,11},{12,13},{... | collective-permute-start | bytes 589832 | tf_op jit(solution)/shard_map/ppermute | solution.py:720
  5.4 1.3 %collective-permute-start.1 = (bf16[12,64,128]{2,1,0:T(8,128)(2,1)S(1)}, bf16[12,64,128]{2,1,0:T(8,128)(2,1)S(1)}, u32[]{:S(2)}, u32[]{:S(2)}) collective-permute-start(bf16[12,64,128]{2,1,0:T(8,128)(2,1)S(1)} %get-tuple-element.38), channel_id=1, source_target_pairs={{1,0},{2,1},{3,2},{5,4},{6,5},{7,6},{9,8},{10,9},{11,10},{13,12},{... | collective-permute-start | bytes 589832 | tf_op jit(solution)/shard_map/ppermute | solution.py:719
  6.7 0.0 copy-done
  6.7 0.0 copy-done.1
  6.7 3.3 %turn_both.1 = (bf16[32,64,512]{2,1,0:T(8,128)(2,1)S(1)}, bf16[27,64,256]{2,1,0:T(8,128)(2,1)}, bf16[27,64,256]{2,1,0:T(8,128)(2,1)}, bf16[32,64,512]{2,1,0:T(8,...) custom-call(bf16[64,32,512]{2,1,0:T(8,128)(2,1)S(1)} %copy-done, bf16[64,32,512]{2,1,0:T(8,128)(2,1)S(1)} %copy-done.1), custom_call_target="tpu_custom_call" | custom-call | tf_op jit(solution)/shard_map/turn_both/pallas_call | solution.py:131
  10.0 0.0 copy-start.2
  10.0 0.0 copy-start.3
  10.0 0.0 copy-start.4
  10.0 0.0 collective-permute-done.left
  10.0 2.2 %collective-permute-done.1.right = bf16[12,64,128]{2,1,0:T(8,128)(2,1)S(1)} collective-permute-done((bf16[12,64,128]{2,1,0:T(8,128)(2,1)S(1)}, bf16[12,64,128]{2,1,0:T(8,128)(2,1)S(1)}, u32[]{:S(2)}, u32[]{:S(2)}) %collective-permute-start.1) | collective-permute-done | bytes 196640 | tf_op jit(solution)/shard_map/ppermute | solution.py:719
  12.2 0.8 fill_messages.1
  13.0 3.9 %collective-permute-start.2 = (bf16[27,64,256]{2,1,0:T(8,128)(2,1)}, bf16[27,64,256]{2,1,0:T(8,128)(2,1)S(1)}, u32[]{:S(2)}, u32[]{:S(2)}) collective-permute-start(bf16[27,64,256]{2,1,0:T(8,128)(2,1)} %get-tuple-element.39), channel_id=1, source_target_pairs={{0,4},{4,8},{8,12},{12,16},{16,20},{20,24},{24,28},{28,32},{32,36}... | collective-permute-start | bytes 2654216 | tf_op jit(solution)/shard_map/ppermute | solution.py:723
  16.9 1.3 %collective-permute-start.3 = (bf16[27,64,256]{2,1,0:T(8,128)(2,1)}, bf16[27,64,256]{2,1,0:T(8,128)(2,1)S(1)}, u32[]{:S(2)}, u32[]{:S(2)}) collective-permute-start(bf16[27,64,256]{2,1,0:T(8,128)(2,1)} %get-tuple-element.40), channel_id=1, source_target_pairs={{4,0},{8,4},{12,8},{16,12},{20,16},{24,20},{28,24},{32,28},{36,32}... | collective-permute-start | bytes 2654216 | tf_op jit(solution)/shard_map/ppermute | solution.py:724
  18.2 4.6 %collective-permute-start.4 = (bf16[13,64,512]{2,1,0:T(8,128)(2,1)}, bf16[13,64,512]{2,1,0:T(8,128)(2,1)S(1)}, u32[]{:S(2)}, u32[]{:S(2)}) collective-permute-start(bf16[13,64,512]{2,1,0:T(8,128)(2,1)} %get-tuple-element.48), channel_id=1, source_target_pairs={{0,4},{4,8},{8,12},{12,16},{16,20},{20,24},{24,28},{28,32},{32,36}... | collective-permute-start | bytes 2555912 | tf_op jit(solution)/shard_map/ppermute | solution.py:725
  22.8 1.3 %collective-permute-start.5 = (bf16[13,64,512]{2,1,0:T(8,128)(2,1)}, bf16[13,64,512]{2,1,0:T(8,128)(2,1)S(1)}, u32[]{:S(2)}, u32[]{:S(2)}) collective-permute-start(bf16[13,64,512]{2,1,0:T(8,128)(2,1)} %get-tuple-element.49), channel_id=1, source_target_pairs={{4,0},{8,4},{12,8},{16,12},{20,16},{24,20},{28,24},{32,28},{36,32}... | collective-permute-start | bytes 2555912 | tf_op jit(solution)/shard_map/ppermute | solution.py:726
  24.1 0.0 copy-done.2
  24.1 0.0 copy-done.3
  24.1 0.0 copy-done.4
  24.1 9.5 %forward_inner.1 = (bf16[32,64,128]{2,1,0:T(8,128)(2,1)S(1)}, bf16[32,64,640]{2,1,0:T(8,128)(2,1)S(1)}, bf16[24,64,640]{2,1,0:T(8,128)(2,1)S(1)}, bf16[24,64,640...) custom-call(s32[8,16]{1,0:T(8,128)S(1)} %copy-done.4, ...), custom_call_target="tpu_custom_call" | custom-call | flops 7000000000 | bytes 14000000 | tf_op jit(solution)/shard_map/forward_inner/pallas_call | solution.py:342
  33.6 0.0 collective-permute-done.2.above
  33.7 3.3 %collective-permute-done.3.below = bf16[27,64,256]{2,1,0:T(8,128)(2,1)S(1)} collective-permute-done((bf16[27,64,256]{2,1,0:T(8,128)(2,1)}, bf16[27,64,256]{2,1,0:T(8,128)(2,1)S(1)}, u32[]{:S(2)}, u32[]{:S(2)}) %collective-permute-start.3) | collective-permute-done | bytes 884768 | tf_op jit(solution)/shard_map/ppermute | solution.py:724
  36.9 8.0 %forward_outer.1 = (bf16[64,32,512]{2,1,0:T(8,128)(2,1)}, bf16[2,12,64,640]{3,2,1,0:T(8,128)(2,1)S(1)}, bf16[2,12,64,640]{3,2,1,0:T(8,128)(2,1)S(1)}) custom-call(s32[8,16]{1,0:T(8,128)S(1)} %copy-done.4, bf16[27,64,256]{2,1,0:T(8,128)(2,1)S(1)} %collective-permute-done.2.above, bf16[27,64,256]{2,1,0:T(8,128)(2,1)S(1)} %collective-permute-done.3.below, ...), custom_call_target="tpu_custom_call" | custom-call | flops 7000000000 | bytes 14000000 | tf_op jit(solution)/shard_map/forward_outer/pallas_call | solution.py:342
  44.9 5.7 %collective-permute-done.4.above = bf16[13,64,512]{2,1,0:T(8,128)(2,1)S(1)} collective-permute-done((bf16[13,64,512]{2,1,0:T(8,128)(2,1)}, bf16[13,64,512]{2,1,0:T(8,128)(2,1)S(1)}, u32[]{:S(2)}, u32[]{:S(2)}) %collective-permute-start.4) | collective-permute-done | bytes 852000 | tf_op jit(solution)/shard_map/ppermute | solution.py:725
  50.7 4.5 %collective-permute-done.5.below = bf16[13,64,512]{2,1,0:T(8,128)(2,1)S(1)} collective-permute-done((bf16[13,64,512]{2,1,0:T(8,128)(2,1)}, bf16[13,64,512]{2,1,0:T(8,128)(2,1)S(1)}, u32[]{:S(2)}, u32[]{:S(2)}) %collective-permute-start.5) | collective-permute-done | bytes 852000 | tf_op jit(solution)/shard_map/ppermute | solution.py:726
  55.2 9.5 %backward.1 = (f32[32,12,128]{2,1,0:T(8,128)S(1)}, bf16[32,64,640]{2,1,0:T(8,128)(2,1)S(1)}, f32[32,64,512]{2,1,0:T(8,128)}) custom-call(s32[8,16]{1,0:T(8,128)S(1)} %copy-done.4, bf16[13,64,512]{2,1,0:T(8,128)(2,1)S(1)} %collective-permute-done.4.above, bf16[13,64,512]{2,1,0:T(8,128)(2,1)S(1)} %collective-permute-done.5.below, ...), custom_call_target="tpu_custom_call" | custom-call | flops 8000000000 | bytes 16000000 | tf_op jit(solution)/shard_map/backward/pallas_call | solution.py:342
  64.7 19.1 %all_to_all.10 = f32[32,12,128]{2,1,0:T(8,128)S(1)} all-to-all(f32[32,12,128]{2,1,0:T(8,128)S(1)} %get-tuple-element.61), channel_id=1, replica_groups=mesh['rows'=32,'y_hi'=2,'core'=2] {'rows'}, dimensions={0} | all-to-all | bytes 393216 | tf_op jit(solution)/shard_map/all_to_all | solution.py:692
  83.8 9.5 %all-gather.1 = f32[4,12,128]{2,1,0:T(8,128)S(1)} all-gather(f32[1,12,128]{2,1,0:T(8,128)S(1)} %bitcast.1), channel_id=2, replica_groups=mesh['rows'=32,'y_hi'=2,'core'=2] {'y_hi','core'}, dimensions={0}, use_global_device_ids=true | all-gather | bytes 30720 | tf_op jit(solution)/shard_map/all_gather | solution.py:693
  93.3 0.7 broadcast_in_dim.2
  94.1 3.9 %all-to-all-start.1 = ((f32[32,12,128]{2,1,0:T(8,128)}), f32[32,12,128]{2,1,0:T(8,128)S(1)}, u32[]{:S(2)}, u32[]{:S(2)}) async-start(f32[32,12,128]{2,1,0:T(8,128)} %broadcast_in_dim.2), calls=%async_computation.1 | async-start | bytes 524288 | tf_op jit(solution)/shard_map/all_to_all | solution.py:695
  97.9 5.9 %backward_map.1 = bf16[64,32,512]{2,1,0:T(8,128)(2,1)} custom-call(bf16[32,64,640]{2,1,0:T(8,128)(2,1)S(1)} %get-tuple-element.59.a1, f32[32,64,512]{2,1,0:T(8,128)} %get-tuple-element.60.g1_in, bf16[2,3,64,64]{3,2,1,0:T(8,128)(2,1)S(1)} %copy-done.2), custom_call_target="tpu_custom_call" | custom-call | flops 2000000000 | bytes 4000000 | tf_op jit(solution)/shard_map/backward_map/pallas_call | solution.py:342
  103.9 4.1 %all-to-all-done.1 = f32[32,12,128]{2,1,0:T(8,128)S(1)} async-done(((f32[32,12,128]{2,1,0:T(8,128)}), f32[32,12,128]{2,1,0:T(8,128)S(1)}, u32[]{:S(2)}, u32[]{:S(2)}) %all-to-all-start.1) | async-done | bytes 196640 | tf_op jit(solution)/shard_map/all_to_all | solution.py:695
  108.0 0.8 fusion
  (4 shorter events, 0.1 us)
Async XLA Ops:
  0.6 6.1 %copy-start = (bf16[64,32,512]{2,1,0:T(8,128)(2,1)S(1)}, bf16[64,32,512]{2,1,0:T(8,128)(2,1)}, u32[]{:S(2)}) copy-start(bf16[64,32,512]{2,1,0:T(8,128)(2,1)} %x_high.1) | copy-start | bytes 6291460
  0.6 6.1 %copy-start.1 = (bf16[64,32,512]{2,1,0:T(8,128)(2,1)S(1)}, bf16[64,32,512]{2,1,0:T(8,128)(2,1)}, u32[]{:S(2)}) copy-start(bf16[64,32,512]{2,1,0:T(8,128)(2,1)} %c_high.1) | copy-start | bytes 6291460
  4.1 5.9 %collective-permute-start = (bf16[12,64,128]{2,1,0:T(8,128)(2,1)S(1)}, bf16[12,64,128]{2,1,0:T(8,128)(2,1)S(1)}, u32[]{:S(2)}, u32[]{:S(2)}) collective-permute-start(bf16[12,64,128]{2,1,0:T(8,128)(2,1)S(1)} %get-tuple-element.37), channel_id=1, source_target_pairs={{0,1},{1,2},{2,3},{4,5},{5,6},{6,7},{8,9},{9,10},{10,11},{12,13},{... | collective-permute-start | bytes 589832 | tf_op jit(solution)/shard_map/ppermute | solution.py:720
  5.4 6.8 %collective-permute-start.1 = (bf16[12,64,128]{2,1,0:T(8,128)(2,1)S(1)}, bf16[12,64,128]{2,1,0:T(8,128)(2,1)S(1)}, u32[]{:S(2)}, u32[]{:S(2)}) collective-permute-start(bf16[12,64,128]{2,1,0:T(8,128)(2,1)S(1)} %get-tuple-element.38), channel_id=1, source_target_pairs={{1,0},{2,1},{3,2},{5,4},{6,5},{7,6},{9,8},{10,9},{11,10},{13,12},{... | collective-permute-start | bytes 589832 | tf_op jit(solution)/shard_map/ppermute | solution.py:719
  10.0 14.1 %copy-start.2 = (bf16[2,3,64,64]{3,2,1,0:T(8,128)(2,1)S(1)}, bf16[2,3,64,64]{3,2,1,0:T(8,128)(2,1)}, u32[]{:S(2)}) copy-start(bf16[2,3,64,64]{3,2,1,0:T(8,128)(2,1)} %wr.7) | copy-start | bytes 147460
  10.0 14.1 %copy-start.3 = (bf16[2,3,64,64]{3,2,1,0:T(8,128)(2,1)S(1)}, bf16[2,3,64,64]{3,2,1,0:T(8,128)(2,1)}, u32[]{:S(2)}) copy-start(bf16[2,3,64,64]{3,2,1,0:T(8,128)(2,1)} %wc.5) | copy-start | bytes 147460
  10.0 14.1 %copy-start.4 = (s32[8,16]{1,0:T(8,128)S(1)}, s32[8,16]{1,0:T(8,128)}, u32[]{:S(2)}) copy-start(s32[8,16]{1,0:T(8,128)} %tiles.5) | copy-start | bytes 1540
  13.0 20.6 %collective-permute-start.2 = (bf16[27,64,256]{2,1,0:T(8,128)(2,1)}, bf16[27,64,256]{2,1,0:T(8,128)(2,1)S(1)}, u32[]{:S(2)}, u32[]{:S(2)}) collective-permute-start(bf16[27,64,256]{2,1,0:T(8,128)(2,1)} %get-tuple-element.39), channel_id=1, source_target_pairs={{0,4},{4,8},{8,12},{12,16},{16,20},{20,24},{24,28},{28,32},{32,36}... | collective-permute-start | bytes 2654216 | tf_op jit(solution)/shard_map/ppermute | solution.py:723
  16.9 20.0 %collective-permute-start.3 = (bf16[27,64,256]{2,1,0:T(8,128)(2,1)}, bf16[27,64,256]{2,1,0:T(8,128)(2,1)S(1)}, u32[]{:S(2)}, u32[]{:S(2)}) collective-permute-start(bf16[27,64,256]{2,1,0:T(8,128)(2,1)} %get-tuple-element.40), channel_id=1, source_target_pairs={{4,0},{8,4},{12,8},{16,12},{20,16},{24,20},{28,24},{32,28},{36,32}... | collective-permute-start | bytes 2654216 | tf_op jit(solution)/shard_map/ppermute | solution.py:724
  18.2 32.5 %collective-permute-start.4 = (bf16[13,64,512]{2,1,0:T(8,128)(2,1)}, bf16[13,64,512]{2,1,0:T(8,128)(2,1)S(1)}, u32[]{:S(2)}, u32[]{:S(2)}) collective-permute-start(bf16[13,64,512]{2,1,0:T(8,128)(2,1)} %get-tuple-element.48), channel_id=1, source_target_pairs={{0,4},{4,8},{8,12},{12,16},{16,20},{20,24},{24,28},{28,32},{32,36}... | collective-permute-start | bytes 2555912 | tf_op jit(solution)/shard_map/ppermute | solution.py:725
  22.8 32.4 %collective-permute-start.5 = (bf16[13,64,512]{2,1,0:T(8,128)(2,1)}, bf16[13,64,512]{2,1,0:T(8,128)(2,1)S(1)}, u32[]{:S(2)}, u32[]{:S(2)}) collective-permute-start(bf16[13,64,512]{2,1,0:T(8,128)(2,1)} %get-tuple-element.49), channel_id=1, source_target_pairs={{4,0},{8,4},{12,8},{16,12},{20,16},{24,20},{28,24},{32,28},{36,32}... | collective-permute-start | bytes 2555912 | tf_op jit(solution)/shard_map/ppermute | solution.py:726
  94.1 13.9 %all-to-all-start.1 = ((f32[32,12,128]{2,1,0:T(8,128)}), f32[32,12,128]{2,1,0:T(8,128)S(1)}, u32[]{:S(2)}, u32[]{:S(2)}) async-start(f32[32,12,128]{2,1,0:T(8,128)} %broadcast_in_dim.2), calls=%async_computation.1 | async-start | bytes 524288 | tf_op jit(solution)/shard_map/all_to_all | solution.py:695
